TPU v7x, 32 devices: a whole 2x2x4 slice. The times are simulated.
32 devices in a mesh: lev: 4 (over y, x), lon: 8 (over z, core).
Axes of the slice: x: 2, y: 2, z: 4, core: 2. Of those that a mesh axis runs over, the one named last changes fastest.
Arguments:
- snapshot: bfloat16 [384, 12, 1024], P('lev', None, 'lon'), may hold values from -6 to 6
- cotangent: bfloat16 [384, 12, 1024], P(None, 'lev', 'lon'), may hold values from -6 to 6
- ocean_mask: int32 [12, 1024], P('lev', 'lon'), may hold values 0 or 1
- kernel: bfloat16 [384, 49], replicated, may hold values from -0.875 to 0.875
- norm_gain: float32 [384], replicated, may hold values from 0.1 to 1.9
- norm_shift: float32 [384], replicated, may hold values from -3 to 3
- weight_in: bfloat16 [384, 1536], replicated, may hold values from -0.3125 to 0.3125
- weight_out: bfloat16 [1536, 384], replicated, may hold values from -0.15625 to 0.15625
Outputs:
- result: bfloat16 [384, 12, 1024], P(None, 'lev', 'lon')
- d_snapshot: bfloat16 [384, 12, 1024], P('lev', None, 'lon')
- kernel_grad: float32 [384, 49], replicated
All inputs are finite; a program needn't handle non-finite values. No bound on the sum of `ocean_mask` on one device may be relied on, other than what follows from the above.
Results may differ from a plain program's by a relative error of at most 0.0057.
Values may be sent and summed in bfloat16 or wider, within the bound.
No kernel may reach another device: no remote copies, remote signals or barrier semaphores. Data moves between devices by JAX's collectives and lax.ppermute only.
A program may use at most 64 MiB of HBM per device.

v0:
```python
import jax
import jax.numpy as jnp
from jax import lax
from jax.sharding import PartitionSpec as P

TAPS = 7


epsilon = 1e-06
root_half = 0.7071067811865476
inv_root_tau = 0.3989422804014327


def padded_2(shard, sides, width):
    for axis, dim in sides:
        count, length = (lax.axis_size(axis), shard.shape[dim])
        up = [(i, (i + 1) % count) for i in range(count)]
        down = [(j, i) for i, j in up]
        last = lax.slice_in_dim(shard, length - width, length, axis=dim)
        leading = lax.slice_in_dim(shard, 0, width, axis=dim)
        before = lax.ppermute(last, axis, up)
        after = lax.ppermute(leading, axis, down)
        shard = jnp.concatenate([before, shard, after], axis=dim)
    return shard


def taps(padded, weights, height, width):
    source = padded.astype(jnp.float32)
    total = jnp.zeros((padded.shape[0], height, width), jnp.float32)
    for row_off in range(TAPS):
        for col_off in range(TAPS):
            piece = source[:, row_off : row_off + height, col_off : col_off + width]
            total = total + weights[:, row_off, col_off][:, None, None] * piece
    return total


def kernel_terms(padded, d_conv, height, width):
    source = padded.astype(jnp.float32)
    flat = d_conv.astype(jnp.float32)
    terms = []
    for row_off in range(TAPS):
        for col_off in range(TAPS):
            piece = source[:, row_off : row_off + height, col_off : col_off + width]
            terms.append(jnp.sum(flat * piece, axis=(1, 2)))
    return jnp.stack(terms, axis=1)


def fold_term(fold_rows, weights, width):
    reach = TAPS // 2
    lines = []
    for depth in range(reach):
        total = jnp.zeros((fold_rows.shape[0], width), jnp.float32)
        for source in range(reach - depth):
            for col_off in range(TAPS):
                piece = fold_rows[:, source, col_off : col_off + width].astype(jnp.float32)
                total = total + weights[:, reach + 1 + depth + source, col_off][:, None] * piece
        lines.append(total)
    return jnp.stack(lines[::-1], axis=1)


def gelu_slope(hidden):
    return (
        0.5 * (1.0 + lax.erf(hidden * root_half))
        + hidden * jnp.exp(-0.5 * hidden * hidden) * inv_root_tau
    )


def cell_pass(convolved, residual, incoming, ocean, norm_gain, norm_shift, weight_in, weight_out):
    centre = jnp.mean(convolved, axis=0, keepdims=True)
    centred = convolved - centre
    spread = jnp.mean(centred * centred, axis=0, keepdims=True)
    rstd = lax.rsqrt(spread + epsilon)
    normed = centred * rstd
    lifted = (normed * norm_gain[:, None] + norm_shift[:, None]).astype(jnp.bfloat16)
    hidden = lax.dot_general(
        weight_in, lifted, (((0,), (0,)), ((), ())), preferred_element_type=jnp.float32
    )
    active = jax.nn.gelu(hidden, approximate=False).astype(jnp.bfloat16)
    projected = lax.dot_general(
        weight_out, active, (((0,), (0,)), ((), ())), preferred_element_type=jnp.float32
    )
    wet = ocean.astype(jnp.float32)[None, :]
    result = (wet * (residual.astype(jnp.float32) + projected)).astype(jnp.bfloat16)
    upstream = incoming.astype(jnp.float32) * wet
    d_active = jnp.dot(
        weight_out, upstream.astype(jnp.bfloat16), preferred_element_type=jnp.float32
    )
    d_hidden = (d_active * gelu_slope(hidden)).astype(jnp.bfloat16)
    d_lifted = jnp.dot(weight_in, d_hidden, preferred_element_type=jnp.float32)
    d_normed = d_lifted * norm_gain[:, None]
    first = jnp.mean(d_normed, axis=0, keepdims=True)
    second = jnp.mean(d_normed * normed, axis=0, keepdims=True)
    d_conv = (rstd * (d_normed - first - normed * second)).astype(jnp.bfloat16)
    return (result, upstream, d_conv)


def fold_edge(edge_rows):
    lanes = lax.axis_size("lon")
    depth_rows = edge_rows.shape[1]
    span = edge_rows.shape[2]
    channels = edge_rows.shape[0]
    blocks = edge_rows.reshape(lanes, channels // lanes, depth_rows, span)
    spread = lax.all_to_all(blocks, "lon", split_axis=0, concat_axis=0, tiled=True)
    collected = lax.all_to_all(spread[::-1], "lon", split_axis=0, concat_axis=0, tiled=True)
    edge_rows = collected.reshape(channels, depth_rows, span)
    return edge_rows[:, ::-1, ::-1]


def tile_pad(tile):
    reach = TAPS // 2
    height = tile.shape[1]
    padded = padded_2(tile, (("lev", 1), ("lon", 2)), reach)
    position = lax.axis_index("lev")
    folded = fold_edge(padded[:, height : height + reach, :])
    lower = jnp.where(position == 0, jnp.zeros_like(padded[:, :reach]), padded[:, :reach])
    upper = jnp.where(
        position == lax.axis_size("lev") - 1, jnp.zeros_like(folded), padded[:, height + reach :]
    )
    regular = jnp.concatenate([lower, padded[:, reach : height + reach], upper], axis=1)
    return (regular, folded)


def shards(snapshot, cotangent, ocean_mask, kernel, norm_gain, norm_shift, weight_in, weight_out):
    reach = TAPS // 2
    levels = lax.axis_size("lev")
    channels = snapshot.shape[0] * levels
    height = snapshot.shape[1] // levels
    width = snapshot.shape[2]
    is_top = lax.axis_index("lev") == levels - 1
    weights = kernel.astype(jnp.float32).reshape(channels, TAPS, TAPS)
    tile = lax.all_to_all(snapshot, "lev", split_axis=1, concat_axis=0, tiled=True)
    regular, folded = tile_pad(tile)
    upper = jnp.where(is_top, folded, regular[:, height + reach :])
    padded = jnp.concatenate([regular[:, : height + reach], upper], axis=1)
    count = height * width
    convolved = taps(padded, weights, height, width)
    residual = padded[:, reach : height + reach, reach : width + reach]
    result, upstream, d_conv = cell_pass(
        convolved.reshape(channels, count),
        residual.reshape(channels, count),
        cotangent.reshape(channels, count),
        ocean_mask.reshape(count),
        norm_gain,
        norm_shift,
        weight_in,
        weight_out,
    )
    d_conv = d_conv.reshape(channels, height, width)
    local_terms = kernel_terms(padded, d_conv, height, width)
    kernel_grad = lax.psum(local_terms, ("lev", "lon"))
    d_regular, d_folded = tile_pad(d_conv)
    adjoint = taps(d_regular, weights[:, ::-1, ::-1], height, width)
    edge = jnp.where(is_top, fold_term(d_folded, weights, width), 0.0)
    adjoint = adjoint.at[:, height - reach :, :].add(edge)
    d_tile = (upstream.reshape(channels, height, width) + adjoint).astype(jnp.bfloat16)
    d_snapshot = lax.all_to_all(d_tile, "lev", split_axis=0, concat_axis=1, tiled=True)
    return (result.reshape(channels, height, width), d_snapshot, kernel_grad)


def solution(mesh):
    placed = (
        P("lev", None, "lon"),
        P(None, "lev", "lon"),
        P("lev", "lon"),
        P(),
        P(),
        P(),
        P(),
        P(),
    )
    return jax.shard_map(
        shards,
        mesh=mesh,
        in_specs=placed,
        out_specs=(P(None, "lev", "lon"), P("lev", None, "lon"), P()),
        check_vma=False,
    )
```

profile of v0, /device:TPU:0, one launch (start us, length us, event | category | flops | bytes accessed | tf_op | source)
XLA Modules:
  0.0 324.4 jit_solution(15254796559230861288)
XLA Ops:
  7.2 11.6 %all_to_all.56 = bf16[96,12,128]{2,0,1:T(8,128)(2,1)S(1)} all-to-all(bf16[96,12,128]{2,0,1:T(8,128)(2,1)} %param.12), channel_id=1, replica_groups=mesh['lev'=4,'lon'=8] {'lev'}, dimensions={1} | all-to-all | bytes 589824 | tf_op jit(solution)/shard_map/all_to_all | solution.py:131
  20.9 7.9 %collective-permute-done.1 = bf16[384,3,128]{2,0,1:T(8,128)(2,1)S(1)} collective-permute-done((bf16[384,3,128]{2,0,1:T(8,128)(2,1)S(1)}, bf16[384,3,128]{2,0,1:T(8,128)(2,1)S(1)}, u32[]{:S(2)}, u32[]{:S(2)}) %collective-permute-start.1) | collective-permute-done | bytes 294944 | tf_op jit(solution)/shard_map/ppermute | solution.py:22
  28.8 4.0 %collective-permute-done = bf16[384,3,128]{2,0,1:T(8,128)(2,1)S(1)} collective-permute-done((bf16[384,3,128]{2,0,1:T(8,128)(2,1)S(1)}, bf16[384,3,128]{2,0,1:T(8,128)(2,1)S(1)}, u32[]{:S(2)}, u32[]{:S(2)}) %collective-permute-start) | collective-permute-done | bytes 294944 | tf_op jit(solution)/shard_map/ppermute | solution.py:21
  35.2 3.6 %collective-permute-start.3 = (bf16[384,9,3]{0,1,2:T(8,128)(2,1)S(1)}, bf16[384,9,3]{0,1,2:T(8,128)(2,1)S(1)}, u32[]{:S(2)}, u32[]{:S(2)}) collective-permute-start(bf16[384,9,3]{0,1,2:T(8,128)(2,1)S(1)} %copy.100), channel_id=1, source_target_pairs={{1,0},{2,1},{3,2},{4,3},{5,4},{6,5},{7,6},{0,7},{9,8},{10,9},{11,1... | collective-permute-start | bytes 62216 | tf_op jit(solution)/shard_map/ppermute | solution.py:22
  42.5 2.6 pad_maximum_fusion
  46.0 4.2 %all-to-all-start.1 = ((bf16[8,48,3,134]{3,1,2,0:T(8,128)(2,1)}), bf16[8,48,3,134]{3,1,2,0:T(8,128)(2,1)}, u32[]{:S(2)}, u32[]{:S(2)}) async-start(bf16[8,48,3,134]{3,1,2,0:T(8,128)(2,1)} %copy.104), calls=%async_computation.1 | async-start | bytes 1179648 | tf_op jit(solution)/shard_map/all_to_all | solution.py:103
  51.6 1.9 copy.109
  57.4 9.6 %all-to-all-done.1 = bf16[8,48,3,134]{3,1,2,0:T(8,128)(2,1)} async-done(((bf16[8,48,3,134]{3,1,2,0:T(8,128)(2,1)}), bf16[8,48,3,134]{3,1,2,0:T(8,128)(2,1)}, u32[]{:S(2)}, u32[]{:S(2)}) %all-to-all-start.1) | async-done | bytes 308768 | tf_op jit(solution)/shard_map/all_to_all | solution.py:103
  67.0 2.0 rev.11
  68.9 4.2 %all-to-all-start.2 = ((bf16[8,48,3,134]{3,1,2,0:T(8,128)(2,1)}), bf16[8,48,3,134]{3,1,2,0:T(8,128)(2,1)}, u32[]{:S(2)}, u32[]{:S(2)}) async-start(bf16[8,48,3,134]{3,1,2,0:T(8,128)(2,1)} %rev.11), calls=%async_computation.2 | async-start | bytes 1179648 | tf_op jit(solution)/shard_map/all_to_all | solution.py:104
  78.5 11.4 %all-to-all-done.2 = bf16[8,48,3,134]{3,1,2,0:T(8,128)(2,1)} async-done(((bf16[8,48,3,134]{3,1,2,0:T(8,128)(2,1)}), bf16[8,48,3,134]{3,1,2,0:T(8,128)(2,1)}, u32[]{:S(2)}, u32[]{:S(2)}) %all-to-all-start.2) | async-done | bytes 308768 | tf_op jit(solution)/shard_map/all_to_all | solution.py:104
  89.9 1.9 copy.148
  91.8 9.6 %reverse.70 = bf16[384,3,256]{2,0,1:T(8,128)(2,1)} reverse(bf16[384,3,256]{2,0,1:T(8,128)(2,1)} %bitcast.88), dimensions={1,2} | reverse | bytes 1179648
  103.9 10.8 %fusion.209 = (f32[3,128]{1,0:T(4,128)S(1)}, f32[384,3,128]{2,0,1:T(8,128)S(1)}) fusion(f32[384,9,134]{2,0,1:T(8,128)S(1)} %maximum_convert_fusion, f32[384]{0:T(512)S(1)} %get-tuple-element.88, f32[384]{0:T(512)S(1)} %get-tuple-element.89, f32[384]{0:T(512)S(1)} %get-tuple-element.90, f32[384]{0:T(512)S(1)} %get-tuple-element.91, f32[384]{0:T(512)S(1)} %copy-done.13, ...), kind=kLoop, calls=%fused_computation.426 | loop fusion | flops 14450304 | bytes 29568000 | tf_op jit(solution)/shard_map/reduce_sum | solution.py:69
  116.0 2.2 convolution_bitcast_fusion.1
  118.2 3.8 %fusion.131 = (f32[384]{0:T(512)S(1)}, f32[384,384]{1,0:T(8,128)S(1)}) fusion(f32[384,3,128]{0,2,1:T(8,128)S(1)} %copy.107, f32[384]{0:T(512)S(1)} %rsqrt_bitcast_fusion, f32[384]{0:T(512)S(1)} %get-tuple-element.170, f32[384]{0:T(512)S(1)} %copy-done.90, bf16[384,1536]{1,0:T(8,128)(2,1)S(1)} %copy-done, bf16[384,384]{0,1:T(8,128)(2,1)S(1)} %copy-done.12, ...), kind=kOutput, calls=%fused_computation.254 | convolution fusion | flops 912604800 | bytes 6199296 | tf_op jit(solution)/shard_map/dot_general | solution.py:89
  124.7 7.9 %collective-permute-done.5 = bf16[384,3,128]{2,0,1:T(8,128)(2,1)S(1)} collective-permute-done((bf16[384,3,128]{2,0,1:T(8,128)(2,1)S(1)}, bf16[384,3,128]{2,0,1:T(8,128)(2,1)S(1)}, u32[]{:S(2)}, u32[]{:S(2)}) %collective-permute-start.5) | collective-permute-done | bytes 294944 | tf_op jit(solution)/shard_map/ppermute | solution.py:22
  132.6 5.7 %collective-permute-done.4 = bf16[384,3,128]{2,0,1:T(8,128)(2,1)S(1)} collective-permute-done((bf16[384,3,128]{2,0,1:T(8,128)(2,1)S(1)}, bf16[384,3,128]{2,0,1:T(8,128)(2,1)S(1)}, u32[]{:S(2)}, u32[]{:S(2)}) %collective-permute-start.4) | collective-permute-done | bytes 294944 | tf_op jit(solution)/shard_map/ppermute | solution.py:21
  141.2 3.8 %collective-permute-start.7 = (bf16[384,9,3]{0,1,2:T(8,128)(2,1)S(1)}, bf16[384,9,3]{0,1,2:T(8,128)(2,1)}, u32[]{:S(2)}, u32[]{:S(2)}) collective-permute-start(bf16[384,9,3]{0,1,2:T(8,128)(2,1)S(1)} %copy.114), channel_id=1, source_target_pairs={{1,0},{2,1},{3,2},{4,3},{5,4},{6,5},{7,6},{0,7},{9,8},{10,9},{11,1... | collective-permute-start | bytes 62216 | tf_op jit(solution)/shard_map/ppermute | solution.py:22
  147.8 1.9 pad_maximum_fusion.1
  151.8 4.9 %all-to-all-start.3 = ((bf16[8,48,3,134]{3,1,2,0:T(8,128)(2,1)}), bf16[8,48,3,134]{3,1,2,0:T(8,128)(2,1)}, u32[]{:S(2)}, u32[]{:S(2)}) async-start(bf16[8,48,3,134]{3,1,2,0:T(8,128)(2,1)} %copy.118), calls=%async_computation.3 | async-start | bytes 1179648 | tf_op jit(solution)/shard_map/all_to_all | solution.py:103
  158.2 12.4 %fusion.75 = (f32[384]{0:T(512)S(1)}, f32[384]{0:T(512)S(1)}, f32[384]{0:T(512)S(1)}, f32[384]{0:T(512)S(1)}, f32[384]{0:T(512)S(1)}, /*index=5*/f32[384]{0:T(51...) fusion(bf16[384,3,128]{2,0,1:T(8,128)(2,1)S(1)} %copy.110, ...), kind=kLoop, calls=%fused_computation.142 | loop fusion | flops 5448960 | bytes 10939392 | tf_op jit(solution)/shard_map/reduce_sum | solution.py:44
  170.6 3.0 all-to-all-done.3
  175.5 3.5 %all-to-all-start.4 = ((bf16[8,48,3,134]{3,1,2,0:T(8,128)(2,1)}), bf16[8,48,3,134]{3,1,2,0:T(8,128)(2,1)S(1)}, u32[]{:S(2)}, u32[]{:S(2)}) async-start(bf16[8,48,3,134]{3,1,2,0:T(8,128)(2,1)} %rev.13), calls=%async_computation.4 | async-start | bytes 1179648 | tf_op jit(solution)/shard_map/all_to_all | solution.py:104
  179.1 9.0 %fusion.73 = (f32[384]{0:T(512)S(1)}, f32[384]{0:T(512)S(1)}, f32[384]{0:T(512)S(1)}, f32[384]{0:T(512)S(1)}, f32[384]{0:T(512)S(1)}, /*index=5*/f32[384]{0:T(51...) fusion(bf16[384,3,128]{2,0,1:T(8,128)(2,1)S(1)} %copy.110, ...), kind=kLoop, calls=%fused_computation.140 | loop fusion | flops 3976320 | bytes 7982592 | tf_op jit(solution)/shard_map/reduce_sum | solution.py:44
  188.3 3.5 %fusion.74 = (f32[384]{0:T(512)S(1)}, f32[384]{0:T(512)S(1)}, f32[384]{0:T(512)S(1)}, f32[384]{0:T(512)S(1)}, f32[384]{0:T(512)S(1)}, /*index=5*/f32[384]{0:T(51...) fusion(bf16[384,3,128]{2,0,1:T(8,128)(2,1)S(1)} %copy.110, ...), kind=kLoop, calls=%fused_computation.141 | loop fusion | flops 5448960 | bytes 10939392 | tf_op jit(solution)/shard_map/reduce_sum | solution.py:44
  192.2 4.4 %stack.206 = f32[384,49]{0,1:T(8,128)} concatenate(f32[384,1]{0,1:T(1,128)S(1)} %stack.157, f32[384,1]{0,1:T(1,128)S(1)} %stack.158, f32[384,1]{0,1:T(1,128)S(1)} %stack.159, f32[384,1]{0,1:T(1,128)S(1)} %stack.160, f32[384,1]{0,1:T(1,128)S(1)} %stack.161, f32[384,1]{0,1:T(1,128)S(1)} %stack.162, f32[384,1]{0,1:T(1,128)S(1)} %stack.163, f32[384,1]{0,1:T(1,128)S(1)} %stack.164, ...), dimensions={1} | concatenate | bytes 150528 | tf_op jit(solution)/shard_map/stack | solution.py:45
  196.6 3.3 %maximum_convert_fusion.1 = f32[384,9,134]{2,0,1:T(8,128)} fusion(bf16[384,3,134]{2,0,1:T(8,128)(2,1)} %get-tuple-element.139, bf16[384,3,134]{2,0,1:T(8,128)(2,1)S(1)} %get-tuple-element.140, bf16[384,3,134]{2,0,1:T(8,128)(2,1)S(1)} %copy-done.7), kind=kLoop, calls=%fused_computation.80 | loop fusion | flops 1389312 | bytes 2778624 | tf_op jit(solution)/shard_map/convert_element_type | solution.py:28
  210.8 11.6 %fusion.79 = bf16[384,3,128]{2,0,1:T(8,128)(2,1)S(1)} fusion(f32[384,9,134]{2,0,1:T(8,128)S(1)} %copy-done.3, f32[384,1,128]{2,0,1:T(8,128)S(1)} %fusion.154, f32[384,1,128]{2,0,1:T(8,128)S(1)} %fusion.140, f32[384,1,128]{2,0,1:T(8,128)S(1)} %fusion.160, f32[3,128]{1,0:T(4,128)} %get-tuple-element.168, f32[384]{0:T(512)S(1)} %get-tuple-element.88, ...), kind=kLoop, calls=%fused_computation.147 | loop fusion | flops 15482880 | bytes 30157824 | tf_op jit(solution)/shard_map/convert_element_type | solution.py:155
  223.4 4.3 %all-to-all-start.5 = ((bf16[384,3,128]{2,1,0:T(4,128)(2,1)}), bf16[384,3,128]{2,1,0:T(4,128)(2,1)}, u32[]{:S(2)}, u32[]{:S(2)}) async-start(bf16[384,3,128]{2,1,0:T(4,128)(2,1)} %copy.141), calls=%async_computation.5 | async-start | bytes 786432 | tf_op jit(solution)/shard_map/all_to_all | solution.py:156
  227.7 7.5 %fusion.20 = bf16[384,384]{0,1:T(8,128)(2,1)} fusion(f32[384,384]{0,1:T(8,128)} %reshape.476, bf16[1536,384]{1,0:T(8,128)(2,1)} %param.19, f32[1536,384]{0,1:T(8,128)S(1)} %copy-done.6, f32[384]{0:T(512)} %copy-done.89), kind=kOutput, calls=%fused_computation.86 | convolution fusion | flops 491765760 | bytes 4425216 | tf_op jit(solution)/shard_map/dot_general | solution.py:79
  238.8 77.2 %all-reduce.2.cloned.1.call-done = f32[384,49]{0,1:T(8,128)} async-done(((f32[384,49]{0,1:T(8,128)}), f32[384,49]{0,1:T(8,128)}) %all-reduce.2.cloned.1.call-update) | async-done | bytes 75280 | tf_op jit(solution)/shard_map/psum | solution.py:150
  (313 shorter events, 53.1 us)
Async XLA Ops:
  7.2 108.8 %copy-start = (bf16[384,1536]{1,0:T(8,128)(2,1)S(1)}, bf16[384,1536]{1,0:T(8,128)(2,1)}, u32[]{:S(2)}) copy-start(bf16[384,1536]{1,0:T(8,128)(2,1)} %param.18) | copy-start | bytes 3538948
  18.8 10.0 %copy-start.4 = (bf16[96,12,128]{2,0,1:T(8,128)(2,1)}, bf16[96,12,128]{2,0,1:T(8,128)(2,1)S(1)}, u32[]{:S(2)}) copy-start(bf16[96,12,128]{2,0,1:T(8,128)(2,1)S(1)} %all_to_all.56) | copy-start | bytes 884740
  18.8 10.0 %collective-permute-start.1 = (bf16[384,3,128]{2,0,1:T(8,128)(2,1)S(1)}, bf16[384,3,128]{2,0,1:T(8,128)(2,1)S(1)}, u32[]{:S(2)}, u32[]{:S(2)}) collective-permute-start(bf16[384,3,128]{2,0,1:T(8,128)(2,1)S(1)} %bitcast.82), channel_id=1, source_target_pairs={{8,0},{16,8},{24,16},{0,24},{9,1},{17,9},{25,17},{1,25},{10,2},{18... | collective-permute-start | bytes 884744 | tf_op jit(solution)/shard_map/ppermute | solution.py:22
  19.5 13.3 %collective-permute-start = (bf16[384,3,128]{2,0,1:T(8,128)(2,1)S(1)}, bf16[384,3,128]{2,0,1:T(8,128)(2,1)S(1)}, u32[]{:S(2)}, u32[]{:S(2)}) collective-permute-start(bf16[384,3,128]{2,0,1:T(8,128)(2,1)S(1)} %bitcast.83), channel_id=1, source_target_pairs={{0,8},{8,16},{16,24},{24,0},{1,9},{9,17},{17,25},{25,1},{2,10},{10... | collective-permute-start | bytes 884744 | tf_op jit(solution)/shard_map/ppermute | solution.py:21
  34.6 5.2 %collective-permute-start.2 = (bf16[384,9,3]{0,1,2:T(8,128)(2,1)S(1)}, bf16[384,9,3]{0,1,2:T(8,128)(2,1)S(1)}, u32[]{:S(2)}, u32[]{:S(2)}) collective-permute-start(bf16[384,9,3]{0,1,2:T(8,128)(2,1)S(1)} %copy.99), channel_id=1, source_target_pairs={{0,1},{1,2},{2,3},{3,4},{4,5},{5,6},{6,7},{7,0},{8,9},{9,10},{10,1... | collective-permute-start | bytes 62216 | tf_op jit(solution)/shard_map/ppermute | solution.py:21
  35.2 5.9 %collective-permute-start.3 = (bf16[384,9,3]{0,1,2:T(8,128)(2,1)S(1)}, bf16[384,9,3]{0,1,2:T(8,128)(2,1)S(1)}, u32[]{:S(2)}, u32[]{:S(2)}) collective-permute-start(bf16[384,9,3]{0,1,2:T(8,128)(2,1)S(1)} %copy.100), channel_id=1, source_target_pairs={{1,0},{2,1},{3,2},{4,3},{5,4},{6,5},{7,6},{0,7},{9,8},{10,9},{11,1... | collective-permute-start | bytes 62216 | tf_op jit(solution)/shard_map/ppermute | solution.py:22
  46.0 21.0 %all-to-all-start.1 = ((bf16[8,48,3,134]{3,1,2,0:T(8,128)(2,1)}), bf16[8,48,3,134]{3,1,2,0:T(8,128)(2,1)}, u32[]{:S(2)}, u32[]{:S(2)}) async-start(bf16[8,48,3,134]{3,1,2,0:T(8,128)(2,1)} %copy.104), calls=%async_computation.1 | async-start | bytes 1179648 | tf_op jit(solution)/shard_map/all_to_all | solution.py:103
  68.9 21.0 %all-to-all-start.2 = ((bf16[8,48,3,134]{3,1,2,0:T(8,128)(2,1)}), bf16[8,48,3,134]{3,1,2,0:T(8,128)(2,1)}, u32[]{:S(2)}, u32[]{:S(2)}) async-start(bf16[8,48,3,134]{3,1,2,0:T(8,128)(2,1)} %rev.11), calls=%async_computation.2 | async-start | bytes 1179648 | tf_op jit(solution)/shard_map/all_to_all | solution.py:104
  103.5 11.2 %copy-start.1 = (f32[384,9,134]{2,0,1:T(8,128)}, f32[384,9,134]{2,0,1:T(8,128)S(1)}, u32[]{:S(2)}) copy-start(f32[384,9,134]{2,0,1:T(8,128)S(1)} %maximum_convert_fusion) | copy-start | bytes 5557252
  122.7 10.0 %collective-permute-start.5 = (bf16[384,3,128]{2,0,1:T(8,128)(2,1)S(1)}, bf16[384,3,128]{2,0,1:T(8,128)(2,1)S(1)}, u32[]{:S(2)}, u32[]{:S(2)}) collective-permute-start(bf16[384,3,128]{2,0,1:T(8,128)(2,1)S(1)} %copy.110), channel_id=1, source_target_pairs={{8,0},{16,8},{24,16},{0,24},{9,1},{17,9},{25,17},{1,25},{10,2},{18... | collective-permute-start | bytes 884744 | tf_op jit(solution)/shard_map/ppermute | solution.py:22
  123.9 14.4 %collective-permute-start.4 = (bf16[384,3,128]{2,0,1:T(8,128)(2,1)S(1)}, bf16[384,3,128]{2,0,1:T(8,128)(2,1)S(1)}, u32[]{:S(2)}, u32[]{:S(2)}) collective-permute-start(bf16[384,3,128]{2,0,1:T(8,128)(2,1)S(1)} %copy.110), channel_id=1, source_target_pairs={{0,8},{8,16},{16,24},{24,0},{1,9},{9,17},{17,25},{25,1},{2,10},{10... | collective-permute-start | bytes 884744 | tf_op jit(solution)/shard_map/ppermute | solution.py:21
  140.6 5.4 %collective-permute-start.6 = (bf16[384,9,3]{0,1,2:T(8,128)(2,1)}, bf16[384,9,3]{0,1,2:T(8,128)(2,1)S(1)}, u32[]{:S(2)}, u32[]{:S(2)}) collective-permute-start(bf16[384,9,3]{0,1,2:T(8,128)(2,1)} %copy.113), channel_id=1, source_target_pairs={{0,1},{1,2},{2,3},{3,4},{4,5},{5,6},{6,7},{7,0},{8,9},{9,10},{10,1... | collective-permute-start | bytes 62216 | tf_op jit(solution)/shard_map/ppermute | solution.py:21
  141.2 5.4 %collective-permute-start.7 = (bf16[384,9,3]{0,1,2:T(8,128)(2,1)S(1)}, bf16[384,9,3]{0,1,2:T(8,128)(2,1)}, u32[]{:S(2)}, u32[]{:S(2)}) collective-permute-start(bf16[384,9,3]{0,1,2:T(8,128)(2,1)S(1)} %copy.114), channel_id=1, source_target_pairs={{1,0},{2,1},{3,2},{4,3},{5,4},{6,5},{7,6},{0,7},{9,8},{10,9},{11,1... | collective-permute-start | bytes 62216 | tf_op jit(solution)/shard_map/ppermute | solution.py:22
  149.8 7.0 %copy-start.5 = (bf16[96,12,128]{2,0,1:T(8,128)(2,1)S(1)}, bf16[96,12,128]{2,0,1:T(8,128)(2,1)}, u32[]{:S(2)}) copy-start(bf16[96,12,128]{2,0,1:T(8,128)(2,1)} %copy-done.4) | copy-start | bytes 884740
  151.8 21.8 %all-to-all-start.3 = ((bf16[8,48,3,134]{3,1,2,0:T(8,128)(2,1)}), bf16[8,48,3,134]{3,1,2,0:T(8,128)(2,1)}, u32[]{:S(2)}, u32[]{:S(2)}) async-start(bf16[8,48,3,134]{3,1,2,0:T(8,128)(2,1)} %copy.118), calls=%async_computation.3 | async-start | bytes 1179648 | tf_op jit(solution)/shard_map/all_to_all | solution.py:103
  175.5 24.3 %all-to-all-start.4 = ((bf16[8,48,3,134]{3,1,2,0:T(8,128)(2,1)}), bf16[8,48,3,134]{3,1,2,0:T(8,128)(2,1)S(1)}, u32[]{:S(2)}, u32[]{:S(2)}) async-start(bf16[8,48,3,134]{3,1,2,0:T(8,128)(2,1)} %rev.13), calls=%async_computation.4 | async-start | bytes 1179648 | tf_op jit(solution)/shard_map/all_to_all | solution.py:104
  179.1 136.9 %all-reduce.2.cloned.1.call-start = ((), (), s32[]{:S(2)}) async-start(), calls=%async_computation.6 | async-start | bytes 172032 | tf_op jit(solution)/shard_map/psum | solution.py:150
  179.1 9.1 %copy-start.2 = (f32[384,9,134]{2,0,1:T(8,128)S(1)}, f32[384,9,134]{2,0,1:T(8,128)}, u32[]{:S(2)}) copy-start(f32[384,9,134]{2,0,1:T(8,128)} %copy-done.1) | copy-start | bytes 5557252
  188.3 8.3 %copy-start.7 = (bf16[384,3,134]{2,0,1:T(8,128)(2,1)S(1)}, bf16[384,3,134]{2,0,1:T(8,128)(2,1)}, u32[]{:S(2)}) copy-start(bf16[384,3,134]{2,0,1:T(8,128)(2,1)} %get-tuple-element.138) | copy-start | bytes 926212
  200.5 6.8 %copy-start.14 = (f32[384]{0:T(512)S(1)}, f32[384]{0:T(512)}, u32[]{:S(2)}) copy-start(f32[384]{0:T(512)} %get-tuple-element.92) | copy-start | bytes 4612
  200.5 6.8 %copy-start.17 = (f32[384]{0:T(512)S(1)}, f32[384]{0:T(512)}, u32[]{:S(2)}) copy-start(f32[384]{0:T(512)} %get-tuple-element.93) | copy-start | bytes 4612
  200.5 6.8 %copy-start.20 = (f32[384]{0:T(512)S(1)}, f32[384]{0:T(512)}, u32[]{:S(2)}) copy-start(f32[384]{0:T(512)} %get-tuple-element.94) | copy-start | bytes 4612
  201.2 6.8 %copy-start.23 = (f32[384]{0:T(512)S(1)}, f32[384]{0:T(512)}, u32[]{:S(2)}) copy-start(f32[384]{0:T(512)} %get-tuple-element.95) | copy-start | bytes 4612
  201.2 6.8 %copy-start.26 = (f32[384]{0:T(512)S(1)}, f32[384]{0:T(512)}, u32[]{:S(2)}) copy-start(f32[384]{0:T(512)} %get-tuple-element.96) | copy-start | bytes 4612
  201.2 6.8 %copy-start.29 = (f32[384]{0:T(512)S(1)}, f32[384]{0:T(512)}, u32[]{:S(2)}) copy-start(f32[384]{0:T(512)} %get-tuple-element.97) | copy-start | bytes 4612
  201.2 6.8 %copy-start.32 = (f32[384]{0:T(512)S(1)}, f32[384]{0:T(512)}, u32[]{:S(2)}) copy-start(f32[384]{0:T(512)} %get-tuple-element.98) | copy-start | bytes 4612
  201.2 6.8 %copy-start.35 = (f32[384]{0:T(512)S(1)}, f32[384]{0:T(512)}, u32[]{:S(2)}) copy-start(f32[384]{0:T(512)} %get-tuple-element.99) | copy-start | bytes 4612
  201.2 6.8 %copy-start.38 = (f32[384]{0:T(512)S(1)}, f32[384]{0:T(512)}, u32[]{:S(2)}) copy-start(f32[384]{0:T(512)} %get-tuple-element.100) | copy-start | bytes 4612
  201.2 6.8 %copy-start.41 = (f32[384]{0:T(512)S(1)}, f32[384]{0:T(512)}, u32[]{:S(2)}) copy-start(f32[384]{0:T(512)} %get-tuple-element.101) | copy-start | bytes 4612
  203.8 5.2 %copy-start.44 = (f32[384]{0:T(512)S(1)}, f32[384]{0:T(512)}, u32[]{:S(2)}) copy-start(f32[384]{0:T(512)} %get-tuple-element.107) | copy-start | bytes 4612
  210.8 16.9 %copy-start.6 = (f32[1536,384]{0,1:T(8,128)S(1)}, f32[1536,384]{0,1:T(8,128)}, u32[]{:S(2)}) copy-start(f32[1536,384]{0,1:T(8,128)} %convolution_bitcast_fusion.1) | copy-start | bytes 7077892
  223.4 13.7 %all-to-all-start.5 = ((bf16[384,3,128]{2,1,0:T(4,128)(2,1)}), bf16[384,3,128]{2,1,0:T(4,128)(2,1)}, u32[]{:S(2)}, u32[]{:S(2)}) async-start(bf16[384,3,128]{2,1,0:T(4,128)(2,1)} %copy.141), calls=%async_computation.5 | async-start | bytes 786432 | tf_op jit(solution)/shard_map/all_to_all | solution.py:156
  (73 other events, 148.2 us)
Sparse Core Ops, SparseCore 0:
  196.7 119.2 all-reduce.1
where the time goes:
time: 328 us; the launch traced here: 324 us
  waiting for transfers between devices  129 us (39%)
  other arithmetic  65.5 us (20%)
  local copies, waits for them, and re-layouts  55.8 us (17%)
  starting transfers between devices  32.8 us (10%)
  between operations  16.2 us (5%)
  matrix products  13.5 us (4%)
  blocking collectives  11.6 us (4%)
    psum x1, waiting for transfers between devices, shards(): kernel_grad = lax.psum(local_terms, ('lev', 'lon'))  77.2 us
    reduce_sum x3, other arithmetic, kernel_terms(): terms.append(jnp.sum(flat * piece, axis=(1, 2)))  24.8 us
    ppermute x4, waiting for transfers between devices, padded_2(): after = lax.ppermute(leading, axis, down)  15.9 us
    unnamed x185, local copies, waits for them, and re-layouts  15.3 us
    all_to_all x2, waiting for transfers between devices, fold_edge(): lax.all_to_all(blocks, 'lon', split_axis=0, concat_axis=0, tiled=True)  12.6 us
    ppermute x4, waiting for transfers between devices, padded_2(): before = lax.ppermute(last, axis, up)  11.8 us
    all_to_all x1, blocking collectives, shards(): lax.all_to_all(snapshot, 'lev', split_axis=1, concat_axis=0, tiled=True)  11.6 us
    convert_element_type x1, other arithmetic, shards(): (upstream.reshape(channels, height, width) + adjoint).astype(jnp.bfloat16)  11.6 us
  transfers between devices with their start and end apart: 14, of which 11 were waited for; matrix products, arithmetic and copies ran while one was open for 25% of the time, Pallas kernels for 0%

commit v1 on v0

v1 whole, which is shorter than its diff:
```python
import jax
import jax.numpy as jnp
from jax import lax
from jax.experimental import pallas as pl
from jax.experimental.pallas import tpu as pltpu
from jax.sharding import PartitionSpec as P

TAPS = 7
REACH = TAPS // 2
EPSILON = 1e-06
ROOT_HALF = 0.7071067811865476
INV_ROOT_TAU = 0.3989422804014327
F32 = jnp.float32
BF16 = jnp.bfloat16
VMEM = pl.BlockSpec(memory_space=pltpu.VMEM)
SMEM = pl.BlockSpec(memory_space=pltpu.SMEM)
SPAN = 2 * REACH
LIMIT = 48 * 1024 * 1024


def call(body, out, specs, scratch, flops, moved, name):
    return pl.pallas_call(
        body,
        out_shape=out,
        in_specs=specs,
        out_specs=jax.tree.map(lambda _: VMEM, out),
        scratch_shapes=scratch,
        compiler_params=pltpu.CompilerParams(vmem_limit_bytes=LIMIT),
        cost_estimate=pl.CostEstimate(flops=flops, bytes_accessed=moved, transcendentals=0),
        name=name,
    )


def shaped(*shape, dtype=BF16):
    return jax.ShapeDtypeStruct(shape, dtype)


def lanes_of(shape):
    return lax.broadcasted_iota(jnp.int32, shape, len(shape) - 1)


def groups_of(rows):
    per = rows
    while per * SPAN > 128 or rows % per:
        per -= 1
    return rows // per, per


def pack_edges(read, odd, off_ref, on_ref, rows, channels, width):
    count, per = groups_of(rows)
    lane = lanes_of((channels, width))
    for group in range(count):
        off = jnp.zeros((channels, width), F32)
        on = jnp.zeros((channels, width), F32)
        for place in range(per):
            line = read(group * per + place)
            base = SPAN * place
            first = pltpu.roll(line, base % width, 1)
            last = pltpu.roll(line, base % width, 1)
            in_first = (lane >= base) & (lane < base + REACH)
            spot = (base - REACH) % width
            in_last = (lane >= spot) & (lane < spot + REACH)
            far = jnp.where(odd == 1, in_last.astype(jnp.int32), in_first.astype(jnp.int32))
            near = jnp.where(odd == 1, in_first.astype(jnp.int32), in_last.astype(jnp.int32))
            off = jnp.where(far == 1, first, off)
            on = jnp.where(near == 1, last, on)
        off_ref[group] = off.astype(BF16)
        on_ref[group] = on.astype(BF16)


def near_edges(off, on, odd, lane, width):
    right = ((lane % SPAN < REACH) & (lane < width - REACH)).astype(jnp.int32)
    use_on = jnp.where(odd == 1, 1 - right, right)
    return jnp.where(use_on == 1, on, off)


def flip_lanes(value, width):
    row = lax.broadcasted_iota(jnp.int32, (width, width), 0)
    col = lax.broadcasted_iota(jnp.int32, (width, width), 1)
    exchange = (row + col == width - 1).astype(BF16)
    return jnp.dot(value, exchange, preferred_element_type=F32)


def fill(lines, edges, read, off_ref, on_ref, top_ref, mate_ref, top_off_ref, odd, rows, channels, width):
    count, per = groups_of(rows)
    lane = lanes_of((channels, width))
    for group in range(count):
        mixed = near_edges(off_ref[group].astype(F32), on_ref[group].astype(F32), odd, lane, width)
        for place in range(per):
            row = group * per + place
            lines[row] = read(row)
            edges[row] = pltpu.roll(mixed, (width - SPAN * place) % width, 1)
    for depth in range(REACH):
        row = rows - 1 - depth
        group, place = row // per, row % per
        far = pltpu.roll(top_off_ref[group].astype(F32), (width - SPAN * place) % width, 1)
        near = mate_ref[REACH - 1 - depth].astype(F32)
        right = (lane < width // 2).astype(jnp.int32)
        use_near = jnp.where(odd == 1, right, 1 - right)
        edge = jnp.where(use_near == 1, near, far)
        lines[rows + depth] = flip_lanes(top_ref[REACH - 1 - depth], width)
        edges[rows + depth] = flip_lanes(edge.astype(BF16), width)


def shifted(line, edge, step, lane, width):
    if step == 0:
        return line
    if step > 0:
        return pltpu.roll(jnp.where(lane < step, edge, line), width - step, 1)
    return pltpu.roll(jnp.where(lane >= width + step, edge, line), -step, 1)


def prepare_body(levels, channels, rows, width):
    height = rows // levels

    def body(place_ref, snap_ref, off_ref, on_ref, top_ref, *rest):
        sends, lines = rest[:levels], rest[levels]
        lev, odd = place_ref[0], place_ref[1]
        lines[...] = jnp.swapaxes(snap_ref[...].astype(F32), 0, 1)
        for hop in range(levels):
            start = (lev ^ hop) * height
            sends[hop][...] = lines[pl.ds(start, height)].astype(BF16)
        top_ref[...] = lines[rows - REACH :].astype(BF16)
        pack_edges(lambda row: lines[row], odd, off_ref, on_ref, rows, channels, width)

    return body


def conv_body(levels, channels, rows, width):
    height = rows // levels

    def body(place_ref, snap_ref, off_ref, on_ref, top_ref, mate_ref, top_off_ref, weight_ref, *rest):
        sends, (lines, edges, total) = rest[:levels], rest[levels:]
        lev, odd = place_ref[0], place_ref[1]
        total[...] = jnp.swapaxes(snap_ref[...].astype(F32), 0, 1)
        fill(lines, edges, lambda row: total[row], off_ref, on_ref, top_ref, mate_ref, top_off_ref, odd, rows, channels, width)
        lane = lanes_of((8, width))

        def step(block, carry):
            span = pl.ds(block * 8, 8)
            weights = weight_ref[span, :]
            sums = [None] * rows
            for col in range(TAPS):
                taps = [jnp.broadcast_to(weights[:, a * TAPS + col : a * TAPS + col + 1], (8, width)) for a in range(TAPS)]
                for source in range(rows + REACH):
                    moved = shifted(lines[source, span, :], edges[source, span, :], col - REACH, lane, width)
                    for a in range(TAPS):
                        row = source - a + REACH
                        if 0 <= row < rows:
                            term = taps[a] * moved
                            sums[row] = term if sums[row] is None else sums[row] + term
            for row in range(rows):
                total[row, span, :] = sums[row]
            return carry

        lax.fori_loop(0, channels // 8, step, 0)
        for hop in range(levels):
            sends[hop][...] = total[pl.ds((lev ^ hop) * height, height)].astype(BF16)

    return body


def cotangent_body(levels, channels, height, width):
    def body(place_ref, cot_ref, mask_ref, up_ref, *rest):
        sends, lines = rest[:levels], rest[levels]
        lev = place_ref[0]
        wet = mask_ref[...].astype(F32)
        lines[...] = jnp.swapaxes(cot_ref[...].astype(F32), 0, 1) * wet[:, None, :]
        for row in range(height):
            up_ref[:, row * width : (row + 1) * width] = lines[row].astype(BF16)
        for hop in range(levels):
            start = pl.multiple_of((lev ^ hop) * channels, 8)
            for row in range(height):
                sends[hop][row] = lines[row, pl.ds(start, channels), :].astype(BF16)

    return body


def cell_body(levels, channels, height, width, chunk):
    total_channels = levels * channels
    cells = height * width

    def body(place_ref, *refs):
        convs, snaps, refs = refs[:levels], refs[levels : 2 * levels], refs[2 * levels :]
        up_ref, mask_ref, gain_ref, shift_ref, win_ref, wint_ref, wout_ref, woutt_ref = refs[:8]
        result_ref, sends = refs[8], refs[9 : 9 + levels]
        field, d_lifted, projected = refs[9 + levels :]
        lev = place_ref[0]
        for hop in range(levels):
            start = pl.multiple_of((lev ^ hop) * channels, 8)
            for row in range(height):
                field[pl.ds(start, channels), row * width : (row + 1) * width] = convs[hop][row].astype(F32)
        convolved = field[...]
        centre = jnp.mean(convolved, axis=0, keepdims=True)
        centred = convolved - centre
        spread = jnp.mean(centred * centred, axis=0, keepdims=True)
        rstd = lax.rsqrt(spread + EPSILON)
        normed = centred * rstd
        field[...] = normed
        gain = gain_ref[...]
        lifted = (normed * gain + shift_ref[...]).astype(BF16)
        upstream = up_ref[...]
        features = wout_ref.shape[0]
        for piece in range(features // chunk):
            span = slice(piece * chunk, (piece + 1) * chunk)
            hidden = jnp.dot(wint_ref[span, :], lifted, preferred_element_type=F32)
            d_active = jnp.dot(wout_ref[span, :], upstream, preferred_element_type=F32)
            half = 0.5 * (1.0 + lax.erf(hidden * ROOT_HALF))
            active = (hidden * half).astype(BF16)
            slope = half + hidden * jnp.exp(-0.5 * hidden * hidden) * INV_ROOT_TAU
            d_hidden = (d_active * slope).astype(BF16)
            out = jnp.dot(woutt_ref[:, span], active, preferred_element_type=F32)
            back = jnp.dot(win_ref[:, span], d_hidden, preferred_element_type=F32)
            if piece == 0:
                projected[...] = out
                d_lifted[...] = back
            else:
                projected[...] += out
                d_lifted[...] += back
        for hop in range(levels):
            start = pl.multiple_of((lev ^ hop) * channels, 8)
            for row in range(height):
                wet = mask_ref[row : row + 1, :].astype(F32)
                value = snaps[hop][row].astype(F32) + projected[pl.ds(start, channels), row * width : (row + 1) * width]
                projected[pl.ds(start, channels), row * width : (row + 1) * width] = wet * value
        for row in range(height):
            result_ref[row] = projected[:, row * width : (row + 1) * width].astype(BF16)
        d_normed = d_lifted[...] * gain
        normed = field[...]
        first = jnp.mean(d_normed, axis=0, keepdims=True)
        second = jnp.mean(d_normed * normed, axis=0, keepdims=True)
        field[...] = rstd * (d_normed - first - normed * second)
        for hop in range(levels):
            start = pl.multiple_of((lev ^ hop) * channels, 8)
            for row in range(height):
                sends[hop][row] = field[pl.ds(start, channels), row * width : (row + 1) * width].astype(BF16)

    return body


def gather_body(levels, channels, rows, width):
    height = rows // levels

    def body(place_ref, *refs):
        blocks, (lines_ref, off_ref, on_ref, top_ref, lines) = refs[:levels], refs[levels:]
        lev, odd = place_ref[0], place_ref[1]
        for hop in range(levels):
            lines[pl.ds((lev ^ hop) * height, height)] = blocks[hop][...].astype(F32)
        lines_ref[...] = lines[...].astype(BF16)
        top_ref[...] = lines[rows - REACH :].astype(BF16)
        pack_edges(lambda row: lines[row], odd, off_ref, on_ref, rows, channels, width)

    return body


def kernel_body(channels, rows, width):
    def body(place_ref, snap_ref, off_ref, on_ref, top_ref, mate_ref, top_off_ref, d_ref, out_ref, lines, edges, source_lines, d_lines):
        odd = place_ref[1]
        source_lines[...] = jnp.swapaxes(snap_ref[...].astype(F32), 0, 1)
        d_lines[...] = d_ref[...].astype(F32)
        fill(lines, edges, lambda row: source_lines[row], off_ref, on_ref, top_ref, mate_ref, top_off_ref, odd, rows, channels, width)
        lane = lanes_of((8, width))
        out_lane = lanes_of((8, 128))

        def step(block, carry):
            span = pl.ds(block * 8, 8)
            grad = [d_lines[row, span, :] for row in range(rows)]
            found = jnp.zeros((8, 128), F32)
            for col in range(TAPS):
                sums = [None] * TAPS
                for source in range(rows + REACH):
                    moved = shifted(lines[source, span, :], edges[source, span, :], col - REACH, lane, width)
                    for a in range(TAPS):
                        row = source - a + REACH
                        if 0 <= row < rows:
                            term = grad[row] * moved
                            sums[a] = term if sums[a] is None else sums[a] + term
                for a in range(TAPS):
                    found = jnp.where(out_lane == a * TAPS + col, jnp.sum(sums[a], axis=1, keepdims=True), found)
            out_ref[span, :] = found
            return carry

        lax.fori_loop(0, channels // 8, step, 0)

    return body


def adjoint_body(levels, channels, rows, width):
    height = rows // levels

    def body(place_ref, d_ref, off_ref, on_ref, top_ref, mate_ref, top_off_ref, weight_ref, *refs):
        ups, (out_ref, lines, edges, total) = refs[:levels], refs[levels:]
        lev, odd = place_ref[0], place_ref[1]
        fill(lines, edges, lambda row: d_ref[row].astype(F32), off_ref, on_ref, top_ref, mate_ref, top_off_ref, odd, rows, channels, width)
        for hop in range(levels):
            total[pl.ds((lev ^ hop) * height, height)] = ups[hop][...].astype(F32)
        lane = lanes_of((8, width))

        def step(block, carry):
            span = pl.ds(block * 8, 8)
            weights = weight_ref[span, :]
            sums = [None] * rows
            for col in range(TAPS):
                taps = [jnp.broadcast_to(weights[:, a * TAPS + col : a * TAPS + col + 1], (8, width)) for a in range(TAPS)]
                for source in range(rows):
                    moved = shifted(lines[source, span, :], edges[source, span, :], REACH - col, lane, width)
                    for a in range(TAPS):
                        row = source + a - REACH
                        if 0 <= row < rows:
                            term = taps[a] * moved
                            sums[row] = term if sums[row] is None else sums[row] + term
                for source in range(REACH):
                    moved = shifted(lines[rows + source, span, :], edges[rows + source, span, :], col - REACH, lane, width)
                    for depth in range(REACH - source):
                        row = rows - 1 - depth
                        sums[row] = sums[row] + taps[REACH + 1 + depth + source] * moved
            for row in range(rows):
                total[row, span, :] = total[row, span, :] + sums[row]
            return carry

        lax.fori_loop(0, channels // 8, step, 0)
        out_ref[...] = jnp.swapaxes(total[...], 0, 1).astype(BF16)

    return body


def across(value, axis, target):
    count = lax.axis_size(axis)
    return lax.ppermute(value, axis, [(i, target(i) % count) for i in range(count)])


def level_swap(blocks):
    return [blocks[0]] + [across(blocks[hop], "lev", lambda i: i ^ hop) for hop in range(1, len(blocks))]


def edge_swap(off, on, top):
    lanes = lax.axis_size("lon")
    near = across(on, "lon", lambda i: i ^ 1)
    far = across(off, "lon", lambda i: i + 1 if i % 2 else i - 1)
    folded = across(top, "lon", lambda i: lanes - 1 - i)
    fold_far = across(off, "lon", lambda i: lanes - 2 - i if i % 2 else lanes - i)
    mate = across(folded, "lon", lambda i: i ^ 1)
    return far, near, folded, mate, fold_far


def shards(snapshot, cotangent, ocean_mask, kernel, norm_gain, norm_shift, weight_in, weight_out):
    levels = lax.axis_size("lev")
    lanes = lax.axis_size("lon")
    channels, rows, width = snapshot.shape
    height = rows // levels
    total_channels = channels * levels
    features = weight_in.shape[1]
    cells = height * width
    lev = lax.axis_index("lev")
    place = jnp.stack([lev, lax.axis_index("lon") % 2]).astype(jnp.int32)
    groups = groups_of(rows)[0]
    weights = lax.dynamic_slice_in_dim(kernel, lev * channels, channels, 0).astype(F32)
    weights = jnp.pad(weights, ((0, 0), (0, 128 - TAPS * TAPS)))
    block = shaped(height, channels, width)
    pack = shaped(groups, channels, width)
    top_shape = shaped(REACH, channels, width)
    field = pltpu.VMEM((rows, channels, width), F32)
    deep = pltpu.VMEM((rows + REACH, channels, width), F32)
    moved = channels * rows * width * 2

    off, on, top, *snap_sends = call(
        prepare_body(levels, channels, rows, width),
        [pack, pack, top_shape] + [block] * levels,
        [SMEM, VMEM],
        [field],
        moved,
        2 * moved,
        "prepare",
    )(place, snapshot)
    snap_edges = edge_swap(off, on, top)
    snaps = level_swap(snap_sends)
    upstream, *up_sends = call(
        cotangent_body(levels, channels, height, width),
        [shaped(total_channels, cells)] + [block] * levels,
        [SMEM, VMEM, VMEM],
        [pltpu.VMEM((height, total_channels, width), F32)],
        moved,
        2 * moved,
        "cotangent",
    )(place, cotangent, ocean_mask)
    ups = level_swap(up_sends)
    conv_sends = call(
        conv_body(levels, channels, rows, width),
        [block] * levels,
        [SMEM] + [VMEM] * 7,
        [deep, deep, field],
        98 * moved,
        2 * moved,
        "depthwise",
    )(place, snapshot, *snap_edges, weights)
    convs = level_swap(conv_sends)
    cell_fields = [pltpu.VMEM((total_channels, cells), F32)] * 3
    result, *d_sends = call(
        cell_body(levels, channels, height, width, 256),
        [shaped(height, total_channels, width)] + [block] * levels,
        [SMEM] + [VMEM] * (2 * levels + 8),
        cell_fields,
        8 * total_channels * features * cells,
        10 * moved,
        "cells",
    )(
        place,
        *convs,
        *snaps,
        upstream,
        ocean_mask,
        norm_gain[:, None],
        norm_shift[:, None],
        weight_in,
        weight_in.T,
        weight_out,
        weight_out.T,
    )
    d_blocks = level_swap(d_sends)
    d_lines, off, on, top = call(
        gather_body(levels, channels, rows, width),
        [shaped(rows, channels, width), pack, pack, top_shape],
        [SMEM] + [VMEM] * levels,
        [field],
        moved,
        2 * moved,
        "regroup",
    )(place, *d_blocks)
    d_edges = edge_swap(off, on, top)
    terms = call(
        kernel_body(channels, rows, width),
        shaped(channels, 128, dtype=F32),
        [SMEM] + [VMEM] * 7,
        [deep, deep, field, field],
        98 * moved,
        2 * moved,
        "kernel_terms",
    )(place, snapshot, *snap_edges, d_lines)
    hop = 1
    while hop < lanes:
        terms = terms + across(terms, "lon", lambda i: i ^ hop)
        hop *= 2
    parts = level_swap([terms] * levels)
    stacked = jnp.zeros((levels, channels, 128), F32)
    for hop, part in enumerate(parts):
        stacked = lax.dynamic_update_slice(stacked, part[None], (lev ^ hop, 0, 0))
    kernel_grad = stacked.reshape(total_channels, 128)[:, : TAPS * TAPS]
    d_snapshot = call(
        adjoint_body(levels, channels, rows, width),
        shaped(channels, rows, width),
        [SMEM] + [VMEM] * (7 + levels),
        [deep, deep, field],
        98 * moved,
        2 * moved,
        "adjoint",
    )(place, d_lines, *d_edges, weights, *ups)
    return (jnp.swapaxes(result, 0, 1), d_snapshot, kernel_grad)


def solution(mesh):
    placed = (
        P("lev", None, "lon"),
        P(None, "lev", "lon"),
        P("lev", "lon"),
        P(),
        P(),
        P(),
        P(),
        P(),
    )
    return jax.shard_map(
        shards,
        mesh=mesh,
        in_specs=placed,
        out_specs=(P(None, "lev", "lon"), P("lev", None, "lon"), P()),
        check_vma=False,
    )
```

time: 328 us -> 84.6 us (0.26)
  waiting for transfers between devices: 129 us -> 14.5 us
  other arithmetic: 65.5 us -> 0.11 us
  local copies, waits for them, and re-layouts: 55.8 us -> 13.4 us
  Pallas kernels: 0 us -> 24.5 us
  between operations: 16.2 us -> 0.95 us
  matrix products: 13.5 us -> 0 us
  blocking collectives: 11.6 us -> 0 us
    psum x1 -> x0, waiting for transfers between devices: 77.2 us -> none  [shards(): kernel_grad = lax.psum(local_terms, ('lev', 'lon'))]
    reduce_sum x6 -> x0, other arithmetic: 35.8 us -> none  [the longest x3 24.8 us: kernel_terms(): terms.append(jnp.sum(flat * piece, axis=(1, 2)))]
    pallas_call x0 -> x7, Pallas kernels: none -> 24.5 us  [the longest x1 6.25 us: shards(): call(kernel_body(channels, rows, width), shaped(channels, 128, dtype=F32)...]
    all_to_all x5 -> x0, waiting for transfers between devices: 24.1 us -> none  [the longest x2 12.6 us: fold_edge(): lax.all_to_all(blocks, 'lon', split_axis=0, concat_axis=0, tiled=True)]
    all_to_all x5 -> x0, starting transfers between devices: 21.2 us -> none  [the longest x2 9.11 us: fold_edge(): lax.all_to_all(blocks, 'lon', split_axis=0, concat_axis=0, tiled=True)]
    convert_element_type x7 -> x0, other arithmetic: 19.6 us -> none  [the longest x1 11.6 us: shards(): (upstream.reshape(channels, height, width) + adjoint).astype(jnp.bfloat16)]
    ppermute x8 -> x28, starting transfers between devices: 11.6 us -> 30.8 us  [across(): lax.ppermute(value, axis, [(i, target(i) % count) for i in range(count)])]
    slice x33 -> x0, local copies, waits for them, and re-layouts: 16 us -> none  [the longest x23 7.08 us: fold_term(): piece = fold_rows[:, source, col_off:col_off + width].astype(jnp.float32)]
  transfers between devices with their start and end apart: 14 -> 28, of which waited for: 11 -> 9; matrix products, arithmetic and copies ran while one was open for 25% -> 5% of each run, Pallas kernels for 0% -> 12%
where the time goes in v1:
time: 84.6 us; the launch traced here: 84.2 us
  starting transfers between devices  30.8 us (36%)
  Pallas kernels  24.5 us (29%)
  waiting for transfers between devices  14.5 us (17%)
  local copies, waits for them, and re-layouts  13.4 us (16%)
  between operations  0.95 us (1%)
    ppermute x28, starting transfers between devices, across(): lax.ppermute(value, axis, [(i, target(i) % count) for i in range(count)])  30.8 us
    ppermute x28, waiting for transfers between devices, across(): lax.ppermute(value, axis, [(i, target(i) % count) for i in range(count)])  14.5 us
    unnamed x43, local copies, waits for them, and re-layouts  13.1 us
    pallas_call x1, Pallas kernels, shards(): call(kernel_body(channels, rows, width), shaped(channels, 128, dtype=F32)...  6.25 us
    pallas_call x1, Pallas kernels, shards(): call(cell_body(levels, channels, height, width, 256), [shaped(height, tot...  5.96 us
    pallas_call x1, Pallas kernels, shards(): call(conv_body(levels, channels, rows, width), [block] * levels, [SMEM] +...  4.91 us
    pallas_call x1, Pallas kernels, shards(): call(adjoint_body(levels, channels, rows, width), shaped(channels, rows,...  4.19 us
  transfers between devices with their start and end apart: 28, of which 9 were waited for; matrix products, arithmetic and copies ran while one was open for 5% of the time, Pallas kernels for 12%

profile of v1, /device:TPU:0, one launch (start us, length us, event | category | flops | bytes accessed | tf_op | source)
XLA Modules:
  0.0 84.2 jit_solution(9110947061379444024)
XLA Ops:
  0.7 1.1 %copy.23.snap_ref = bf16[96,12,128]{2,1,0:T(8,128)(2,1)S(1)} copy(bf16[96,12,128]{2,0,1:T(8,128)(2,1)} %param.8) | data formatting | bytes 589824 | tf_op args[0]
  1.9 1.4 %prepare.1 = (bf16[1,96,128]{2,1,0:T(8,128)(2,1)S(1)}, bf16[1,96,128]{2,1,0:T(8,128)(2,1)S(1)}, bf16[3,96,128]{2,1,0:T(8,128)(2,1)S(1)}, bf16[3,96,128]{2,1,0:T(...) custom-call(s32[2]{0:T(128)S(1)} %pad_add_fusion.place_ref, ...), custom_call_target="tpu_custom_call" | custom-call | flops 294912 | bytes 589824 | tf_op jit(solution)/shard_map/prepare/pallas_call | solution.py:366
  3.9 4.5 %collective-permute-start = (bf16[1,96,128]{2,1,0:T(8,128)(2,1)S(1)}, bf16[1,96,128]{2,1,0:T(8,128)(2,1)S(1)}, u32[]{:S(2)}, u32[]{:S(2)}) collective-permute-start(bf16[1,96,128]{2,1,0:T(8,128)(2,1)S(1)} %get-tuple-element.28), channel_id=1, source_target_pairs={{0,7},{1,2},{2,1},{3,4},{4,3},{5,6},{6,5},{7,0},{8,15},{9,10},{10,... | collective-permute-start | bytes 73736 | tf_op jit(solution)/shard_map/ppermute | solution.py:329
  9.2 2.3 %collective-permute-start.1 = (bf16[1,96,128]{2,1,0:T(8,128)(2,1)S(1)}, bf16[1,96,128]{2,1,0:T(8,128)(2,1)S(1)}, u32[]{:S(2)}, u32[]{:S(2)}) collective-permute-start(bf16[1,96,128]{2,1,0:T(8,128)(2,1)S(1)} %get-tuple-element.29), channel_id=1, source_target_pairs={{0,1},{1,0},{2,3},{3,2},{4,5},{5,4},{6,7},{7,6},{8,9},{9,8},{10,11... | collective-permute-start | bytes 73736 | tf_op jit(solution)/shard_map/ppermute | solution.py:329
  11.4 2.4 %collective-permute-start.10 = (bf16[3,96,128]{2,1,0:T(8,128)(2,1)S(1)}, bf16[3,96,128]{2,1,0:T(8,128)(2,1)S(1)}, u32[]{:S(2)}, u32[]{:S(2)}) collective-permute-start(bf16[3,96,128]{2,1,0:T(8,128)(2,1)S(1)} %get-tuple-element.38), channel_id=1, source_target_pairs={{0,24},{8,16},{16,8},{24,0},{1,25},{9,17},{17,9},{25,1},{2,26},{10... | collective-permute-start | bytes 221192 | tf_op jit(solution)/shard_map/ppermute | solution.py:329
  14.8 2.1 %collective-permute-start.3 = (bf16[3,96,128]{2,1,0:T(8,128)(2,1)S(1)}, bf16[3,96,128]{2,1,0:T(8,128)(2,1)S(1)}, u32[]{:S(2)}, u32[]{:S(2)}) collective-permute-start(bf16[3,96,128]{2,1,0:T(8,128)(2,1)S(1)} %collective-permute-done.2.top_ref), channel_id=1, source_target_pairs={{0,1},{1,0},{2,3},{3,2},{4,5},{5,4},{6,7},{7,6},{8,9},{9,8},{10,11... | collective-permute-start | bytes 221192 | tf_op jit(solution)/shard_map/ppermute | solution.py:329
  16.9 1.6 %collective-permute-start.8 = (bf16[3,96,128]{2,1,0:T(8,128)(2,1)}, bf16[3,96,128]{2,1,0:T(8,128)(2,1)}, u32[]{:S(2)}, u32[]{:S(2)}) collective-permute-start(bf16[3,96,128]{2,1,0:T(8,128)(2,1)} %get-tuple-element.36), channel_id=1, source_target_pairs={{0,8},{8,0},{16,24},{24,16},{1,9},{9,1},{17,25},{25,17},{2,10},{10... | collective-permute-start | bytes 221192 | tf_op jit(solution)/shard_map/ppermute | solution.py:329
  18.5 1.5 %collective-permute-start.9 = (bf16[3,96,128]{2,1,0:T(8,128)(2,1)}, bf16[3,96,128]{2,1,0:T(8,128)(2,1)}, u32[]{:S(2)}, u32[]{:S(2)}) collective-permute-start(bf16[3,96,128]{2,1,0:T(8,128)(2,1)} %get-tuple-element.37), channel_id=1, source_target_pairs={{0,16},{8,24},{16,0},{24,8},{1,17},{9,25},{17,1},{25,9},{2,18},{10... | collective-permute-start | bytes 221192 | tf_op jit(solution)/shard_map/ppermute | solution.py:329
  20.0 4.9 %depthwise.1 = (bf16[3,96,128]{2,1,0:T(8,128)(2,1)S(1)}, bf16[3,96,128]{2,1,0:T(8,128)(2,1)}, bf16[3,96,128]{2,1,0:T(8,128)(2,1)}, bf16[3,96,128]{2,1,0:T(8,128)(2,1)}) custom-call(s32[2]{0:T(128)S(1)} %pad_add_fusion.place_ref, bf16[96,12,128]{2,1,0:T(8,128)(2,1)S(1)} %copy.23.snap_ref, bf16[1,96,128]{2,1,0:T(8,128)(2,1)S(1)} %collective-permute-done.off_ref, ...), custom_call_target="tpu_custom_call" | custom-call | flops 28901376 | bytes 589824 | tf_op jit(solution)/shard_map/depthwise/pallas_call | solution.py:387
  27.2 2.4 %collective-permute-start.7 = (bf16[3,96,128]{2,1,0:T(8,128)(2,1)}, bf16[3,96,128]{2,1,0:T(8,128)(2,1)}, u32[]{:S(2)}, u32[]{:S(2)}) collective-permute-start(bf16[3,96,128]{2,1,0:T(8,128)(2,1)} %get-tuple-element.34), channel_id=1, source_target_pairs={{0,24},{8,16},{16,8},{24,0},{1,25},{9,17},{17,9},{25,1},{2,26},{10... | collective-permute-start | bytes 221192 | tf_op jit(solution)/shard_map/ppermute | solution.py:329
  29.9 1.0 %cotangent.1 = (bf16[384,384]{1,0:T(8,128)(2,1)S(1)}, bf16[3,96,128]{2,1,0:T(8,128)(2,1)S(1)}, bf16[3,96,128]{2,1,0:T(8,128)(2,1)S(1)}, bf16[3,96,128]{2,1,0:T(8,128)(2,1)S(1)}, bf16[3,96,128]{2,1,0:T(8,128)(2,1)S(1)}) custom-call(s32[2]{0:T(128)S(1)} %pad_add_fusion.place_ref, bf16[384,3,128]{2,1,0:T(4,128)(2,1)S(1)} %copy.24.cot_ref, s32[3,128]{1,0:T(4,128)S(1)} %copy-done.4), custom_call_target="tpu_custom_call" | custom-call | flops 294912 | bytes 589824 | tf_op jit(solution)/shard_map/cotangent/pallas_call | solution.py:377
  32.2 1.4 %copy.25 = bf16[384,1536]{0,1:T(8,128)(2,1)} copy(bf16[384,1536]{1,0:T(8,128)(2,1)S(1)} %copy-done.1) | data formatting | bytes 2359296 | tf_op args[6]
  33.6 1.6 %copy.26 = bf16[1536,384]{0,1:T(8,128)(2,1)} copy(bf16[1536,384]{1,0:T(8,128)(2,1)S(1)} %copy-done.2) | data formatting | bytes 2359296 | tf_op args[7]
  35.5 1.3 %copy-done.3 = bf16[384,1536]{0,1:T(8,128)(2,1)S(1)} copy-done((bf16[384,1536]{0,1:T(8,128)(2,1)S(1)}, bf16[384,1536]{0,1:T(8,128)(2,1)}, u32[]{:S(2)}) %copy-start.3) | copy-done | bytes 1179672
  36.8 0.9 %copy-done.10 = bf16[3,96,128]{2,1,0:T(8,128)(2,1)S(1)} copy-done((bf16[3,96,128]{2,1,0:T(8,128)(2,1)S(1)}, bf16[3,96,128]{2,1,0:T(8,128)(2,1)}, u32[]{:S(2)}) %copy-start.10) | copy-done | bytes 73752
  37.6 0.9 %copy-done.12 = bf16[3,96,128]{2,1,0:T(8,128)(2,1)S(1)} copy-done((bf16[3,96,128]{2,1,0:T(8,128)(2,1)S(1)}, bf16[3,96,128]{2,1,0:T(8,128)(2,1)}, u32[]{:S(2)}) %copy-start.12) | copy-done | bytes 73752
  38.5 0.9 %copy-done.14 = bf16[3,96,128]{2,1,0:T(8,128)(2,1)S(1)} copy-done((bf16[3,96,128]{2,1,0:T(8,128)(2,1)S(1)}, bf16[3,96,128]{2,1,0:T(8,128)(2,1)}, u32[]{:S(2)}) %copy-start.14) | copy-done | bytes 73752
  39.4 6.0 %cells.1 = (bf16[3,384,128]{2,1,0:T(8,128)(2,1)}, bf16[3,96,128]{2,1,0:T(8,128)(2,1)S(1)}, bf16[3,96,128]{2,1,0:T(8,128)(2,1)S(1)}, bf16[3,96,128]{2,1,0:T(8,128)(2,1)S(1)}, bf16[3,96,128]{2,1,0:T(8,128)(2,1)S(1)}) custom-call(s32[2]{0:T(128)S(1)} %pad_add_fusion.place_ref, bf16[3,96,128]{2,1,0:T(8,128)(2,1)S(1)} %copy-done.14, ...), custom_call_target="tpu_custom_call" | custom-call | flops 1811939328 | bytes 2949120 | tf_op jit(solution)/shard_map/cells/pallas_call | solution.py:398
  46.4 2.4 %collective-permute-start.13 = (bf16[3,96,128]{2,1,0:T(8,128)(2,1)S(1)}, bf16[3,96,128]{2,1,0:T(8,128)(2,1)S(1)}, u32[]{:S(2)}, u32[]{:S(2)}) collective-permute-start(bf16[3,96,128]{2,1,0:T(8,128)(2,1)S(1)} %get-tuple-element.44), channel_id=1, source_target_pairs={{0,24},{8,16},{16,8},{24,0},{1,25},{9,17},{17,9},{25,1},{2,26},{10... | collective-permute-start | bytes 221192 | tf_op jit(solution)/shard_map/ppermute | solution.py:329
  48.9 0.9 %collective-permute-done.11.refs_1_ = bf16[3,96,128]{2,1,0:T(8,128)(2,1)S(1)} collective-permute-done((bf16[3,96,128]{2,1,0:T(8,128)(2,1)S(1)}, bf16[3,96,128]{2,1,0:T(8,128)(2,1)S(1)}, u32[]{:S(2)}, u32[]{:S(2)}) %collective-permute-start.11) | collective-permute-done | bytes 73760 | tf_op jit(solution)/shard_map/ppermute | solution.py:329
  50.5 1.2 %collective-permute-done.13.refs_3_ = bf16[3,96,128]{2,1,0:T(8,128)(2,1)S(1)} collective-permute-done((bf16[3,96,128]{2,1,0:T(8,128)(2,1)S(1)}, bf16[3,96,128]{2,1,0:T(8,128)(2,1)S(1)}, u32[]{:S(2)}, u32[]{:S(2)}) %collective-permute-start.13) | collective-permute-done | bytes 73760 | tf_op jit(solution)/shard_map/ppermute | solution.py:329
  52.4 6.3 %kernel_terms.1 = f32[96,128]{1,0:T(8,128)S(1)} custom-call(s32[2]{0:T(128)S(1)} %pad_add_fusion.place_ref, bf16[96,12,128]{2,1,0:T(8,128)(2,1)S(1)} %copy.23.snap_ref, bf16[1,96,128]{2,1,0:T(8,128)(2,1)S(1)} %collective-permute-done.off_ref, bf16[1,96,128]{2,1,0:T(8,128)(2,1)S(1)} %collective-permute-done.1.on_ref, ...), custom_call_target="tpu_custom_call" | custom-call | flops 28901376 | bytes 589824 | tf_op jit(solution)/shard_map/kernel_terms/pallas_call | solution.py:430
  58.8 1.2 %collective-permute-done.22 = f32[96,128]{1,0:T(8,128)S(1)} collective-permute-done((f32[96,128]{1,0:T(8,128)S(1)}, f32[96,128]{1,0:T(8,128)S(1)}, u32[]{:S(2)}, u32[]{:S(2)}) %collective-permute-start.22) | collective-permute-done | bytes 49184 | tf_op jit(solution)/shard_map/ppermute | solution.py:329
  60.6 3.5 %collective-permute-done.23 = f32[96,128]{1,0:T(8,128)S(1)} collective-permute-done((f32[96,128]{1,0:T(8,128)S(1)}, f32[96,128]{1,0:T(8,128)S(1)}, u32[]{:S(2)}, u32[]{:S(2)}) %collective-permute-start.23) | collective-permute-done | bytes 49184 | tf_op jit(solution)/shard_map/ppermute | solution.py:329
  64.2 1.6 %collective-permute-start.19 = (bf16[3,96,128]{2,1,0:T(8,128)(2,1)S(1)}, bf16[3,96,128]{2,1,0:T(8,128)(2,1)S(1)}, u32[]{:S(2)}, u32[]{:S(2)}) collective-permute-start(bf16[3,96,128]{2,1,0:T(8,128)(2,1)S(1)} %copy-done.8), channel_id=1, source_target_pairs={{0,8},{8,0},{16,24},{24,16},{1,9},{9,1},{17,25},{25,17},{2,10},{10... | collective-permute-start | bytes 221192 | tf_op jit(solution)/shard_map/ppermute | solution.py:329
  65.8 1.5 %collective-permute-start.20 = (bf16[3,96,128]{2,1,0:T(8,128)(2,1)S(1)}, bf16[3,96,128]{2,1,0:T(8,128)(2,1)S(1)}, u32[]{:S(2)}, u32[]{:S(2)}) collective-permute-start(bf16[3,96,128]{2,1,0:T(8,128)(2,1)S(1)} %copy-done.6), channel_id=1, source_target_pairs={{0,16},{8,24},{16,0},{24,8},{1,17},{9,25},{17,1},{25,9},{2,18},{10... | collective-permute-start | bytes 221192 | tf_op jit(solution)/shard_map/ppermute | solution.py:329
  67.8 2.0 %collective-permute-done.24 = f32[96,128]{1,0:T(8,128)S(1)} collective-permute-done((f32[96,128]{1,0:T(8,128)S(1)}, f32[96,128]{1,0:T(8,128)S(1)}, u32[]{:S(2)}, u32[]{:S(2)}) %collective-permute-start.24) | collective-permute-done | bytes 49184 | tf_op jit(solution)/shard_map/ppermute | solution.py:329
  69.8 1.6 %collective-permute-start.25 = (f32[96,128]{1,0:T(8,128)S(1)}, f32[96,128]{1,0:T(8,128)S(1)}, u32[]{:S(2)}, u32[]{:S(2)}) collective-permute-start(f32[96,128]{1,0:T(8,128)S(1)} %get-tuple-element.60), channel_id=1, source_target_pairs={{0,8},{8,0},{16,24},{24,16},{1,9},{9,1},{17,25},{25,17},{2,10},{10... | collective-permute-start | bytes 147464 | tf_op jit(solution)/shard_map/ppermute | solution.py:329
  71.5 1.0 %collective-permute-done.21.refs_3_ = bf16[3,96,128]{2,1,0:T(8,128)(2,1)S(1)} collective-permute-done((bf16[3,96,128]{2,1,0:T(8,128)(2,1)S(1)}, bf16[3,96,128]{2,1,0:T(8,128)(2,1)S(1)}, u32[]{:S(2)}, u32[]{:S(2)}) %collective-permute-start.21) | collective-permute-done | bytes 73760 | tf_op jit(solution)/shard_map/ppermute | solution.py:329
  73.2 3.2 %collective-permute-done.14.off_ref = bf16[1,96,128]{2,1,0:T(8,128)(2,1)S(1)} collective-permute-done((bf16[1,96,128]{2,1,0:T(8,128)(2,1)S(1)}, bf16[1,96,128]{2,1,0:T(8,128)(2,1)S(1)}, u32[]{:S(2)}, u32[]{:S(2)}) %collective-permute-start.14) | collective-permute-done | bytes 24608 | tf_op jit(solution)/shard_map/ppermute | solution.py:329
  76.4 1.5 %collective-permute-start.26 = (f32[96,128]{1,0:T(8,128)S(1)}, f32[96,128]{1,0:T(8,128)S(1)}, u32[]{:S(2)}, u32[]{:S(2)}) collective-permute-start(f32[96,128]{1,0:T(8,128)S(1)} %get-tuple-element.60), channel_id=1, source_target_pairs={{0,16},{8,24},{16,0},{24,8},{1,17},{9,25},{17,1},{25,9},{2,18},{10... | collective-permute-start | bytes 147464 | tf_op jit(solution)/shard_map/ppermute | solution.py:329
  78.4 4.2 %adjoint.1 = bf16[96,12,128]{2,1,0:T(8,128)(2,1)S(1)} custom-call(s32[2]{0:T(128)S(1)} %pad_add_fusion.place_ref, bf16[12,96,128]{2,1,0:T(8,128)(2,1)S(1)} %get-tuple-element.45.d_ref, bf16[1,96,128]{2,1,0:T(8,128)(2,1)S(1)} %collective-permute-done.14.off_ref, bf16[1,96,128]{2,1,0:T(8,128)(2,1)S(1)} %collective-permute-done.15.on_ref, ...), custom_call_target="tpu_custom_call" | custom-call | flops 28901376 | bytes 589824 | tf_op jit(solution)/shard_map/adjoint/pallas_call | solution.py:448
  (86 shorter events, 13.2 us)
Async XLA Ops:
  0.6 29.0 %copy-start.15 = (bf16[384,3,128]{2,0,1:T(8,128)(2,1)S(1)}, bf16[384,3,128]{2,0,1:T(8,128)(2,1)}, u32[]{:S(2)}) copy-start(bf16[384,3,128]{2,0,1:T(8,128)(2,1)} %param.9) | copy-start | bytes 884740
  0.7 29.2 %copy-start.4 = (s32[3,128]{1,0:T(4,128)S(1)}, s32[3,128]{1,0:T(4,128)}, u32[]{:S(2)}) copy-start(s32[3,128]{1,0:T(4,128)} %refs_9_.1) | copy-start | bytes 4612
  1.9 30.4 %copy-start.1 = (bf16[384,1536]{1,0:T(8,128)(2,1)S(1)}, bf16[384,1536]{1,0:T(8,128)(2,1)}, u32[]{:S(2)}) copy-start(bf16[384,1536]{1,0:T(8,128)(2,1)} %refs_12_.1) | copy-start | bytes 3538948
  3.9 13.0 %collective-permute-start = (bf16[1,96,128]{2,1,0:T(8,128)(2,1)S(1)}, bf16[1,96,128]{2,1,0:T(8,128)(2,1)S(1)}, u32[]{:S(2)}, u32[]{:S(2)}) collective-permute-start(bf16[1,96,128]{2,1,0:T(8,128)(2,1)S(1)} %get-tuple-element.28), channel_id=1, source_target_pairs={{0,7},{1,2},{2,1},{3,4},{4,3},{5,6},{6,5},{7,0},{8,15},{9,10},{10,... | collective-permute-start | bytes 73736 | tf_op jit(solution)/shard_map/ppermute | solution.py:329
  8.4 10.1 %collective-permute-start.4 = (bf16[1,96,128]{2,1,0:T(8,128)(2,1)S(1)}, bf16[1,96,128]{2,1,0:T(8,128)(2,1)S(1)}, u32[]{:S(2)}, u32[]{:S(2)}) collective-permute-start(bf16[1,96,128]{2,1,0:T(8,128)(2,1)S(1)} %get-tuple-element.28), channel_id=1, source_target_pairs={{0,0},{1,5},{2,6},{3,3},{4,4},{5,1},{6,2},{7,7},{8,8},{9,13},{10,1... | collective-permute-start | bytes 73736 | tf_op jit(solution)/shard_map/ppermute | solution.py:329
  9.1 5.7 %collective-permute-start.2 = (bf16[3,96,128]{2,1,0:T(8,128)(2,1)S(1)}, bf16[3,96,128]{2,1,0:T(8,128)(2,1)S(1)}, u32[]{:S(2)}, u32[]{:S(2)}) collective-permute-start(bf16[3,96,128]{2,1,0:T(8,128)(2,1)S(1)} %get-tuple-element.30), channel_id=1, source_target_pairs={{0,7},{1,6},{2,5},{3,4},{4,3},{5,2},{6,1},{7,0},{8,15},{9,14},{10,... | collective-permute-start | bytes 221192 | tf_op jit(solution)/shard_map/ppermute | solution.py:329
  9.2 10.9 %collective-permute-start.1 = (bf16[1,96,128]{2,1,0:T(8,128)(2,1)S(1)}, bf16[1,96,128]{2,1,0:T(8,128)(2,1)S(1)}, u32[]{:S(2)}, u32[]{:S(2)}) collective-permute-start(bf16[1,96,128]{2,1,0:T(8,128)(2,1)S(1)} %get-tuple-element.29), channel_id=1, source_target_pairs={{0,1},{1,0},{2,3},{3,2},{4,5},{5,4},{6,7},{7,6},{8,9},{9,8},{10,11... | collective-permute-start | bytes 73736 | tf_op jit(solution)/shard_map/ppermute | solution.py:329
  11.4 15.2 %collective-permute-start.10 = (bf16[3,96,128]{2,1,0:T(8,128)(2,1)S(1)}, bf16[3,96,128]{2,1,0:T(8,128)(2,1)S(1)}, u32[]{:S(2)}, u32[]{:S(2)}) collective-permute-start(bf16[3,96,128]{2,1,0:T(8,128)(2,1)S(1)} %get-tuple-element.38), channel_id=1, source_target_pairs={{0,24},{8,16},{16,8},{24,0},{1,25},{9,17},{17,9},{25,1},{2,26},{10... | collective-permute-start | bytes 221192 | tf_op jit(solution)/shard_map/ppermute | solution.py:329
  14.8 5.2 %collective-permute-start.3 = (bf16[3,96,128]{2,1,0:T(8,128)(2,1)S(1)}, bf16[3,96,128]{2,1,0:T(8,128)(2,1)S(1)}, u32[]{:S(2)}, u32[]{:S(2)}) collective-permute-start(bf16[3,96,128]{2,1,0:T(8,128)(2,1)S(1)} %collective-permute-done.2.top_ref), channel_id=1, source_target_pairs={{0,1},{1,0},{2,3},{3,2},{4,5},{5,4},{6,7},{7,6},{8,9},{9,8},{10,11... | collective-permute-start | bytes 221192 | tf_op jit(solution)/shard_map/ppermute | solution.py:329
  16.9 18.5 %collective-permute-start.8 = (bf16[3,96,128]{2,1,0:T(8,128)(2,1)}, bf16[3,96,128]{2,1,0:T(8,128)(2,1)}, u32[]{:S(2)}, u32[]{:S(2)}) collective-permute-start(bf16[3,96,128]{2,1,0:T(8,128)(2,1)} %get-tuple-element.36), channel_id=1, source_target_pairs={{0,8},{8,0},{16,24},{24,16},{1,9},{9,1},{17,25},{25,17},{2,10},{10... | collective-permute-start | bytes 221192 | tf_op jit(solution)/shard_map/ppermute | solution.py:329
  18.5 17.0 %collective-permute-start.9 = (bf16[3,96,128]{2,1,0:T(8,128)(2,1)}, bf16[3,96,128]{2,1,0:T(8,128)(2,1)}, u32[]{:S(2)}, u32[]{:S(2)}) collective-permute-start(bf16[3,96,128]{2,1,0:T(8,128)(2,1)} %get-tuple-element.37), channel_id=1, source_target_pairs={{0,16},{8,24},{16,0},{24,8},{1,17},{9,25},{17,1},{25,9},{2,18},{10... | collective-permute-start | bytes 221192 | tf_op jit(solution)/shard_map/ppermute | solution.py:329
  25.5 9.9 %collective-permute-start.5 = (bf16[3,96,128]{2,1,0:T(8,128)(2,1)}, bf16[3,96,128]{2,1,0:T(8,128)(2,1)}, u32[]{:S(2)}, u32[]{:S(2)}) collective-permute-start(bf16[3,96,128]{2,1,0:T(8,128)(2,1)} %get-tuple-element.32), channel_id=1, source_target_pairs={{0,8},{8,0},{16,24},{24,16},{1,9},{9,1},{17,25},{25,17},{2,10},{10... | collective-permute-start | bytes 221192 | tf_op jit(solution)/shard_map/ppermute | solution.py:329
  26.1 9.4 %collective-permute-start.6 = (bf16[3,96,128]{2,1,0:T(8,128)(2,1)}, bf16[3,96,128]{2,1,0:T(8,128)(2,1)}, u32[]{:S(2)}, u32[]{:S(2)}) collective-permute-start(bf16[3,96,128]{2,1,0:T(8,128)(2,1)} %get-tuple-element.33), channel_id=1, source_target_pairs={{0,16},{8,24},{16,0},{24,8},{1,17},{9,25},{17,1},{25,9},{2,18},{10... | collective-permute-start | bytes 221192 | tf_op jit(solution)/shard_map/ppermute | solution.py:329
  27.2 8.3 %collective-permute-start.7 = (bf16[3,96,128]{2,1,0:T(8,128)(2,1)}, bf16[3,96,128]{2,1,0:T(8,128)(2,1)}, u32[]{:S(2)}, u32[]{:S(2)}) collective-permute-start(bf16[3,96,128]{2,1,0:T(8,128)(2,1)} %get-tuple-element.34), channel_id=1, source_target_pairs={{0,24},{8,16},{16,8},{24,0},{1,25},{9,17},{17,9},{25,1},{2,26},{10... | collective-permute-start | bytes 221192 | tf_op jit(solution)/shard_map/ppermute | solution.py:329
  45.4 20.4 %copy-start.6 = (bf16[3,96,128]{2,1,0:T(8,128)(2,1)S(1)}, bf16[3,96,128]{2,1,0:T(8,128)(2,1)}, u32[]{:S(2)}) copy-start(bf16[3,96,128]{2,1,0:T(8,128)(2,1)} %copy-done.5) | copy-start | bytes 221188
  45.4 4.4 %collective-permute-start.11 = (bf16[3,96,128]{2,1,0:T(8,128)(2,1)S(1)}, bf16[3,96,128]{2,1,0:T(8,128)(2,1)S(1)}, u32[]{:S(2)}, u32[]{:S(2)}) collective-permute-start(bf16[3,96,128]{2,1,0:T(8,128)(2,1)S(1)} %get-tuple-element.42), channel_id=1, source_target_pairs={{0,8},{8,0},{16,24},{24,16},{1,9},{9,1},{17,25},{25,17},{2,10},{10... | collective-permute-start | bytes 221192 | tf_op jit(solution)/shard_map/ppermute | solution.py:329
  45.9 4.6 %collective-permute-start.12 = (bf16[3,96,128]{2,1,0:T(8,128)(2,1)S(1)}, bf16[3,96,128]{2,1,0:T(8,128)(2,1)S(1)}, u32[]{:S(2)}, u32[]{:S(2)}) collective-permute-start(bf16[3,96,128]{2,1,0:T(8,128)(2,1)S(1)} %get-tuple-element.43), channel_id=1, source_target_pairs={{0,16},{8,24},{16,0},{24,8},{1,17},{9,25},{17,1},{25,9},{2,18},{10... | collective-permute-start | bytes 221192 | tf_op jit(solution)/shard_map/ppermute | solution.py:329
  46.4 5.3 %collective-permute-start.13 = (bf16[3,96,128]{2,1,0:T(8,128)(2,1)S(1)}, bf16[3,96,128]{2,1,0:T(8,128)(2,1)S(1)}, u32[]{:S(2)}, u32[]{:S(2)}) collective-permute-start(bf16[3,96,128]{2,1,0:T(8,128)(2,1)S(1)} %get-tuple-element.44), channel_id=1, source_target_pairs={{0,24},{8,16},{16,8},{24,0},{1,25},{9,17},{17,9},{25,1},{2,26},{10... | collective-permute-start | bytes 221192 | tf_op jit(solution)/shard_map/ppermute | solution.py:329
  58.7 1.3 %collective-permute-start.22 = (f32[96,128]{1,0:T(8,128)S(1)}, f32[96,128]{1,0:T(8,128)S(1)}, u32[]{:S(2)}, u32[]{:S(2)}) collective-permute-start(f32[96,128]{1,0:T(8,128)S(1)} %kernel_terms.1), channel_id=1, source_target_pairs={{0,1},{1,0},{2,3},{3,2},{4,5},{5,4},{6,7},{7,6},{8,9},{9,8},{10,11... | collective-permute-start | bytes 147464 | tf_op jit(solution)/shard_map/ppermute | solution.py:329
  60.0 4.1 %collective-permute-start.23 = (f32[96,128]{1,0:T(8,128)S(1)}, f32[96,128]{1,0:T(8,128)S(1)}, u32[]{:S(2)}, u32[]{:S(2)}) collective-permute-start(f32[96,128]{1,0:T(8,128)S(1)} %add.32), channel_id=1, source_target_pairs={{0,2},{1,3},{2,0},{3,1},{4,6},{5,7},{6,4},{7,5},{8,10},{9,11},{10,... | collective-permute-start | bytes 147464 | tf_op jit(solution)/shard_map/ppermute | solution.py:329
  60.0 7.7 %collective-permute-start.16 = (bf16[3,96,128]{2,1,0:T(8,128)(2,1)S(1)}, bf16[3,96,128]{2,1,0:T(8,128)(2,1)S(1)}, u32[]{:S(2)}, u32[]{:S(2)}) collective-permute-start(bf16[3,96,128]{2,1,0:T(8,128)(2,1)S(1)} %get-tuple-element.48), channel_id=1, source_target_pairs={{0,7},{1,6},{2,5},{3,4},{4,3},{5,2},{6,1},{7,0},{8,15},{9,14},{10,... | collective-permute-start | bytes 221192 | tf_op jit(solution)/shard_map/ppermute | solution.py:329
  64.1 5.6 %collective-permute-start.24 = (f32[96,128]{1,0:T(8,128)S(1)}, f32[96,128]{1,0:T(8,128)S(1)}, u32[]{:S(2)}, u32[]{:S(2)}) collective-permute-start(f32[96,128]{1,0:T(8,128)S(1)} %add.33), channel_id=1, source_target_pairs={{0,4},{1,5},{2,6},{3,7},{4,0},{5,1},{6,2},{7,3},{8,12},{9,13},{10,... | collective-permute-start | bytes 147464 | tf_op jit(solution)/shard_map/ppermute | solution.py:329
  64.2 7.1 %collective-permute-start.19 = (bf16[3,96,128]{2,1,0:T(8,128)(2,1)S(1)}, bf16[3,96,128]{2,1,0:T(8,128)(2,1)S(1)}, u32[]{:S(2)}, u32[]{:S(2)}) collective-permute-start(bf16[3,96,128]{2,1,0:T(8,128)(2,1)S(1)} %copy-done.8), channel_id=1, source_target_pairs={{0,8},{8,0},{16,24},{24,16},{1,9},{9,1},{17,25},{25,17},{2,10},{10... | collective-permute-start | bytes 221192 | tf_op jit(solution)/shard_map/ppermute | solution.py:329
  65.8 5.7 %collective-permute-start.20 = (bf16[3,96,128]{2,1,0:T(8,128)(2,1)S(1)}, bf16[3,96,128]{2,1,0:T(8,128)(2,1)S(1)}, u32[]{:S(2)}, u32[]{:S(2)}) collective-permute-start(bf16[3,96,128]{2,1,0:T(8,128)(2,1)S(1)} %copy-done.6), channel_id=1, source_target_pairs={{0,16},{8,24},{16,0},{24,8},{1,17},{9,25},{17,1},{25,9},{2,18},{10... | collective-permute-start | bytes 221192 | tf_op jit(solution)/shard_map/ppermute | solution.py:329
  67.3 5.3 %collective-permute-start.21 = (bf16[3,96,128]{2,1,0:T(8,128)(2,1)S(1)}, bf16[3,96,128]{2,1,0:T(8,128)(2,1)S(1)}, u32[]{:S(2)}, u32[]{:S(2)}) collective-permute-start(bf16[3,96,128]{2,1,0:T(8,128)(2,1)S(1)} %get-tuple-element.52), channel_id=1, source_target_pairs={{0,24},{8,16},{16,8},{24,0},{1,25},{9,17},{17,9},{25,1},{2,26},{10... | collective-permute-start | bytes 221192 | tf_op jit(solution)/shard_map/ppermute | solution.py:329
  67.8 10.6 %collective-permute-start.17 = (bf16[3,96,128]{2,1,0:T(8,128)(2,1)S(1)}, bf16[3,96,128]{2,1,0:T(8,128)(2,1)S(1)}, u32[]{:S(2)}, u32[]{:S(2)}) collective-permute-start(bf16[3,96,128]{2,1,0:T(8,128)(2,1)S(1)} %collective-permute-done.16.top_ref), channel_id=1, source_target_pairs={{0,1},{1,0},{2,3},{3,2},{4,5},{5,4},{6,7},{7,6},{8,9},{9,8},{10,11... | collective-permute-start | bytes 221192 | tf_op jit(solution)/shard_map/ppermute | solution.py:329
  69.8 13.6 %collective-permute-start.25 = (f32[96,128]{1,0:T(8,128)S(1)}, f32[96,128]{1,0:T(8,128)S(1)}, u32[]{:S(2)}, u32[]{:S(2)}) collective-permute-start(f32[96,128]{1,0:T(8,128)S(1)} %get-tuple-element.60), channel_id=1, source_target_pairs={{0,8},{8,0},{16,24},{24,16},{1,9},{9,1},{17,25},{25,17},{2,10},{10... | collective-permute-start | bytes 147464 | tf_op jit(solution)/shard_map/ppermute | solution.py:329
  71.4 5.1 %collective-permute-start.14 = (bf16[1,96,128]{2,1,0:T(8,128)(2,1)S(1)}, bf16[1,96,128]{2,1,0:T(8,128)(2,1)S(1)}, u32[]{:S(2)}, u32[]{:S(2)}) collective-permute-start(bf16[1,96,128]{2,1,0:T(8,128)(2,1)S(1)} %get-tuple-element.46), channel_id=1, source_target_pairs={{0,7},{1,2},{2,1},{3,4},{4,3},{5,6},{6,5},{7,0},{8,15},{9,10},{10,... | collective-permute-start | bytes 73736 | tf_op jit(solution)/shard_map/ppermute | solution.py:329
  71.5 6.4 %collective-permute-start.15 = (bf16[1,96,128]{2,1,0:T(8,128)(2,1)S(1)}, bf16[1,96,128]{2,1,0:T(8,128)(2,1)S(1)}, u32[]{:S(2)}, u32[]{:S(2)}) collective-permute-start(bf16[1,96,128]{2,1,0:T(8,128)(2,1)S(1)} %get-tuple-element.47), channel_id=1, source_target_pairs={{0,1},{1,0},{2,3},{3,2},{4,5},{5,4},{6,7},{7,6},{8,9},{9,8},{10,11... | collective-permute-start | bytes 73736 | tf_op jit(solution)/shard_map/ppermute | solution.py:329
  72.5 5.9 %collective-permute-start.18 = (bf16[1,96,128]{2,1,0:T(8,128)(2,1)S(1)}, bf16[1,96,128]{2,1,0:T(8,128)(2,1)S(1)}, u32[]{:S(2)}, u32[]{:S(2)}) collective-permute-start(bf16[1,96,128]{2,1,0:T(8,128)(2,1)S(1)} %get-tuple-element.46), channel_id=1, source_target_pairs={{0,0},{1,5},{2,6},{3,3},{4,4},{5,1},{6,2},{7,7},{8,8},{9,13},{10,1... | collective-permute-start | bytes 73736 | tf_op jit(solution)/shard_map/ppermute | solution.py:329
  76.4 7.0 %collective-permute-start.26 = (f32[96,128]{1,0:T(8,128)S(1)}, f32[96,128]{1,0:T(8,128)S(1)}, u32[]{:S(2)}, u32[]{:S(2)}) collective-permute-start(f32[96,128]{1,0:T(8,128)S(1)} %get-tuple-element.60), channel_id=1, source_target_pairs={{0,16},{8,24},{16,0},{24,8},{1,17},{9,25},{17,1},{25,9},{2,18},{10... | collective-permute-start | bytes 147464 | tf_op jit(solution)/shard_map/ppermute | solution.py:329
  77.9 5.5 %collective-permute-start.27 = (f32[96,128]{1,0:T(8,128)S(1)}, f32[96,128]{1,0:T(8,128)S(1)}, u32[]{:S(2)}, u32[]{:S(2)}) collective-permute-start(f32[96,128]{1,0:T(8,128)S(1)} %get-tuple-element.60), channel_id=1, source_target_pairs={{0,24},{8,16},{16,8},{24,0},{1,25},{9,17},{17,9},{25,1},{2,26},{10... | collective-permute-start | bytes 147464 | tf_op jit(solution)/shard_map/ppermute | solution.py:329
  (14 other events, 43.8 us)

commit v2 on v1

v2 whole, which is shorter than its diff:
```python
import jax
import jax.numpy as jnp
from jax import lax
from jax.experimental import pallas as pl
from jax.experimental.pallas import tpu as pltpu
from jax.sharding import PartitionSpec as P

TAPS = 7
REACH = TAPS // 2
EPSILON = 1e-06
ROOT_HALF = 0.7071067811865476
INV_ROOT_TAU = 0.3989422804014327
F32 = jnp.float32
BF16 = jnp.bfloat16
VMEM = pl.BlockSpec(memory_space=pltpu.VMEM)
SMEM = pl.BlockSpec(memory_space=pltpu.SMEM)
SPAN = 2 * REACH
FIRST = (((0,), (0,)), ((), ()))
LIMIT = 24 * 1024 * 1024


def call(body, out, specs, scratch, micros, name):
    return pl.pallas_call(
        body,
        out_shape=out,
        in_specs=specs,
        out_specs=jax.tree.map(lambda _: VMEM, out),
        scratch_shapes=scratch,
        compiler_params=pltpu.CompilerParams(vmem_limit_bytes=LIMIT),
        cost_estimate=pl.CostEstimate(flops=int(micros * 1.1e9), bytes_accessed=0, transcendentals=0),
        name=name,
    )


def shaped(*shape, dtype=BF16):
    return jax.ShapeDtypeStruct(shape, dtype)


def lanes_of(shape):
    return lax.broadcasted_iota(jnp.int32, shape, len(shape) - 1)


def groups_of(rows):
    per = rows
    while (per + 2 * REACH) * SPAN > 128 or rows % per:
        per -= 1
    return rows // per, per


def where_flag(flag, yes, no):
    return jnp.where(flag == 1, yes.astype(jnp.int32), no.astype(jnp.int32)) == 1


def right_lanes(lane, per, width):
    low = (per + REACH) * SPAN - REACH
    base = SPAN * ((width + SPAN - 1) // SPAN) - width
    return jnp.where(lane >= low, lane + base, lane) % SPAN < REACH


def pack_edges(read, odd, off_ref, on_ref, rows, channels, width):
    count, per = groups_of(rows)
    lane = lanes_of((channels, width))
    for group in range(count):
        off = jnp.zeros((channels, width), F32)
        on = jnp.zeros((channels, width), F32)
        for place in range(per):
            base = SPAN * place
            line = pltpu.roll(read(group * per + place), base, 1) if place else read(group * per)
            in_first = (lane >= base) & (lane < base + REACH)
            spot = (base - REACH) % width
            in_last = (lane >= spot) & (lane < spot + REACH)
            off = jnp.where(where_flag(odd, in_last, in_first), line, off)
            on = jnp.where(where_flag(odd, in_first, in_last), line, on)
        off_ref[group] = off.astype(BF16)
        on_ref[group] = on.astype(BF16)


def flip_lanes(value, width, top):
    row = lax.broadcasted_iota(jnp.int32, (width, width), 0)
    col = lax.broadcasted_iota(jnp.int32, (width, width), 1)
    exchange = ((row + col) % width == top % width).astype(BF16)
    return jnp.dot(value, exchange, preferred_element_type=F32)


def packed_edges(off_ref, on_ref, top_ref, mate_ref, fold_ref, odd, rows, channels, width):
    count, per = groups_of(rows)
    lane = lanes_of((channels, width))
    right = right_lanes(lane, per, width)
    near = where_flag(odd, ~right, right)
    groups = [jnp.where(near, on_ref[g].astype(F32), off_ref[g].astype(F32)) for g in range(count)]
    fold = jnp.where(near, fold_ref[count - 1].astype(F32), 0.0)
    ends = SPAN * (per - REACH) - REACH
    fold = jnp.where((lane >= ends) & (lane < SPAN * per - REACH), fold, 0.0)
    for depth in range(REACH):
        base = SPAN * (per - 1 - depth)
        line = pltpu.roll(mate_ref[REACH - 1 - depth].astype(F32), base, 1)
        here = (lane >= base - REACH) & (lane < base + REACH) & ~near
        fold = jnp.where(here, line, fold)
    groups[-1] = groups[-1] + flip_lanes(fold.astype(BF16), width, 2 * SPAN * per - SPAN - 1)
    return groups


def unpack(group, place, width):
    shift = (-SPAN * place) % width
    return pltpu.roll(group, shift, 1) if shift else group


def fill(lines, edges, read, off_ref, on_ref, top_ref, mate_ref, fold_ref, odd, rows, channels, width):
    count, per = groups_of(rows)
    groups = packed_edges(off_ref, on_ref, top_ref, mate_ref, fold_ref, odd, rows, channels, width)
    for row in range(rows):
        lines[row] = read(row)
        edges[row] = unpack(groups[row // per], row % per, width)
    for depth in range(REACH):
        lines[rows + depth] = flip_lanes(top_ref[REACH - 1 - depth], width, width - 1)
        edges[rows + depth] = unpack(groups[-1], per + depth, width)


def shifted(line, edge, step, lane, width):
    if step == 0:
        return line
    if step > 0:
        return pltpu.roll(jnp.where(lane < step, edge, line), width - step, 1)
    return pltpu.roll(jnp.where(lane >= width + step, edge, line), -step, 1)


def prepare_body(levels, channels, rows, width):
    height = rows // levels

    def body(place_ref, snap_ref, off_ref, on_ref, top_ref, *sends):
        lev, odd = place_ref[0], place_ref[1]
        pack_edges(lambda row: snap_ref[row].astype(F32), odd, off_ref, on_ref, rows, channels, width)
        top_ref[...] = snap_ref[rows - REACH :]
        for hop in range(1, levels):
            sends[hop - 1][...] = snap_ref[pl.ds((lev ^ hop) * height, height)]

    return body


def inner_body(channels, rows, width):
    def body(snap_ref, weight_ref, out_ref, spread_ref, lines):
        lines[...] = snap_ref[...].astype(F32)
        lane = lanes_of((8, width))

        def step(block, carry):
            span = pl.ds(block * 8, 8)
            weights = weight_ref[span, :]
            sums = [None] * rows
            for col in range(TAPS):
                taps = [jnp.broadcast_to(weights[:, a * TAPS + col : a * TAPS + col + 1], (8, width)) for a in range(TAPS)]
                for a in range(TAPS):
                    spread_ref[a * TAPS + col, span, :] = taps[a]
                for source in range(rows):
                    moved = shifted(lines[source, span, :], 0.0, col - REACH, lane, width)
                    for a in range(TAPS):
                        row = source - a + REACH
                        if 0 <= row < rows:
                            term = taps[a] * moved
                            sums[row] = term if sums[row] is None else sums[row] + term
            for row in range(rows):
                out_ref[row, span, :] = sums[row]
            return carry

        lax.fori_loop(0, channels // 8, step, 0)

    return body


def outer_body(levels, channels, rows, width):
    height = rows // levels
    count, per = groups_of(rows)

    def body(place_ref, inner_ref, off_ref, on_ref, top_ref, mate_ref, fold_ref, spread_ref, *rest):
        sends, (total, packed, folded) = rest[:levels], rest[levels:]
        lev, odd = place_ref[0], place_ref[1]
        groups = packed_edges(off_ref, on_ref, top_ref, mate_ref, fold_ref, odd, rows, channels, width)
        wide = lanes_of((channels, width))
        for group in range(count):
            value = groups[group]
            if group:
                tail = (wide >= SPAN * (per - REACH) - REACH) & (wide < SPAN * per - REACH)
                value = value + pltpu.roll(jnp.where(tail, groups[group - 1], 0.0), (-SPAN * per) % width, 1)
            if group + 1 < count:
                begin = (wide < SPAN * REACH - REACH) | (wide >= width - REACH)
                value = value + pltpu.roll(jnp.where(begin, groups[group + 1], 0.0), SPAN * per, 1)
            packed[group] = value
        for depth in range(REACH):
            folded[depth] = flip_lanes(top_ref[REACH - 1 - depth], width, width - 1)
        lane = lanes_of((8, width))
        right = right_lanes(lane, per, width)
        rim = (lane < REACH) | (lane >= width - REACH)

        def step(block, carry):
            span = pl.ds(block * 8, 8)
            for group in range(count):
                near = packed[group, span, :]
                from_right = jnp.where(right, near, 0.0)
                from_left = jnp.where(right, 0.0, near)
                sums = [None, None]
                for a in range(TAPS):
                    for col in range(TAPS):
                        if col == REACH:
                            continue
                        side = col > REACH
                        move = (-(SPAN * (a - REACH) + col - REACH)) % width
                        term = spread_ref[a * TAPS + col, span, :] * pltpu.roll(from_right if side else from_left, move, 1)
                        sums[side] = term if sums[side] is None else sums[side] + term
                rims = jnp.where(right, sums[0], sums[1])
                for place in range(per):
                    row = group * per + place
                    value = inner_ref[row, span, :] + jnp.where(rim, unpack(rims, place, width), 0.0)
                    if row >= rows - REACH:
                        for depth in range(REACH):
                            a = rows + depth - row + REACH
                            if a < TAPS:
                                for col in range(TAPS):
                                    moved = shifted(folded[depth, span, :], 0.0, col - REACH, lane, width)
                                    value = value + spread_ref[a * TAPS + col, span, :] * moved
                    total[row, span, :] = value
            return carry

        lax.fori_loop(0, channels // 8, step, 0)
        for hop in range(levels):
            sends[hop][...] = total[pl.ds((lev ^ hop) * height, height)].astype(BF16)

    return body


def columns_body(channels, rows, width):
    def body(place_ref, snap_ref, off_ref, on_ref, top_ref, mate_ref, fold_ref, out_ref, lines, edges):
        odd = place_ref[1]
        fill(lines, edges, lambda row: snap_ref[row].astype(F32), off_ref, on_ref, top_ref, mate_ref, fold_ref, odd, rows, channels, width)
        lane = lanes_of((channels, width))
        for col in range(TAPS):
            for source in range(rows + REACH):
                out_ref[col, source] = shifted(lines[source], edges[source], col - REACH, lane, width)

    return body


def cotangent_body(levels, channels, height, width):
    def body(place_ref, cot_ref, mask_ref, up_ref, *rest):
        sends, lines = rest[:levels], rest[levels]
        lev = place_ref[0]
        wet = mask_ref[...].astype(F32)
        lines[...] = cot_ref[...].astype(F32) * wet[:, None, :]
        for row in range(height):
            up_ref[:, row * width : (row + 1) * width] = lines[row].astype(BF16)
        for hop in range(levels):
            start = pl.multiple_of((lev ^ hop) * channels, 8)
            for row in range(height):
                sends[hop][row] = lines[row, pl.ds(start, channels), :].astype(BF16)

    return body


def cell_body(levels, channels, height, width, chunk):
    total_channels = levels * channels
    cells = height * width

    def body(place_ref, *refs):
        convs, snaps, own_ref, refs = refs[:levels], refs[levels : 2 * levels - 1], refs[2 * levels - 1], refs[2 * levels :]
        up_ref, mask_ref, gain_ref, shift_ref, win_ref, wout_ref = refs[:6]
        result_ref, sends = refs[6], refs[7 : 7 + levels]
        field, d_lifted, projected = refs[7 + levels :]
        lev = place_ref[0]
        for hop in range(levels):
            start = pl.multiple_of((lev ^ hop) * channels, 8)
            for row in range(height):
                field[pl.ds(start, channels), row * width : (row + 1) * width] = convs[hop][row].astype(F32)
        convolved = field[...]
        centre = jnp.mean(convolved, axis=0, keepdims=True)
        centred = convolved - centre
        spread = jnp.mean(centred * centred, axis=0, keepdims=True)
        rstd = lax.rsqrt(spread + EPSILON)
        normed = centred * rstd
        field[...] = normed
        gain = gain_ref[...]
        lifted = (normed * gain + shift_ref[...]).astype(BF16)
        upstream = up_ref[...]
        features = wout_ref.shape[0]
        for piece in range(features // chunk):
            span = slice(piece * chunk, (piece + 1) * chunk)
            hidden = lax.dot_general(win_ref[:, span], lifted, FIRST, preferred_element_type=F32)
            d_active = jnp.dot(wout_ref[span, :], upstream, preferred_element_type=F32)
            half = 0.5 * (1.0 + lax.erf(hidden * ROOT_HALF))
            active = (hidden * half).astype(BF16)
            slope = half + hidden * jnp.exp(-0.5 * hidden * hidden) * INV_ROOT_TAU
            d_hidden = (d_active * slope).astype(BF16)
            out = lax.dot_general(wout_ref[span, :], active, FIRST, preferred_element_type=F32)
            back = jnp.dot(win_ref[:, span], d_hidden, preferred_element_type=F32)
            if piece == 0:
                projected[...] = out
                d_lifted[...] = back
            else:
                projected[...] += out
                d_lifted[...] += back
        for hop in range(levels):
            start = pl.multiple_of((lev ^ hop) * channels, 8)
            for row in range(height):
                wet = mask_ref[row : row + 1, :].astype(F32)
                held = snaps[hop - 1][row] if hop else own_ref[lev * height + row]
                value = held.astype(F32) + projected[pl.ds(start, channels), row * width : (row + 1) * width]
                projected[pl.ds(start, channels), row * width : (row + 1) * width] = wet * value
        for row in range(height):
            result_ref[row] = projected[:, row * width : (row + 1) * width].astype(BF16)
        d_normed = d_lifted[...] * gain
        normed = field[...]
        first = jnp.mean(d_normed, axis=0, keepdims=True)
        second = jnp.mean(d_normed * normed, axis=0, keepdims=True)
        field[...] = rstd * (d_normed - first - normed * second)
        for hop in range(levels):
            start = pl.multiple_of((lev ^ hop) * channels, 8)
            for row in range(height):
                sends[hop][row] = field[pl.ds(start, channels), row * width : (row + 1) * width].astype(BF16)

    return body


def gather_body(levels, channels, rows, width):
    height = rows // levels

    def body(place_ref, *refs):
        blocks, (lines_ref, off_ref, on_ref, top_ref, lines) = refs[:levels], refs[levels:]
        lev, odd = place_ref[0], place_ref[1]
        for hop in range(levels):
            lines[pl.ds((lev ^ hop) * height, height)] = blocks[hop][...].astype(F32)
        lines_ref[...] = lines[...].astype(BF16)
        top_ref[...] = lines[rows - REACH :].astype(BF16)
        pack_edges(lambda row: lines[row], odd, off_ref, on_ref, rows, channels, width)

    return body


def kernel_body(levels, channels, rows, width):
    height = rows // levels

    def body(place_ref, columns_ref, *refs):
        blocks, (out_ref, grads) = refs[:levels], refs[levels:]
        lev = place_ref[0]
        for hop in range(levels):
            grads[pl.ds((lev ^ hop) * height, height)] = blocks[hop][...].astype(F32)
        out_lane = lanes_of((8, 128))

        def step(block, carry):
            span = pl.ds(block * 8, 8)
            grad = [grads[row, span, :] for row in range(rows)]
            found = jnp.zeros((8, 128), F32)
            for col in range(TAPS):
                sums = [None] * TAPS
                for source in range(rows + REACH):
                    moved = columns_ref[col, source, span, :]
                    for a in range(TAPS):
                        row = source - a + REACH
                        if 0 <= row < rows:
                            term = grad[row] * moved
                            sums[a] = term if sums[a] is None else sums[a] + term
                for a in range(TAPS):
                    found = jnp.where(out_lane == a * TAPS + col, jnp.sum(sums[a], axis=1, keepdims=True), found)
            out_ref[span, :] = found
            return carry

        lax.fori_loop(0, channels // 8, step, 0)

    return body


def adjoint_body(levels, channels, rows, width):
    height = rows // levels

    def body(place_ref, d_ref, off_ref, on_ref, top_ref, mate_ref, fold_ref, spread_ref, *refs):
        ups, (out_ref, lines, edges, total) = refs[:levels], refs[levels:]
        lev, odd = place_ref[0], place_ref[1]
        fill(lines, edges, lambda row: d_ref[row].astype(F32), off_ref, on_ref, top_ref, mate_ref, fold_ref, odd, rows, channels, width)
        for hop in range(levels):
            total[pl.ds((lev ^ hop) * height, height)] = ups[hop][...].astype(F32)
        lane = lanes_of((8, width))

        def step(block, carry):
            span = pl.ds(block * 8, 8)
            sums = [None] * rows
            for col in range(TAPS):
                taps = [spread_ref[a * TAPS + col, span, :] for a in range(TAPS)]
                for source in range(rows):
                    moved = shifted(lines[source, span, :], edges[source, span, :], REACH - col, lane, width)
                    for a in range(TAPS):
                        row = source + a - REACH
                        if 0 <= row < rows:
                            term = taps[a] * moved
                            sums[row] = term if sums[row] is None else sums[row] + term
                for source in range(REACH):
                    moved = shifted(lines[rows + source, span, :], edges[rows + source, span, :], col - REACH, lane, width)
                    for depth in range(REACH - source):
                        row = rows - 1 - depth
                        sums[row] = sums[row] + taps[REACH + 1 + depth + source] * moved
            for row in range(rows):
                total[row, span, :] = total[row, span, :] + sums[row]
            return carry

        lax.fori_loop(0, channels // 8, step, 0)
        out_ref[...] = total[...].astype(BF16)

    return body


def across(value, axis, target):
    count = lax.axis_size(axis)
    return lax.ppermute(value, axis, [(i, target(i) % count) for i in range(count)])


def level_swap(blocks):
    return [blocks[0]] + [across(blocks[hop], "lev", lambda i: i ^ hop) for hop in range(1, len(blocks))]


def edge_swap(off, on, top):
    lanes = lax.axis_size("lon")
    near = across(on, "lon", lambda i: i ^ 1)
    far = across(off, "lon", lambda i: i + 1 if i % 2 else i - 1)
    folded = across(top, "lon", lambda i: lanes - 1 - i)
    fold_far = across(off, "lon", lambda i: lanes - 2 - i if i % 2 else lanes - i)
    mate = across(folded, "lon", lambda i: i ^ 1)
    return far, near, folded, mate, fold_far


def shards(snapshot, cotangent, ocean_mask, kernel, norm_gain, norm_shift, weight_in, weight_out):
    levels = lax.axis_size("lev")
    lanes = lax.axis_size("lon")
    channels, rows, width = snapshot.shape
    height = rows // levels
    total_channels = channels * levels
    cells = height * width
    lev = lax.axis_index("lev")
    place = jnp.stack([lev, lax.axis_index("lon") % 2]).astype(jnp.int32)
    groups = groups_of(rows)[0]
    weights = lax.dynamic_slice_in_dim(kernel, lev * channels, channels, 0).astype(F32)
    weights = jnp.pad(weights, ((0, 0), (0, 128 - TAPS * TAPS)))
    block = shaped(height, channels, width)
    pack = shaped(groups, channels, width)
    top_shape = shaped(REACH, channels, width)
    field = pltpu.VMEM((rows, channels, width), F32)
    deep = pltpu.VMEM((rows + REACH, channels, width), F32)
    lines = jnp.swapaxes(snapshot, 0, 1)

    off, on, top, *snap_sends = call(
        prepare_body(levels, channels, rows, width),
        [pack, pack, top_shape] + [block] * (levels - 1),
        [SMEM, VMEM],
        [],
        1.0,
        "prepare",
    )(place, lines)
    snap_edges = edge_swap(off, on, top)
    snaps = level_swap([None] + snap_sends)[1:]
    inner, spread = call(
        inner_body(channels, rows, width),
        [shaped(rows, channels, width, dtype=F32), shaped(TAPS * TAPS, channels, width, dtype=F32)],
        [VMEM] * 2,
        [field],
        3.5,
        "inner",
    )(lines, weights)
    conv_sends = call(
        outer_body(levels, channels, rows, width),
        [block] * levels,
        [SMEM] + [VMEM] * 7,
        [field, pltpu.VMEM((groups, channels, width), F32), pltpu.VMEM((REACH, channels, width), F32)],
        1.5,
        "outer",
    )(place, inner, *snap_edges, spread)
    convs = level_swap(conv_sends)
    upstream, *up_sends = call(
        cotangent_body(levels, channels, height, width),
        [shaped(total_channels, cells)] + [block] * levels,
        [SMEM, VMEM, VMEM],
        [pltpu.VMEM((height, total_channels, width), F32)],
        1.0,
        "cotangent",
    )(place, jnp.swapaxes(cotangent, 0, 1), ocean_mask)
    ups = level_swap(up_sends)
    columns = call(
        columns_body(channels, rows, width),
        shaped(TAPS, rows + REACH, channels, width, dtype=F32),
        [SMEM] + [VMEM] * 6,
        [deep, deep],
        2.0,
        "columns",
    )(place, lines, *snap_edges)
    result, *d_sends = call(
        cell_body(levels, channels, height, width, 512),
        [shaped(height, total_channels, width)] + [block] * levels,
        [SMEM] + [VMEM] * (2 * levels + 6),
        [pltpu.VMEM((total_channels, cells), F32)] * 3,
        5.0,
        "cells",
    )(place, *convs, *snaps, lines, upstream, ocean_mask, norm_gain[:, None], norm_shift[:, None], weight_in, weight_out)
    d_blocks = level_swap(d_sends)
    d_lines, off, on, top = call(
        gather_body(levels, channels, rows, width),
        [shaped(rows, channels, width), pack, pack, top_shape],
        [SMEM] + [VMEM] * levels,
        [field],
        0.8,
        "regroup",
    )(place, *d_blocks)
    d_edges = edge_swap(off, on, top)
    terms = call(
        kernel_body(levels, channels, rows, width),
        shaped(channels, 128, dtype=F32),
        [SMEM] + [VMEM] * (1 + levels),
        [field],
        2.5,
        "kernel_terms",
    )(place, columns, *d_blocks)
    hop = 1
    while hop < lanes:
        terms = terms + across(terms, "lon", lambda i: i ^ hop)
        hop *= 2
    parts = level_swap([terms] * levels)
    stacked = jnp.zeros((levels, channels, 128), F32)
    for hop, part in enumerate(parts):
        stacked = lax.dynamic_update_slice(stacked, part[None], (lev ^ hop, 0, 0))
    kernel_grad = stacked.reshape(total_channels, 128)[:, : TAPS * TAPS]
    d_snapshot = call(
        adjoint_body(levels, channels, rows, width),
        shaped(rows, channels, width),
        [SMEM] + [VMEM] * (7 + levels),
        [deep, deep, field],
        4.0,
        "adjoint",
    )(place, d_lines, *d_edges, spread, *ups)
    return (jnp.swapaxes(result, 0, 1), jnp.swapaxes(d_snapshot, 0, 1), kernel_grad)


def solution(mesh):
    placed = (
        P("lev", None, "lon"),
        P(None, "lev", "lon"),
        P("lev", "lon"),
        P(),
        P(),
        P(),
        P(),
        P(),
    )
    return jax.shard_map(
        shards,
        mesh=mesh,
        in_specs=placed,
        out_specs=(P(None, "lev", "lon"), P("lev", None, "lon"), P()),
        check_vma=False,
    )
```

time: 84.6 us -> 72 us (0.85)
  local copies, waits for them, and re-layouts: 13.4 us -> 3.88 us
  waiting for transfers between devices: 14.5 us -> 11.7 us
  Pallas kernels: 24.5 us -> 23 us
  starting transfers between devices: 30.8 us -> 32.1 us
    unnamed x43 -> x24, local copies, waits for them, and re-layouts: 13.1 us -> 3.55 us
    ppermute x28, waiting for transfers between devices: 14.5 us -> 11.7 us  [across(): lax.ppermute(value, axis, [(i, target(i) % count) for i in range(count)])]
    ppermute x28, starting transfers between devices: 30.8 us -> 32.1 us  [across(): lax.ppermute(value, axis, [(i, target(i) % count) for i in range(count)])]
    pallas_call x4 -> x6, Pallas kernels: 21.3 us -> 21 us  [the longest x1 4.77 us: shards(): call(cell_body(levels, channels, height, width, 512), [shaped(height, tot...]
  transfers between devices with their start and end apart: 28 -> 28, of which waited for: 9 -> 9; matrix products, arithmetic and copies ran while one was open for 5% -> 1% of each run, Pallas kernels for 12% -> 20%
where the time goes in v2:
time: 72 us; the launch traced here: 71.8 us
  starting transfers between devices  32.1 us (45%)
  Pallas kernels  23 us (32%)
  waiting for transfers between devices  11.7 us (16%)
  local copies, waits for them, and re-layouts  3.88 us (5%)
  between operations  0.94 us (1%)
    ppermute x28, starting transfers between devices, across(): lax.ppermute(value, axis, [(i, target(i) % count) for i in range(count)])  32.1 us
    ppermute x28, waiting for transfers between devices, across(): lax.ppermute(value, axis, [(i, target(i) % count) for i in range(count)])  11.7 us
    pallas_call x1, Pallas kernels, shards(): call(cell_body(levels, channels, height, width, 512), [shaped(height, tot...  4.77 us
    pallas_call x1, Pallas kernels, shards(): call(adjoint_body(levels, channels, rows, width), shaped(rows, channels,...  4.38 us
    unnamed x24, local copies, waits for them, and re-layouts  3.55 us
    pallas_call x1, Pallas kernels, shards(): call(kernel_body(levels, channels, rows, width), shaped(channels, 128, dt...  3.35 us
    pallas_call x1, Pallas kernels, shards(): call(outer_body(levels, channels, rows, width), [block] * levels, [SMEM]...  3.27 us
    pallas_call x1, Pallas kernels, shards(): call(inner_body(channels, rows, width), [shaped(rows, channels, width, dt...  2.98 us
  transfers between devices with their start and end apart: 28, of which 9 were waited for; matrix products, arithmetic and copies ran while one was open for 1% of the time, Pallas kernels for 20%

profile of v2, /device:TPU:0, one launch (start us, length us, event | category | flops | bytes accessed | tf_op | source)
XLA Modules:
  0.0 71.8 jit_solution(8654458128657441268)
XLA Ops:
  0.7 1.0 %copy-done.4 = bf16[96,12,128]{2,0,1:T(8,128)(2,1)S(1)} copy-done((bf16[96,12,128]{2,0,1:T(8,128)(2,1)S(1)}, bf16[96,12,128]{2,0,1:T(8,128)(2,1)}, u32[]{:S(2)}) %copy-start.4) | copy-done | bytes 294936
  2.4 4.6 %collective-permute-start = (bf16[1,96,128]{2,1,0:T(8,128)(2,1)S(1)}, bf16[1,96,128]{2,1,0:T(8,128)(2,1)S(1)}, u32[]{:S(2)}, u32[]{:S(2)}) collective-permute-start(bf16[1,96,128]{2,1,0:T(8,128)(2,1)S(1)} %get-tuple-element.30), channel_id=1, source_target_pairs={{0,7},{1,2},{2,1},{3,4},{4,3},{5,6},{6,5},{7,0},{8,15},{9,10},{10,... | collective-permute-start | bytes 73736 | tf_op jit(solution)/shard_map/ppermute | solution.py:408
  7.6 2.3 %collective-permute-start.1 = (bf16[1,96,128]{2,1,0:T(8,128)(2,1)S(1)}, bf16[1,96,128]{2,1,0:T(8,128)(2,1)S(1)}, u32[]{:S(2)}, u32[]{:S(2)}) collective-permute-start(bf16[1,96,128]{2,1,0:T(8,128)(2,1)S(1)} %get-tuple-element.31), channel_id=1, source_target_pairs={{0,1},{1,0},{2,3},{3,2},{4,5},{5,4},{6,7},{7,6},{8,9},{9,8},{10,11... | collective-permute-start | bytes 73736 | tf_op jit(solution)/shard_map/ppermute | solution.py:408
  10.0 1.5 %collective-permute-start.8 = (bf16[3,96,128]{2,1,0:T(8,128)(2,1)S(1)}, bf16[3,96,128]{2,1,0:T(8,128)(2,1)S(1)}, u32[]{:S(2)}, u32[]{:S(2)}) collective-permute-start(bf16[3,96,128]{2,1,0:T(8,128)(2,1)S(1)} %get-tuple-element.38), channel_id=1, source_target_pairs={{0,8},{8,0},{16,24},{24,16},{1,9},{9,1},{17,25},{25,17},{2,10},{10... | collective-permute-start | bytes 221192 | tf_op jit(solution)/shard_map/ppermute | solution.py:408
  11.7 4.3 %collective-permute-done.2.top_ref = bf16[3,96,128]{2,1,0:T(8,128)(2,1)S(1)} collective-permute-done((bf16[3,96,128]{2,1,0:T(8,128)(2,1)S(1)}, bf16[3,96,128]{2,1,0:T(8,128)(2,1)S(1)}, u32[]{:S(2)}, u32[]{:S(2)}) %collective-permute-start.2) | collective-permute-done | bytes 73760 | tf_op jit(solution)/shard_map/ppermute | solution.py:408
  16.1 3.0 %inner.1 = (f32[12,96,128]{2,1,0:T(8,128)S(1)}, f32[49,96,128]{2,1,0:T(8,128)S(1)}) custom-call(bf16[12,96,128]{2,1,0:T(8,128)(2,1)S(1)} %bitcast.18, f32[96,128]{1,0:T(8,128)S(1)} %pad_convert_fusion.weight_ref), custom_call_target="tpu_custom_call" | custom-call | flops 3849999872 | tf_op jit(solution)/shard_map/inner/pallas_call | solution.py:454
  19.3 1.6 %collective-permute-start.9 = (bf16[3,96,128]{2,1,0:T(8,128)(2,1)S(1)}, bf16[3,96,128]{2,1,0:T(8,128)(2,1)S(1)}, u32[]{:S(2)}, u32[]{:S(2)}) collective-permute-start(bf16[3,96,128]{2,1,0:T(8,128)(2,1)S(1)} %get-tuple-element.39), channel_id=1, source_target_pairs={{0,16},{8,24},{16,0},{24,8},{1,17},{9,25},{17,1},{25,9},{2,18},{10... | collective-permute-start | bytes 221192 | tf_op jit(solution)/shard_map/ppermute | solution.py:408
  21.0 1.4 %collective-permute-start.10 = (bf16[3,96,128]{2,1,0:T(8,128)(2,1)S(1)}, bf16[3,96,128]{2,1,0:T(8,128)(2,1)S(1)}, u32[]{:S(2)}, u32[]{:S(2)}) collective-permute-start(bf16[3,96,128]{2,1,0:T(8,128)(2,1)S(1)} %get-tuple-element.40), channel_id=1, source_target_pairs={{0,24},{8,16},{16,8},{24,0},{1,25},{9,17},{17,9},{25,1},{2,26},{10... | collective-permute-start | bytes 221192 | tf_op jit(solution)/shard_map/ppermute | solution.py:408
  22.4 3.3 %outer.1 = (bf16[3,96,128]{2,1,0:T(8,128)(2,1)S(1)}, bf16[3,96,128]{2,1,0:T(8,128)(2,1)S(1)}, bf16[3,96,128]{2,1,0:T(8,128)(2,1)S(1)}, bf16[3,96,128]{2,1,0:T(8,128)(2,1)S(1)}) custom-call(s32[2]{0:T(128)S(1)} %pad_add_fusion.place_ref, f32[12,96,128]{2,1,0:T(8,128)S(1)} %get-tuple-element.29.inner_ref, ...), custom_call_target="tpu_custom_call" | custom-call | flops 1650000000 | tf_op jit(solution)/shard_map/outer/pallas_call | solution.py:462
  26.3 1.5 %collective-permute-start.6 = (bf16[3,96,128]{2,1,0:T(8,128)(2,1)S(1)}, bf16[3,96,128]{2,1,0:T(8,128)(2,1)S(1)}, u32[]{:S(2)}, u32[]{:S(2)}) collective-permute-start(bf16[3,96,128]{2,1,0:T(8,128)(2,1)S(1)} %get-tuple-element.36), channel_id=1, source_target_pairs={{0,16},{8,24},{16,0},{24,8},{1,17},{9,25},{17,1},{25,9},{2,18},{10... | collective-permute-start | bytes 221192 | tf_op jit(solution)/shard_map/ppermute | solution.py:408
  27.8 1.4 %collective-permute-start.7 = (bf16[3,96,128]{2,1,0:T(8,128)(2,1)S(1)}, bf16[3,96,128]{2,1,0:T(8,128)(2,1)S(1)}, u32[]{:S(2)}, u32[]{:S(2)}) collective-permute-start(bf16[3,96,128]{2,1,0:T(8,128)(2,1)S(1)} %get-tuple-element.37), channel_id=1, source_target_pairs={{0,24},{8,16},{16,8},{24,0},{1,25},{9,17},{17,9},{25,1},{2,26},{10... | collective-permute-start | bytes 221192 | tf_op jit(solution)/shard_map/ppermute | solution.py:408
  29.3 0.7 cotangent.1
  30.8 2.3 %collective-permute-done.7.refs_3_ = bf16[3,96,128]{2,1,0:T(8,128)(2,1)S(1)} collective-permute-done((bf16[3,96,128]{2,1,0:T(8,128)(2,1)S(1)}, bf16[3,96,128]{2,1,0:T(8,128)(2,1)S(1)}, u32[]{:S(2)}, u32[]{:S(2)}) %collective-permute-start.7) | collective-permute-done | bytes 73760 | tf_op jit(solution)/shard_map/ppermute | solution.py:408
  33.1 4.8 %cells.1 = (bf16[3,384,128]{2,1,0:T(8,128)(2,1)}, bf16[3,96,128]{2,1,0:T(8,128)(2,1)S(1)}, bf16[3,96,128]{2,1,0:T(8,128)(2,1)S(1)}, bf16[3,96,128]{2,1,0:T(8,128)(2,1)S(1)}, bf16[3,96,128]{2,1,0:T(8,128)(2,1)S(1)}) custom-call(s32[2]{0:T(128)S(1)} %pad_add_fusion.place_ref, bf16[3,96,128]{2,1,0:T(8,128)(2,1)S(1)} %get-tuple-element.34.refs_0_, ...), custom_call_target="tpu_custom_call" | custom-call | flops 5500000256 | tf_op jit(solution)/shard_map/cells/pallas_call | solution.py:488
  37.9 1.5 %collective-permute-start.11 = (bf16[3,96,128]{2,1,0:T(8,128)(2,1)S(1)}, bf16[3,96,128]{2,1,0:T(8,128)(2,1)S(1)}, u32[]{:S(2)}, u32[]{:S(2)}) collective-permute-start(bf16[3,96,128]{2,1,0:T(8,128)(2,1)S(1)} %get-tuple-element.44), channel_id=1, source_target_pairs={{0,8},{8,0},{16,24},{24,16},{1,9},{9,1},{17,25},{25,17},{2,10},{10... | collective-permute-start | bytes 221192 | tf_op jit(solution)/shard_map/ppermute | solution.py:408
  39.9 1.5 %collective-permute-start.13 = (bf16[3,96,128]{2,1,0:T(8,128)(2,1)S(1)}, bf16[3,96,128]{2,1,0:T(8,128)(2,1)S(1)}, u32[]{:S(2)}, u32[]{:S(2)}) collective-permute-start(bf16[3,96,128]{2,1,0:T(8,128)(2,1)S(1)} %get-tuple-element.46), channel_id=1, source_target_pairs={{0,24},{8,16},{16,8},{24,0},{1,25},{9,17},{17,9},{25,1},{2,26},{10... | collective-permute-start | bytes 221192 | tf_op jit(solution)/shard_map/ppermute | solution.py:408
  41.4 2.2 %columns.1.columns_ref = f32[7,15,96,128]{3,2,1,0:T(8,128)S(1)} custom-call(s32[2]{0:T(128)S(1)} %pad_add_fusion.place_ref, bf16[12,96,128]{2,1,0:T(8,128)(2,1)S(1)} %bitcast.20, bf16[1,96,128]{2,1,0:T(8,128)(2,1)S(1)} %collective-permute-done.off_ref, bf16[1,96,128]{2,1,0:T(8,128)(2,1)S(1)} %collective-permute-done.1.on_ref, ...), custom_call_target="tpu_custom_call" | custom-call | flops 2200000000 | tf_op jit(solution)/shard_map/columns/pallas_call | solution.py:480
  43.7 1.4 %collective-permute-done.13.refs_3_ = bf16[3,96,128]{2,1,0:T(8,128)(2,1)S(1)} collective-permute-done((bf16[3,96,128]{2,1,0:T(8,128)(2,1)S(1)}, bf16[3,96,128]{2,1,0:T(8,128)(2,1)S(1)}, u32[]{:S(2)}, u32[]{:S(2)}) %collective-permute-start.13) | collective-permute-done | bytes 73760 | tf_op jit(solution)/shard_map/ppermute | solution.py:408
  45.1 3.3 %kernel_terms.1 = f32[96,128]{1,0:T(8,128)S(1)} custom-call(s32[2]{0:T(128)S(1)} %pad_add_fusion.place_ref, f32[7,15,96,128]{3,2,1,0:T(8,128)S(1)} %columns.1.columns_ref, bf16[3,96,128]{2,1,0:T(8,128)(2,1)S(1)} %get-tuple-element.43.refs_0_, bf16[3,96,128]{2,1,0:T(8,128)(2,1)S(1)} %collective-permute-done.11.refs_1_, ...), custom_call_target="tpu_custom_call" | custom-call | flops 2750000128 | tf_op jit(solution)/shard_map/kernel_terms/pallas_call | solution.py:506
  49.2 1.5 %collective-permute-start.20 = (bf16[3,96,128]{2,1,0:T(8,128)(2,1)S(1)}, bf16[3,96,128]{2,1,0:T(8,128)(2,1)S(1)}, u32[]{:S(2)}, u32[]{:S(2)}) collective-permute-start(bf16[3,96,128]{2,1,0:T(8,128)(2,1)S(1)} %get-tuple-element.53), channel_id=1, source_target_pairs={{0,16},{8,24},{16,0},{24,8},{1,17},{9,25},{17,1},{25,9},{2,18},{10... | collective-permute-start | bytes 221192 | tf_op jit(solution)/shard_map/ppermute | solution.py:408
  50.8 0.7 %regroup.1 = (bf16[12,96,128]{2,1,0:T(8,128)(2,1)S(1)}, bf16[1,96,128]{2,1,0:T(8,128)(2,1)S(1)}, bf16[1,96,128]{2,1,0:T(8,128)(2,1)S(1)}, bf16[3,96,128]{2,1,0:T(8,128)(2,1)S(1)}) custom-call(s32[2]{0:T(128)S(1)} %pad_add_fusion.place_ref, bf16[3,96,128]{2,1,0:T(8,128)(2,1)S(1)} %get-tuple-element.43.refs_0_, ...), custom_call_target="tpu_custom_call" | custom-call | flops 880000000 | tf_op jit(solution)/shard_map/regroup/pallas_call | solution.py:497
  51.5 0.7 copy-done.7
  52.2 1.1 %collective-permute-start.16 = (bf16[3,96,128]{2,1,0:T(8,128)(2,1)S(1)}, bf16[3,96,128]{2,1,0:T(8,128)(2,1)S(1)}, u32[]{:S(2)}, u32[]{:S(2)}) collective-permute-start(bf16[3,96,128]{2,1,0:T(8,128)(2,1)S(1)} %get-tuple-element.50), channel_id=1, source_target_pairs={{0,7},{1,6},{2,5},{3,4},{4,3},{5,2},{6,1},{7,0},{8,15},{9,14},{10,... | collective-permute-start | bytes 221192 | tf_op jit(solution)/shard_map/ppermute | solution.py:408
  53.3 1.5 %collective-permute-done.23 = f32[96,128]{1,0:T(8,128)S(1)} collective-permute-done((f32[96,128]{1,0:T(8,128)S(1)}, f32[96,128]{1,0:T(8,128)S(1)}, u32[]{:S(2)}, u32[]{:S(2)}) %collective-permute-start.23) | collective-permute-done | bytes 49184 | tf_op jit(solution)/shard_map/ppermute | solution.py:408
  55.4 1.4 %collective-permute-start.21 = (bf16[3,96,128]{2,1,0:T(8,128)(2,1)S(1)}, bf16[3,96,128]{2,1,0:T(8,128)(2,1)S(1)}, u32[]{:S(2)}, u32[]{:S(2)}) collective-permute-start(bf16[3,96,128]{2,1,0:T(8,128)(2,1)S(1)} %get-tuple-element.54), channel_id=1, source_target_pairs={{0,24},{8,16},{16,8},{24,0},{1,25},{9,17},{17,9},{25,1},{2,26},{10... | collective-permute-start | bytes 221192 | tf_op jit(solution)/shard_map/ppermute | solution.py:408
  57.7 0.9 %collective-permute-done.16.top_ref = bf16[3,96,128]{2,1,0:T(8,128)(2,1)S(1)} collective-permute-done((bf16[3,96,128]{2,1,0:T(8,128)(2,1)S(1)}, bf16[3,96,128]{2,1,0:T(8,128)(2,1)S(1)}, u32[]{:S(2)}, u32[]{:S(2)}) %collective-permute-start.16) | collective-permute-done | bytes 73760 | tf_op jit(solution)/shard_map/ppermute | solution.py:408
  58.6 2.5 %collective-permute-start.15 = (bf16[1,96,128]{2,1,0:T(8,128)(2,1)S(1)}, bf16[1,96,128]{2,1,0:T(8,128)(2,1)S(1)}, u32[]{:S(2)}, u32[]{:S(2)}) collective-permute-start(bf16[1,96,128]{2,1,0:T(8,128)(2,1)S(1)} %get-tuple-element.49), channel_id=1, source_target_pairs={{0,1},{1,0},{2,3},{3,2},{4,5},{5,4},{6,7},{7,6},{8,9},{9,8},{10,11... | collective-permute-start | bytes 73736 | tf_op jit(solution)/shard_map/ppermute | solution.py:408
  62.0 1.6 %collective-permute-start.25 = (f32[96,128]{1,0:T(8,128)S(1)}, f32[96,128]{1,0:T(8,128)S(1)}, u32[]{:S(2)}, u32[]{:S(2)}) collective-permute-start(f32[96,128]{1,0:T(8,128)S(1)} %get-tuple-element.59), channel_id=1, source_target_pairs={{0,8},{8,0},{16,24},{24,16},{1,9},{9,1},{17,25},{25,17},{2,10},{10... | collective-permute-start | bytes 147464 | tf_op jit(solution)/shard_map/ppermute | solution.py:408
  64.1 1.5 %collective-permute-start.27 = (f32[96,128]{1,0:T(8,128)S(1)}, f32[96,128]{1,0:T(8,128)S(1)}, u32[]{:S(2)}, u32[]{:S(2)}) collective-permute-start(f32[96,128]{1,0:T(8,128)S(1)} %get-tuple-element.59), channel_id=1, source_target_pairs={{0,24},{8,16},{16,8},{24,0},{1,25},{9,17},{17,9},{25,1},{2,26},{10... | collective-permute-start | bytes 147464 | tf_op jit(solution)/shard_map/ppermute | solution.py:408
  65.6 1.0 %copy-done.8 = bf16[12,96,128]{2,1,0:T(8,128)(2,1)S(1)} copy-done((bf16[12,96,128]{2,1,0:T(8,128)(2,1)S(1)}, bf16[12,96,128]{2,1,0:T(8,128)(2,1)}, u32[]{:S(2)}) %copy-start.8) | copy-done | bytes 294936
  66.6 4.4 %adjoint.1 = bf16[12,96,128]{2,1,0:T(8,128)(2,1)} custom-call(s32[2]{0:T(128)S(1)} %pad_add_fusion.place_ref, bf16[12,96,128]{2,1,0:T(8,128)(2,1)S(1)} %copy-done.8, bf16[1,96,128]{2,1,0:T(8,128)(2,1)S(1)} %collective-permute-done.14.off_ref, bf16[1,96,128]{2,1,0:T(8,128)(2,1)S(1)} %collective-permute-done.15.on_ref, ...), custom_call_target="tpu_custom_call" | custom-call | flops 4400000000 | tf_op jit(solution)/shard_map/adjoint/pallas_call | solution.py:523
  71.0 0.8 %copy.17 = f32[384,49]{0,1:T(8,128)} copy(f32[384,49]{1,0:T(8,128)S(1)} %bitcast.21) | data formatting | bytes 150528
  (69 shorter events, 7.8 us)
Async XLA Ops:
  0.6 10.8 %copy-start = (bf16[384,49]{0,1:T(8,128)(2,1)S(1)}, bf16[384,49]{0,1:T(8,128)(2,1)}, u32[]{:S(2)}) copy-start(bf16[384,49]{0,1:T(8,128)(2,1)} %param.11) | copy-start | bytes 112900
  1.7 14.4 %copy-start.5 = (bf16[96,12,128]{2,0,1:T(8,128)(2,1)S(1)}, bf16[96,12,128]{2,0,1:T(8,128)(2,1)}, u32[]{:S(2)}) copy-start(bf16[96,12,128]{2,0,1:T(8,128)(2,1)} %param.8) | copy-start | bytes 884740
  2.4 16.9 %collective-permute-start = (bf16[1,96,128]{2,1,0:T(8,128)(2,1)S(1)}, bf16[1,96,128]{2,1,0:T(8,128)(2,1)S(1)}, u32[]{:S(2)}, u32[]{:S(2)}) collective-permute-start(bf16[1,96,128]{2,1,0:T(8,128)(2,1)S(1)} %get-tuple-element.30), channel_id=1, source_target_pairs={{0,7},{1,2},{2,1},{3,4},{4,3},{5,6},{6,5},{7,0},{8,15},{9,10},{10,... | collective-permute-start | bytes 73736 | tf_op jit(solution)/shard_map/ppermute | solution.py:408
  6.9 15.5 %collective-permute-start.4 = (bf16[1,96,128]{2,1,0:T(8,128)(2,1)S(1)}, bf16[1,96,128]{2,1,0:T(8,128)(2,1)S(1)}, u32[]{:S(2)}, u32[]{:S(2)}) collective-permute-start(bf16[1,96,128]{2,1,0:T(8,128)(2,1)S(1)} %get-tuple-element.30), channel_id=1, source_target_pairs={{0,0},{1,5},{2,6},{3,3},{4,4},{5,1},{6,2},{7,7},{8,8},{9,13},{10,1... | collective-permute-start | bytes 73736 | tf_op jit(solution)/shard_map/ppermute | solution.py:408
  7.6 13.4 %collective-permute-start.1 = (bf16[1,96,128]{2,1,0:T(8,128)(2,1)S(1)}, bf16[1,96,128]{2,1,0:T(8,128)(2,1)S(1)}, u32[]{:S(2)}, u32[]{:S(2)}) collective-permute-start(bf16[1,96,128]{2,1,0:T(8,128)(2,1)S(1)} %get-tuple-element.31), channel_id=1, source_target_pairs={{0,1},{1,0},{2,3},{3,2},{4,5},{5,4},{6,7},{7,6},{8,9},{9,8},{10,11... | collective-permute-start | bytes 73736 | tf_op jit(solution)/shard_map/ppermute | solution.py:408
  9.9 6.1 %collective-permute-start.2 = (bf16[3,96,128]{2,1,0:T(8,128)(2,1)S(1)}, bf16[3,96,128]{2,1,0:T(8,128)(2,1)S(1)}, u32[]{:S(2)}, u32[]{:S(2)}) collective-permute-start(bf16[3,96,128]{2,1,0:T(8,128)(2,1)S(1)} %get-tuple-element.32), channel_id=1, source_target_pairs={{0,7},{1,6},{2,5},{3,4},{4,3},{5,2},{6,1},{7,0},{8,15},{9,14},{10,... | collective-permute-start | bytes 221192 | tf_op jit(solution)/shard_map/ppermute | solution.py:408
  10.0 17.9 %collective-permute-start.8 = (bf16[3,96,128]{2,1,0:T(8,128)(2,1)S(1)}, bf16[3,96,128]{2,1,0:T(8,128)(2,1)S(1)}, u32[]{:S(2)}, u32[]{:S(2)}) collective-permute-start(bf16[3,96,128]{2,1,0:T(8,128)(2,1)S(1)} %get-tuple-element.38), channel_id=1, source_target_pairs={{0,8},{8,0},{16,24},{24,16},{1,9},{9,1},{17,25},{25,17},{2,10},{10... | collective-permute-start | bytes 221192 | tf_op jit(solution)/shard_map/ppermute | solution.py:408
  11.7 7.4 %copy-start.9 = (f32[384]{0:T(512)S(1)}, f32[384]{0:T(512)}, u32[]{:S(2)}) copy-start(f32[384]{0:T(512)} %param.12) | copy-start | bytes 4612
  11.7 7.5 %copy-start.10 = (f32[384]{0:T(512)S(1)}, f32[384]{0:T(512)}, u32[]{:S(2)}) copy-start(f32[384]{0:T(512)} %param.13) | copy-start | bytes 4612
  16.0 6.4 %collective-permute-start.3 = (bf16[3,96,128]{2,1,0:T(8,128)(2,1)S(1)}, bf16[3,96,128]{2,1,0:T(8,128)(2,1)S(1)}, u32[]{:S(2)}, u32[]{:S(2)}) collective-permute-start(bf16[3,96,128]{2,1,0:T(8,128)(2,1)S(1)} %collective-permute-done.2.top_ref), channel_id=1, source_target_pairs={{0,1},{1,0},{2,3},{3,2},{4,5},{5,4},{6,7},{7,6},{8,9},{9,8},{10,11... | collective-permute-start | bytes 221192 | tf_op jit(solution)/shard_map/ppermute | solution.py:408
  19.3 10.6 %collective-permute-start.9 = (bf16[3,96,128]{2,1,0:T(8,128)(2,1)S(1)}, bf16[3,96,128]{2,1,0:T(8,128)(2,1)S(1)}, u32[]{:S(2)}, u32[]{:S(2)}) collective-permute-start(bf16[3,96,128]{2,1,0:T(8,128)(2,1)S(1)} %get-tuple-element.39), channel_id=1, source_target_pairs={{0,16},{8,24},{16,0},{24,8},{1,17},{9,25},{17,1},{25,9},{2,18},{10... | collective-permute-start | bytes 221192 | tf_op jit(solution)/shard_map/ppermute | solution.py:408
  21.0 9.0 %collective-permute-start.10 = (bf16[3,96,128]{2,1,0:T(8,128)(2,1)S(1)}, bf16[3,96,128]{2,1,0:T(8,128)(2,1)S(1)}, u32[]{:S(2)}, u32[]{:S(2)}) collective-permute-start(bf16[3,96,128]{2,1,0:T(8,128)(2,1)S(1)} %get-tuple-element.40), channel_id=1, source_target_pairs={{0,24},{8,16},{16,8},{24,0},{1,25},{9,17},{17,9},{25,1},{2,26},{10... | collective-permute-start | bytes 221192 | tf_op jit(solution)/shard_map/ppermute | solution.py:408
  25.7 4.9 %collective-permute-start.5 = (bf16[3,96,128]{2,1,0:T(8,128)(2,1)S(1)}, bf16[3,96,128]{2,1,0:T(8,128)(2,1)S(1)}, u32[]{:S(2)}, u32[]{:S(2)}) collective-permute-start(bf16[3,96,128]{2,1,0:T(8,128)(2,1)S(1)} %get-tuple-element.35), channel_id=1, source_target_pairs={{0,8},{8,0},{16,24},{24,16},{1,9},{9,1},{17,25},{25,17},{2,10},{10... | collective-permute-start | bytes 221192 | tf_op jit(solution)/shard_map/ppermute | solution.py:408
  26.3 4.4 %collective-permute-start.6 = (bf16[3,96,128]{2,1,0:T(8,128)(2,1)S(1)}, bf16[3,96,128]{2,1,0:T(8,128)(2,1)S(1)}, u32[]{:S(2)}, u32[]{:S(2)}) collective-permute-start(bf16[3,96,128]{2,1,0:T(8,128)(2,1)S(1)} %get-tuple-element.36), channel_id=1, source_target_pairs={{0,16},{8,24},{16,0},{24,8},{1,17},{9,25},{17,1},{25,9},{2,18},{10... | collective-permute-start | bytes 221192 | tf_op jit(solution)/shard_map/ppermute | solution.py:408
  27.8 5.3 %collective-permute-start.7 = (bf16[3,96,128]{2,1,0:T(8,128)(2,1)S(1)}, bf16[3,96,128]{2,1,0:T(8,128)(2,1)S(1)}, u32[]{:S(2)}, u32[]{:S(2)}) collective-permute-start(bf16[3,96,128]{2,1,0:T(8,128)(2,1)S(1)} %get-tuple-element.37), channel_id=1, source_target_pairs={{0,24},{8,16},{16,8},{24,0},{1,25},{9,17},{17,9},{25,1},{2,26},{10... | collective-permute-start | bytes 221192 | tf_op jit(solution)/shard_map/ppermute | solution.py:408
  37.9 5.7 %collective-permute-start.11 = (bf16[3,96,128]{2,1,0:T(8,128)(2,1)S(1)}, bf16[3,96,128]{2,1,0:T(8,128)(2,1)S(1)}, u32[]{:S(2)}, u32[]{:S(2)}) collective-permute-start(bf16[3,96,128]{2,1,0:T(8,128)(2,1)S(1)} %get-tuple-element.44), channel_id=1, source_target_pairs={{0,8},{8,0},{16,24},{24,16},{1,9},{9,1},{17,25},{25,17},{2,10},{10... | collective-permute-start | bytes 221192 | tf_op jit(solution)/shard_map/ppermute | solution.py:408
  39.4 4.4 %collective-permute-start.12 = (bf16[3,96,128]{2,1,0:T(8,128)(2,1)S(1)}, bf16[3,96,128]{2,1,0:T(8,128)(2,1)S(1)}, u32[]{:S(2)}, u32[]{:S(2)}) collective-permute-start(bf16[3,96,128]{2,1,0:T(8,128)(2,1)S(1)} %get-tuple-element.45), channel_id=1, source_target_pairs={{0,16},{8,24},{16,0},{24,8},{1,17},{9,25},{17,1},{25,9},{2,18},{10... | collective-permute-start | bytes 221192 | tf_op jit(solution)/shard_map/ppermute | solution.py:408
  39.9 5.3 %collective-permute-start.13 = (bf16[3,96,128]{2,1,0:T(8,128)(2,1)S(1)}, bf16[3,96,128]{2,1,0:T(8,128)(2,1)S(1)}, u32[]{:S(2)}, u32[]{:S(2)}) collective-permute-start(bf16[3,96,128]{2,1,0:T(8,128)(2,1)S(1)} %get-tuple-element.46), channel_id=1, source_target_pairs={{0,24},{8,16},{16,8},{24,0},{1,25},{9,17},{17,9},{25,1},{2,26},{10... | collective-permute-start | bytes 221192 | tf_op jit(solution)/shard_map/ppermute | solution.py:408
  48.5 2.2 %collective-permute-start.22 = (f32[96,128]{1,0:T(8,128)S(1)}, f32[96,128]{1,0:T(8,128)S(1)}, u32[]{:S(2)}, u32[]{:S(2)}) collective-permute-start(f32[96,128]{1,0:T(8,128)S(1)} %kernel_terms.1), channel_id=1, source_target_pairs={{0,1},{1,0},{2,3},{3,2},{4,5},{5,4},{6,7},{7,6},{8,9},{9,8},{10,11... | collective-permute-start | bytes 147464 | tf_op jit(solution)/shard_map/ppermute | solution.py:408
  48.5 8.3 %collective-permute-start.19 = (bf16[3,96,128]{2,1,0:T(8,128)(2,1)S(1)}, bf16[3,96,128]{2,1,0:T(8,128)(2,1)S(1)}, u32[]{:S(2)}, u32[]{:S(2)}) collective-permute-start(bf16[3,96,128]{2,1,0:T(8,128)(2,1)S(1)} %get-tuple-element.52), channel_id=1, source_target_pairs={{0,8},{8,0},{16,24},{24,16},{1,9},{9,1},{17,25},{25,17},{2,10},{10... | collective-permute-start | bytes 221192 | tf_op jit(solution)/shard_map/ppermute | solution.py:408
  49.2 7.9 %collective-permute-start.20 = (bf16[3,96,128]{2,1,0:T(8,128)(2,1)S(1)}, bf16[3,96,128]{2,1,0:T(8,128)(2,1)S(1)}, u32[]{:S(2)}, u32[]{:S(2)}) collective-permute-start(bf16[3,96,128]{2,1,0:T(8,128)(2,1)S(1)} %get-tuple-element.53), channel_id=1, source_target_pairs={{0,16},{8,24},{16,0},{24,8},{1,17},{9,25},{17,1},{25,9},{2,18},{10... | collective-permute-start | bytes 221192 | tf_op jit(solution)/shard_map/ppermute | solution.py:408
  50.7 4.2 %collective-permute-start.23 = (f32[96,128]{1,0:T(8,128)S(1)}, f32[96,128]{1,0:T(8,128)S(1)}, u32[]{:S(2)}, u32[]{:S(2)}) collective-permute-start(f32[96,128]{1,0:T(8,128)S(1)} %add.32), channel_id=1, source_target_pairs={{0,2},{1,3},{2,0},{3,1},{4,6},{5,7},{6,4},{7,5},{8,10},{9,11},{10,... | collective-permute-start | bytes 147464 | tf_op jit(solution)/shard_map/ppermute | solution.py:408
  52.2 6.4 %collective-permute-start.16 = (bf16[3,96,128]{2,1,0:T(8,128)(2,1)S(1)}, bf16[3,96,128]{2,1,0:T(8,128)(2,1)S(1)}, u32[]{:S(2)}, u32[]{:S(2)}) collective-permute-start(bf16[3,96,128]{2,1,0:T(8,128)(2,1)S(1)} %get-tuple-element.50), channel_id=1, source_target_pairs={{0,7},{1,6},{2,5},{3,4},{4,3},{5,2},{6,1},{7,0},{8,15},{9,14},{10,... | collective-permute-start | bytes 221192 | tf_op jit(solution)/shard_map/ppermute | solution.py:408
  54.8 6.6 %collective-permute-start.24 = (f32[96,128]{1,0:T(8,128)S(1)}, f32[96,128]{1,0:T(8,128)S(1)}, u32[]{:S(2)}, u32[]{:S(2)}) collective-permute-start(f32[96,128]{1,0:T(8,128)S(1)} %add.33), channel_id=1, source_target_pairs={{0,4},{1,5},{2,6},{3,7},{4,0},{5,1},{6,2},{7,3},{8,12},{9,13},{10,... | collective-permute-start | bytes 147464 | tf_op jit(solution)/shard_map/ppermute | solution.py:408
  55.4 6.7 %collective-permute-start.21 = (bf16[3,96,128]{2,1,0:T(8,128)(2,1)S(1)}, bf16[3,96,128]{2,1,0:T(8,128)(2,1)S(1)}, u32[]{:S(2)}, u32[]{:S(2)}) collective-permute-start(bf16[3,96,128]{2,1,0:T(8,128)(2,1)S(1)} %get-tuple-element.54), channel_id=1, source_target_pairs={{0,24},{8,16},{16,8},{24,0},{1,25},{9,17},{17,9},{25,1},{2,26},{10... | collective-permute-start | bytes 221192 | tf_op jit(solution)/shard_map/ppermute | solution.py:408
  56.8 6.8 %collective-permute-start.14 = (bf16[1,96,128]{2,1,0:T(8,128)(2,1)S(1)}, bf16[1,96,128]{2,1,0:T(8,128)(2,1)S(1)}, u32[]{:S(2)}, u32[]{:S(2)}) collective-permute-start(bf16[1,96,128]{2,1,0:T(8,128)(2,1)S(1)} %get-tuple-element.48), channel_id=1, source_target_pairs={{0,7},{1,2},{2,1},{3,4},{4,3},{5,6},{6,5},{7,0},{8,15},{9,10},{10,... | collective-permute-start | bytes 73736 | tf_op jit(solution)/shard_map/ppermute | solution.py:408
  57.1 8.5 %collective-permute-start.18 = (bf16[1,96,128]{2,1,0:T(8,128)(2,1)S(1)}, bf16[1,96,128]{2,1,0:T(8,128)(2,1)S(1)}, u32[]{:S(2)}, u32[]{:S(2)}) collective-permute-start(bf16[1,96,128]{2,1,0:T(8,128)(2,1)S(1)} %get-tuple-element.48), channel_id=1, source_target_pairs={{0,0},{1,5},{2,6},{3,3},{4,4},{5,1},{6,2},{7,7},{8,8},{9,13},{10,1... | collective-permute-start | bytes 73736 | tf_op jit(solution)/shard_map/ppermute | solution.py:408
  58.6 5.5 %collective-permute-start.15 = (bf16[1,96,128]{2,1,0:T(8,128)(2,1)S(1)}, bf16[1,96,128]{2,1,0:T(8,128)(2,1)S(1)}, u32[]{:S(2)}, u32[]{:S(2)}) collective-permute-start(bf16[1,96,128]{2,1,0:T(8,128)(2,1)S(1)} %get-tuple-element.49), channel_id=1, source_target_pairs={{0,1},{1,0},{2,3},{3,2},{4,5},{5,4},{6,7},{7,6},{8,9},{9,8},{10,11... | collective-permute-start | bytes 73736 | tf_op jit(solution)/shard_map/ppermute | solution.py:408
  61.5 4.1 %collective-permute-start.17 = (bf16[3,96,128]{2,1,0:T(8,128)(2,1)S(1)}, bf16[3,96,128]{2,1,0:T(8,128)(2,1)S(1)}, u32[]{:S(2)}, u32[]{:S(2)}) collective-permute-start(bf16[3,96,128]{2,1,0:T(8,128)(2,1)S(1)} %collective-permute-done.16.top_ref), channel_id=1, source_target_pairs={{0,1},{1,0},{2,3},{3,2},{4,5},{5,4},{6,7},{7,6},{8,9},{9,8},{10,11... | collective-permute-start | bytes 221192 | tf_op jit(solution)/shard_map/ppermute | solution.py:408
  62.0 8.9 %collective-permute-start.25 = (f32[96,128]{1,0:T(8,128)S(1)}, f32[96,128]{1,0:T(8,128)S(1)}, u32[]{:S(2)}, u32[]{:S(2)}) collective-permute-start(f32[96,128]{1,0:T(8,128)S(1)} %get-tuple-element.59), channel_id=1, source_target_pairs={{0,8},{8,0},{16,24},{24,16},{1,9},{9,1},{17,25},{25,17},{2,10},{10... | collective-permute-start | bytes 147464 | tf_op jit(solution)/shard_map/ppermute | solution.py:408
  63.6 7.4 %collective-permute-start.26 = (f32[96,128]{1,0:T(8,128)S(1)}, f32[96,128]{1,0:T(8,128)S(1)}, u32[]{:S(2)}, u32[]{:S(2)}) collective-permute-start(f32[96,128]{1,0:T(8,128)S(1)} %get-tuple-element.59), channel_id=1, source_target_pairs={{0,16},{8,24},{16,0},{24,8},{1,17},{9,25},{17,1},{25,9},{2,18},{10... | collective-permute-start | bytes 147464 | tf_op jit(solution)/shard_map/ppermute | solution.py:408
  64.1 6.9 %collective-permute-start.27 = (f32[96,128]{1,0:T(8,128)S(1)}, f32[96,128]{1,0:T(8,128)S(1)}, u32[]{:S(2)}, u32[]{:S(2)}) collective-permute-start(f32[96,128]{1,0:T(8,128)S(1)} %get-tuple-element.59), channel_id=1, source_target_pairs={{0,24},{8,16},{16,8},{24,0},{1,25},{9,17},{17,9},{25,1},{2,26},{10... | collective-permute-start | bytes 147464 | tf_op jit(solution)/shard_map/ppermute | solution.py:408
  (7 other events, 31.2 us)

commit v3 on v2

v3 whole, which is shorter than its diff:
```python
import jax
import jax.numpy as jnp
from jax import lax
from jax.experimental import pallas as pl
from jax.experimental.pallas import tpu as pltpu
from jax.sharding import PartitionSpec as P

TAPS = 7
REACH = TAPS // 2
EPSILON = 1e-06
ROOT_HALF = 0.7071067811865476
INV_ROOT_TAU = 0.3989422804014327
F32 = jnp.float32
BF16 = jnp.bfloat16
VMEM = pl.BlockSpec(memory_space=pltpu.VMEM)
SMEM = pl.BlockSpec(memory_space=pltpu.SMEM)
SPAN = 2 * REACH
TAP_ROWS = (TAPS * TAPS + 7) // 8 * 8
FIRST = (((0,), (0,)), ((), ()))
LIMIT = 24 * 1024 * 1024


def call(body, out, specs, scratch, micros, name):
    return pl.pallas_call(
        body,
        out_shape=out,
        in_specs=specs,
        out_specs=jax.tree.map(lambda _: VMEM, out),
        scratch_shapes=scratch,
        compiler_params=pltpu.CompilerParams(vmem_limit_bytes=LIMIT),
        cost_estimate=pl.CostEstimate(flops=int(micros * 1.1e9), bytes_accessed=0, transcendentals=0),
        name=name,
    )


def shaped(*shape, dtype=BF16):
    return jax.ShapeDtypeStruct(shape, dtype)


def lanes_of(shape):
    return lax.broadcasted_iota(jnp.int32, shape, len(shape) - 1)


def groups_of(rows):
    per = rows
    while (per + 2 * REACH) * SPAN > 128 or rows % per:
        per -= 1
    return rows // per, per


def ones_where(mask):
    return jnp.where(mask, 1.0, 0.0)


def right_lanes(lane, per, width):
    low = (per + REACH) * SPAN - REACH
    base = SPAN * ((width + SPAN - 1) // SPAN) - width
    place = jnp.where(lane >= low, lane + base, lane)
    return place - SPAN * ((place * 171) >> 10) < REACH


def pack_edges(read, odd, off_ref, on_ref, rows, channels, width):
    count, per = groups_of(rows)
    lane = lanes_of((1, width))
    turn = odd.astype(F32)
    for group in range(count):
        off = jnp.zeros((channels, width), F32)
        on = jnp.zeros((channels, width), F32)
        for place in range(per):
            base = SPAN * place
            line = pltpu.roll(read(group * per + place), base, 1) if place else read(group * per)
            first = ones_where((lane >= base) & (lane < base + REACH))
            spot = (base - REACH) % width
            last = ones_where((lane >= spot) & (lane < spot + REACH))
            off = off + line * (first + turn * (last - first))
            on = on + line * (last + turn * (first - last))
        off_ref[group] = off.astype(BF16)
        on_ref[group] = on.astype(BF16)


def flip_lanes(value, width, top):
    row = lax.broadcasted_iota(jnp.int32, (width, width), 0)
    col = lax.broadcasted_iota(jnp.int32, (width, width), 1)
    exchange = ((row + col == top % width) | (row + col == top % width + width)).astype(BF16)
    return jnp.dot(value, exchange, preferred_element_type=F32)


def flip_fold(lines_of, fold_ref, per, width):
    lane = lanes_of((1, width))
    ends = ones_where((lane >= SPAN * (per - REACH) - REACH) & (lane < SPAN * per - REACH))
    packed = (fold_ref[REACH].astype(F32) * ends).astype(BF16)
    for depth in range(REACH):
        lines_of[depth] = flip_lanes(fold_ref[REACH - 1 - depth], width, width - 1)
    return flip_lanes(packed, width, 2 * SPAN * per - SPAN - 1)


def each_block(channels, step):
    blocks = channels // 8
    unroll = max(n for n in range(1, 5) if blocks % n == 0)
    lax.fori_loop(0, blocks, step, 0, unroll=unroll)


def unpack(group, place, width):
    shift = (-SPAN * place) % width
    return pltpu.roll(group, shift, 1) if shift else group


def fill(lines, edges, read, packs_ref, fold_ref, rows, width):
    per = groups_of(rows)[1]
    folded = flip_fold(lines.at[pl.ds(rows, REACH)], fold_ref, per, width)
    for row in range(rows):
        lines[row] = read(row)
        edges[row] = unpack(packs_ref[row // per], row % per, width)
    for depth in range(REACH):
        edges[rows + depth] = unpack(folded, per + depth, width)


def shifted(line, edge, step, lane, width):
    if step == 0:
        return line
    if step > 0:
        return pltpu.roll(jnp.where(lane < step, edge, line), width - step, 1)
    return pltpu.roll(jnp.where(lane >= width + step, edge, line), -step, 1)


def prepare_body(channels, rows, width):
    def body(place_ref, snap_ref, off_ref, on_ref):
        pack_edges(lambda row: snap_ref[row].astype(F32), place_ref[1], off_ref, on_ref, rows, channels, width)

    return body


def packs_body(channels, rows, width):
    count, per = groups_of(rows)

    def body(place_ref, lines_ref, off_ref, on_ref, packs_ref, fold_ref):
        lane = lanes_of((1, width))
        right = ones_where(right_lanes(lane, per, width))
        near = right + place_ref[1].astype(F32) * (1.0 - 2.0 * right)
        far = 1.0 - near
        for group in range(count):
            value = on_ref[group].astype(F32) * near + off_ref[group].astype(F32) * far
            packs_ref[group] = value
        fold_ref[0:REACH] = lines_ref[rows - REACH :]
        fold_ref[REACH] = value.astype(BF16)

    return body


def inner_body(channels, rows, width):
    def body(snap_ref, weight_ref, out_ref, spread_ref, lines):
        lines[...] = snap_ref[...].astype(F32)
        lane = lanes_of((8, width))

        def step(block, carry):
            span = pl.ds(block * 8, 8)
            weights = weight_ref[span, :]
            sums = [None] * rows
            for col in range(TAPS):
                taps = [jnp.broadcast_to(weights[:, a * TAPS + col : a * TAPS + col + 1], (8, width)) for a in range(TAPS)]
                for a in range(TAPS):
                    spread_ref[a * TAPS + col, span, :] = taps[a]
                for source in range(rows):
                    moved = shifted(lines[source, span, :], 0.0, col - REACH, lane, width)
                    for a in range(TAPS):
                        row = source - a + REACH
                        if 0 <= row < rows:
                            term = taps[a] * moved
                            sums[row] = term if sums[row] is None else sums[row] + term
            for row in range(rows):
                out_ref[row, span, :] = sums[row]
            return carry

        each_block(channels, step)

    return body


def rims_body(channels, rows, width):
    count, per = groups_of(rows)

    def body(inner_ref, packs_ref, spread_ref, out_ref, packed):
        wide = lanes_of((1, width))
        tail = ones_where((wide >= SPAN * (per - REACH) - REACH) & (wide < SPAN * per - REACH))
        begin = ones_where((wide < SPAN * REACH - REACH) | (wide >= width - REACH))
        for group in range(count):
            value = packs_ref[group]
            if group:
                value = value + pltpu.roll(packs_ref[group - 1] * tail, (-SPAN * per) % width, 1)
            if group + 1 < count:
                value = value + pltpu.roll(packs_ref[group + 1] * begin, SPAN * per, 1)
            packed[group] = value
        lane = lanes_of((8, width))
        right = right_lanes(lane, per, width)
        rim = (lane < REACH) | (lane >= width - REACH)

        def step(block, carry):
            span = pl.ds(block * 8, 8)
            for group in range(count):
                near = packed[group, span, :]
                from_right = jnp.where(right, near, 0.0)
                from_left = jnp.where(right, 0.0, near)
                sums = [None, None]
                for a in range(TAPS):
                    for col in range(TAPS):
                        if col == REACH:
                            continue
                        side = col > REACH
                        move = (-(SPAN * (a - REACH) + col - REACH)) % width
                        term = spread_ref[a * TAPS + col, span, :] * pltpu.roll(from_right if side else from_left, move, 1)
                        sums[side] = term if sums[side] is None else sums[side] + term
                rims = jnp.where(right, sums[0], sums[1])
                for place in range(per):
                    row = group * per + place
                    out_ref[row, span, :] = inner_ref[row, span, :] + jnp.where(rim, unpack(rims, place, width), 0.0)
            return carry

        each_block(channels, step)

    return body


def fold_body(levels, channels, rows, width):
    height = rows // levels
    per = groups_of(rows)[1]

    def body(place_ref, part_ref, fold_ref, spread_ref, *rest):
        sends, (total, lines, edges) = rest[:levels], rest[levels:]
        lev = place_ref[0]
        folded = flip_fold(lines, fold_ref, per, width)
        for depth in range(REACH):
            edges[depth] = unpack(folded, per + depth, width)
        lane = lanes_of((8, width))

        def step(block, carry):
            span = pl.ds(block * 8, 8)
            sums = [part_ref[rows - 1 - up, span, :] for up in range(REACH)]
            for depth in range(REACH):
                for col in range(TAPS):
                    moved = shifted(lines[depth, span, :], edges[depth, span, :], col - REACH, lane, width)
                    for up in range(REACH - depth):
                        a = REACH + 1 + depth + up
                        sums[up] = sums[up] + spread_ref[a * TAPS + col, span, :] * moved
            for up in range(REACH):
                total[rows - 1 - up, span, :] = sums[up]
            return carry

        each_block(channels, step)
        total[0 : rows - REACH] = part_ref[0 : rows - REACH]
        for hop in range(levels):
            sends[hop][...] = total[pl.ds((lev ^ hop) * height, height)].astype(BF16)

    return body


def columns_body(channels, rows, width):
    def body(snap_ref, packs_ref, fold_ref, out_ref, lines, edges):
        fill(lines, edges, lambda row: snap_ref[row].astype(F32), packs_ref, fold_ref, rows, width)
        lane = lanes_of((channels, width))
        for col in range(TAPS):
            for source in range(rows + REACH):
                out_ref[col, source] = shifted(lines[source], edges[source], col - REACH, lane, width)

    return body


def cotangent_body(levels, channels, height, width):
    def body(place_ref, snap_ref, cot_ref, mask_ref, up_ref, own_ref, *rest):
        sends, lines = rest[: levels - 1], rest[levels - 1]
        lev = place_ref[0]
        wet = mask_ref[...].astype(F32)
        lines[...] = cot_ref[...].astype(F32) * wet[:, None, :]
        for row in range(height):
            up_ref[:, row * width : (row + 1) * width] = lines[row].astype(BF16)
        for hop in range(levels):
            start = pl.multiple_of((lev ^ hop) * channels, 8)
            for row in range(height):
                value = lines[row, pl.ds(start, channels), :].astype(BF16)
                if hop:
                    sends[hop - 1][height + row] = value
                else:
                    own_ref[row] = value
            if hop:
                sends[hop - 1][0:height] = snap_ref[pl.ds((lev ^ hop) * height, height)]

    return body


def cell_body(levels, channels, height, width, chunk):
    def body(place_ref, *refs):
        convs, refs = refs[:levels], refs[levels:]
        up_ref, gain_ref, shift_ref, win_ref, wout_ref, projected, *refs = refs
        sends, (field, d_lifted) = refs[:levels], refs[levels:]
        lev = place_ref[0]
        for hop in range(levels):
            start = pl.multiple_of((lev ^ hop) * channels, 8)
            for row in range(height):
                field[pl.ds(start, channels), row * width : (row + 1) * width] = convs[hop][row].astype(F32)
        convolved = field[...]
        centre = jnp.mean(convolved, axis=0, keepdims=True)
        centred = convolved - centre
        spread = jnp.mean(centred * centred, axis=0, keepdims=True)
        rstd = lax.rsqrt(spread + EPSILON)
        normed = centred * rstd
        field[...] = normed
        gain = gain_ref[...]
        lifted = (normed * gain + shift_ref[...]).astype(BF16)
        upstream = up_ref[...]
        features = wout_ref.shape[0]
        for piece in range(features // chunk):
            span = slice(piece * chunk, (piece + 1) * chunk)
            hidden = lax.dot_general(win_ref[:, span], lifted, FIRST, preferred_element_type=F32)
            d_active = jnp.dot(wout_ref[span, :], upstream, preferred_element_type=F32)
            half = 0.5 * (1.0 + lax.erf(hidden * ROOT_HALF))
            active = (hidden * half).astype(BF16)
            slope = half + hidden * jnp.exp(-0.5 * hidden * hidden) * INV_ROOT_TAU
            d_hidden = (d_active * slope).astype(BF16)
            out = lax.dot_general(wout_ref[span, :], active, FIRST, preferred_element_type=F32)
            back = jnp.dot(win_ref[:, span], d_hidden, preferred_element_type=F32)
            if piece == 0:
                projected[...] = out
                d_lifted[...] = back
            else:
                projected[...] += out
                d_lifted[...] += back
        d_normed = d_lifted[...] * gain
        normed = field[...]
        first = jnp.mean(d_normed, axis=0, keepdims=True)
        second = jnp.mean(d_normed * normed, axis=0, keepdims=True)
        field[...] = rstd * (d_normed - first - normed * second)
        for hop in range(levels):
            start = pl.multiple_of((lev ^ hop) * channels, 8)
            for row in range(height):
                sends[hop][row] = field[pl.ds(start, channels), row * width : (row + 1) * width].astype(BF16)

    return body


def finish_body(levels, channels, height, width):
    def body(place_ref, snap_ref, mask_ref, projected_ref, *refs):
        others, (result_ref, total) = refs[: levels - 1], refs[levels - 1 :]
        lev = place_ref[0]
        for hop in range(levels):
            start = pl.multiple_of((lev ^ hop) * channels, 8)
            for row in range(height):
                held = others[hop - 1][row] if hop else snap_ref[lev * height + row]
                wet = mask_ref[row : row + 1, :].astype(F32)
                value = held.astype(F32) + projected_ref[pl.ds(start, channels), row * width : (row + 1) * width]
                total[row, pl.ds(start, channels), :] = wet * value
        result_ref[...] = total[...].astype(BF16)

    return body


def gather_body(levels, channels, rows, width):
    height = rows // levels

    def body(place_ref, *refs):
        blocks, (lines_ref, off_ref, on_ref, lines) = refs[:levels], refs[levels:]
        lev, odd = place_ref[0], place_ref[1]
        for hop in range(levels):
            lines[pl.ds((lev ^ hop) * height, height)] = blocks[hop][...].astype(F32)
        lines_ref[...] = lines[...].astype(BF16)
        pack_edges(lambda row: lines[row], odd, off_ref, on_ref, rows, channels, width)

    return body


def kernel_body(levels, channels, rows, width):
    height = rows // levels

    def body(place_ref, columns_ref, *refs):
        blocks, (out_ref, grads, found_ref) = refs[:levels], refs[levels:]
        lev = place_ref[0]
        for hop in range(levels):
            grads[pl.ds((lev ^ hop) * height, height)] = blocks[hop][...].astype(F32)
        out_lane = lanes_of((8, 128))

        def step(block, carry):
            span = pl.ds(block * 8, 8)
            grad = [grads[row, span, :] for row in range(rows)]
            found = jnp.zeros((8, 128), F32)
            for col in range(TAPS):
                sums = [None] * TAPS
                for source in range(rows + REACH):
                    moved = columns_ref[col, source, span, :]
                    for a in range(TAPS):
                        row = source - a + REACH
                        if 0 <= row < rows:
                            term = grad[row] * moved
                            sums[a] = term if sums[a] is None else sums[a] + term
                for a in range(TAPS):
                    found = jnp.where(out_lane == a * TAPS + col, jnp.sum(sums[a], axis=1, keepdims=True), found)
            found_ref[span, :] = found
            return carry

        each_block(channels, step)
        out_ref[:, :channels] = found_ref[...].T[:TAP_ROWS]

    return body


def adjoint_body(levels, channels, rows, width):
    height = rows // levels

    def body(place_ref, d_ref, packs_ref, fold_ref, spread_ref, *refs):
        own_ref, others, (out_ref, lines, edges, total) = refs[0], refs[1:levels], refs[levels:]
        lev = place_ref[0]
        fill(lines, edges, lambda row: d_ref[row].astype(F32), packs_ref, fold_ref, rows, width)
        for hop in range(levels):
            taken = others[hop - 1][height:] if hop else own_ref[...]
            total[pl.ds((lev ^ hop) * height, height)] = taken.astype(F32)
        lane = lanes_of((8, width))

        def step(block, carry):
            span = pl.ds(block * 8, 8)
            sums = [None] * rows
            for col in range(TAPS):
                taps = [spread_ref[a * TAPS + col, span, :] for a in range(TAPS)]
                for source in range(rows):
                    moved = shifted(lines[source, span, :], edges[source, span, :], REACH - col, lane, width)
                    for a in range(TAPS):
                        row = source + a - REACH
                        if 0 <= row < rows:
                            term = taps[a] * moved
                            sums[row] = term if sums[row] is None else sums[row] + term
                for source in range(REACH):
                    moved = shifted(lines[rows + source, span, :], edges[rows + source, span, :], col - REACH, lane, width)
                    for depth in range(REACH - source):
                        row = rows - 1 - depth
                        sums[row] = sums[row] + taps[REACH + 1 + depth + source] * moved
            for row in range(rows):
                total[row, span, :] = total[row, span, :] + sums[row]
            return carry

        each_block(channels, step)
        out_ref[...] = total[...].astype(BF16)

    return body


def across(value, axis, target):
    count = lax.axis_size(axis)
    return lax.ppermute(value, axis, [(i, target(i) % count) for i in range(count)])


def level_swap(blocks):
    return [across(block, "lev", lambda i: i ^ hop) for hop, block in enumerate(blocks, 1)]


def edge_swap(off, on):
    return across(off, "lon", lambda i: i + 1 if i % 2 else i - 1), across(on, "lon", lambda i: i ^ 1)


def mirror(block):
    lanes = lax.axis_size("lon")
    return across(block, "lon", lambda i: lanes - 1 - i)


def by_core(value, moves):
    levels, lanes = lax.axis_size("lev"), lax.axis_size("lon")
    pairs = []
    for lev in range(levels):
        for lon in range(lanes):
            to_lev, to_lon = moves[lon % 2](lev, lon)
            pairs.append((lev * lanes + lon, to_lev * lanes + to_lon))
    return lax.ppermute(value, ("lev", "lon"), pairs)


def fetch_over_lev(terms):
    levels = lax.axis_size("lev")
    got = []
    for hop in range(1, levels, 2):
        other = min(hop + 1, levels - 1)
        got.append(by_core(terms, [lambda v, i: (v ^ hop, i), lambda v, i: (v ^ other, i)]))
    return got, [across(part, "lon", lambda i: i ^ 1) for part in got[:-1]]


def assemble_body(levels, channels):
    count = levels // 2

    def body(place_ref, terms_ref, *refs):
        got, mates, (out_ref, placed) = refs[:count], refs[count : 2 * count - 1], refs[2 * count - 1 :]
        lev, odd = place_ref[0], place_ref[1]
        for hop in range(levels):
            if hop:
                part = (hop - 1) // 2
                value = got[part][...]
                if part < count - 1:
                    mine = odd if hop % 2 == 0 else 1 - odd
                    value = jnp.where(mine == 1, value, mates[part][...])
            else:
                value = terms_ref[...]
            placed[lev ^ hop] = value
        for level in range(levels):
            out_ref[:, level * channels : (level + 1) * channels] = placed[level][: TAPS * TAPS, :channels]

    return body


def shards(snapshot, cotangent, ocean_mask, kernel, norm_gain, norm_shift, weight_in, weight_out):
    levels = lax.axis_size("lev")
    channels, rows, width = snapshot.shape
    height = rows // levels
    total_channels = channels * levels
    cells = height * width
    lev = lax.axis_index("lev")
    odd = lax.axis_index("lon") % 2
    place = jnp.stack([lev, odd]).astype(jnp.int32)
    groups = groups_of(rows)[0]
    weights = lax.dynamic_slice_in_dim(kernel, lev * channels, channels, 0).astype(F32)
    weights = jnp.pad(weights, ((0, 0), (0, 128 - TAPS * TAPS)))
    block = shaped(height, channels, width)
    pack = shaped(groups, channels, width)
    field = pltpu.VMEM((rows, channels, width), F32)
    deep = pltpu.VMEM((rows + REACH, channels, width), F32)
    lines = jnp.swapaxes(snapshot, 0, 1)

    packs_call = call(
        packs_body(channels, rows, width),
        [shaped(groups, channels, width, dtype=F32), shaped(REACH + 1, channels, width)],
        [SMEM] + [VMEM] * 3,
        [],
        0.6,
        "packs",
    )
    off, on = call(prepare_body(channels, rows, width), [pack, pack], [SMEM, VMEM], [], 1.0, "prepare")(place, lines)
    off, on = edge_swap(off, on)
    inner, spread = call(
        inner_body(channels, rows, width),
        [shaped(rows, channels, width, dtype=F32), shaped(TAPS * TAPS, channels, width, dtype=F32)],
        [VMEM] * 2,
        [field],
        3.0,
        "inner",
    )(lines, weights)
    packs, fold = packs_call(place, lines, off, on)
    upstream, up_own, *early_sends = call(
        cotangent_body(levels, channels, height, width),
        [shaped(total_channels, cells), block] + [shaped(2 * height, channels, width)] * (levels - 1),
        [SMEM] + [VMEM] * 3,
        [pltpu.VMEM((height, total_channels, width), F32)],
        1.0,
        "cotangent",
    )(place, lines, jnp.swapaxes(cotangent, 0, 1), ocean_mask)
    early_sends, fold = lax.optimization_barrier((early_sends, fold))
    others = level_swap(early_sends)
    fold = mirror(fold)
    part = call(
        rims_body(channels, rows, width),
        shaped(rows, channels, width, dtype=F32),
        [VMEM] * 3,
        [pltpu.VMEM((groups, channels, width), F32)],
        2.0,
        "rims",
    )(inner, packs, spread)
    conv_own, *conv_sends = call(
        fold_body(levels, channels, rows, width),
        [block] * levels,
        [SMEM] + [VMEM] * 3,
        [field] + [pltpu.VMEM((REACH, channels, width), F32)] * 2,
        1.2,
        "fold",
    )(place, part, fold, spread)
    convs = [conv_own] + level_swap(conv_sends)
    convs, others = lax.optimization_barrier((convs, others))
    columns = call(
        columns_body(channels, rows, width),
        shaped(TAPS, rows + REACH, channels, width, dtype=F32),
        [VMEM] * 3,
        [deep, deep],
        2.0,
        "columns",
    )(lines, packs, fold)
    projected, d_own, *d_sends = call(
        cell_body(levels, channels, height, width, 512),
        [shaped(total_channels, cells, dtype=F32)] + [block] * levels,
        [SMEM] + [VMEM] * (levels + 5),
        [pltpu.VMEM((total_channels, cells), F32)] * 2,
        5.0,
        "cells",
    )(place, *convs, upstream, norm_gain[:, None], norm_shift[:, None], weight_in, weight_out)
    d_blocks = [d_own] + level_swap(d_sends)
    result = call(
        finish_body(levels, channels, height, width),
        shaped(height, total_channels, width),
        [SMEM] + [VMEM] * (levels + 2),
        [pltpu.VMEM((height, total_channels, width), F32)],
        1.0,
        "finish",
    )(place, lines, ocean_mask, projected, *others)
    result, d_blocks = lax.optimization_barrier((result, d_blocks))
    d_lines, off, on = call(
        gather_body(levels, channels, rows, width),
        [shaped(rows, channels, width), pack, pack],
        [SMEM] + [VMEM] * levels,
        [field],
        0.8,
        "regroup",
    )(place, *d_blocks)
    columns, off = lax.optimization_barrier((columns, off))
    terms = call(
        kernel_body(levels, channels, rows, width),
        shaped(TAP_ROWS, 128, dtype=F32),
        [SMEM] + [VMEM] * (1 + levels),
        [field, pltpu.VMEM((channels, 128), F32)],
        0.01,
        "kernel_terms",
    )(place, columns, *d_blocks)
    terms = terms + across(terms, "lon", lambda i: i ^ 1)
    d_packs, d_fold = packs_call(place, d_lines, *edge_swap(off, on))
    terms, d_fold = lax.optimization_barrier((terms, d_fold))
    d_fold = mirror(d_fold)
    terms = terms + across(terms, "lon", lambda i: i ^ 2)
    terms, d_fold = lax.optimization_barrier((terms, d_fold))
    hop = 4
    while hop < lax.axis_size("lon"):
        terms = terms + across(terms, "lon", lambda i: i ^ hop)
        hop *= 2
    d_snapshot = call(
        adjoint_body(levels, channels, rows, width),
        shaped(rows, channels, width),
        [SMEM] + [VMEM] * (4 + levels),
        [deep, deep, field],
        4.0,
        "adjoint",
    )(place, d_lines, d_packs, d_fold, spread, up_own, *others)
    terms, d_snapshot = lax.optimization_barrier((terms, d_snapshot))
    got, mates = fetch_over_lev(terms)
    kernel_grad = call(
        assemble_body(levels, channels),
        shaped(TAPS * TAPS, total_channels, dtype=F32),
        [SMEM] + [VMEM] * (2 * len(got)),
        [pltpu.VMEM((levels, TAP_ROWS, 128), F32)],
        0.8,
        "assemble",
    )(place, terms, *got, *mates)
    return (jnp.swapaxes(result, 0, 1), jnp.swapaxes(d_snapshot, 0, 1), kernel_grad.T)


def solution(mesh):
    placed = (
        P("lev", None, "lon"),
        P(None, "lev", "lon"),
        P("lev", "lon"),
        P(),
        P(),
        P(),
        P(),
        P(),
    )
    return jax.shard_map(
        shards,
        mesh=mesh,
        in_specs=placed,
        out_specs=(P(None, "lev", "lon"), P("lev", None, "lon"), P()),
        check_vma=False,
    )
```

time: 72 us -> 64.1 us (0.89)
  starting transfers between devices: 32.1 us -> 22.3 us
  waiting for transfers between devices: 11.7 us -> 15.9 us
  local copies, waits for them, and re-layouts: 3.88 us -> 1.41 us
    ppermute x28 -> x19, starting transfers between devices: 32.1 us -> 19.2 us  [across(): lax.ppermute(value, axis, [(i, target(i) % count) for i in range(count)])]
    ppermute x0 -> x2, waiting for transfers between devices: none -> 3.15 us  [by_core(): return lax.ppermute(value, ('lev', 'lon'), pairs)]
    ppermute x0 -> x2, starting transfers between devices: none -> 3.11 us  [by_core(): return lax.ppermute(value, ('lev', 'lon'), pairs)]
    unnamed x24 -> x19, local copies, waits for them, and re-layouts: 3.55 us -> 1.12 us
    pallas_call x4 -> x9, Pallas kernels: 12.1 us -> 13.9 us  [the longest x1 4.08 us: shards(): call(cell_body(levels, channels, height, width, 512), [shaped(total_chann...]
    ppermute x28 -> x19, waiting for transfers between devices: 11.7 us -> 12.7 us  [across(): lax.ppermute(value, axis, [(i, target(i) % count) for i in range(count)])]
    pallas_call x1, Pallas kernels: 2.22 us -> 1.4 us  [shards(): call(columns_body(channels, rows, width), shaped(TAPS, rows + REACH, chan...]
  transfers between devices with their start and end apart: 28 -> 21, of which waited for: 9 -> 9; matrix products, arithmetic and copies ran while one was open for 1% -> 1% of each run, Pallas kernels for 20% -> 25%
where the time goes in v3:
time: 64.1 us; the launch traced here: 64 us
  Pallas kernels  23.4 us (37%)
  starting transfers between devices  22.3 us (35%)
  waiting for transfers between devices  15.9 us (25%)
  local copies, waits for them, and re-layouts  1.41 us (2%)
  between operations  0.9 us (1%)
    ppermute x19, starting transfers between devices, across(): lax.ppermute(value, axis, [(i, target(i) % count) for i in range(count)])  19.2 us
    ppermute x19, waiting for transfers between devices, across(): lax.ppermute(value, axis, [(i, target(i) % count) for i in range(count)])  12.7 us
    pallas_call x1, Pallas kernels, shards(): call(cell_body(levels, channels, height, width, 512), [shaped(total_chann...  4.08 us
    pallas_call x1, Pallas kernels, shards(): call(adjoint_body(levels, channels, rows, width), shaped(rows, channels,...  3.67 us
    ppermute x2, waiting for transfers between devices, by_core(): return lax.ppermute(value, ('lev', 'lon'), pairs)  3.15 us
    ppermute x2, starting transfers between devices, by_core(): return lax.ppermute(value, ('lev', 'lon'), pairs)  3.11 us
    pallas_call x1, Pallas kernels, shards(): call(inner_body(channels, rows, width), [shaped(rows, channels, width, dt...  2.92 us
    pallas_call x1, Pallas kernels, shards(): call(kernel_body(levels, channels, rows, width), shaped(TAP_ROWS, 128, dt...  2.66 us
  transfers between devices with their start and end apart: 21, of which 9 were waited for; matrix products, arithmetic and copies ran while one was open for 1% of the time, Pallas kernels for 25%

profile of v3, /device:TPU:0, one launch (start us, length us, event | category | flops | bytes accessed | tf_op | source)
XLA Modules:
  0.0 64.0 jit_solution(16329438733218829579)
XLA Ops:
  0.7 1.0 %copy-done.4 = bf16[96,12,128]{2,0,1:T(8,128)(2,1)S(1)} copy-done((bf16[96,12,128]{2,0,1:T(8,128)(2,1)S(1)}, bf16[96,12,128]{2,0,1:T(8,128)(2,1)}, u32[]{:S(2)}) %copy-start.4) | copy-done | bytes 294936
  1.7 0.7 %prepare.1 = (bf16[1,96,128]{2,1,0:T(8,128)(2,1)S(1)}, bf16[1,96,128]{2,1,0:T(8,128)(2,1)S(1)}) custom-call(s32[2]{0:T(128)S(1)} %pad_add_fusion.place_ref, bf16[12,96,128]{2,1,0:T(8,128)(2,1)S(1)} %bitcast.8), custom_call_target="tpu_custom_call" | custom-call | flops 1100000000 | tf_op jit(solution)/shard_map/prepare/pallas_call | solution.py:527
  2.4 4.6 %collective-permute-start = (bf16[1,96,128]{2,1,0:T(8,128)(2,1)S(1)}, bf16[1,96,128]{2,1,0:T(8,128)(2,1)S(1)}, u32[]{:S(2)}, u32[]{:S(2)}) collective-permute-start(bf16[1,96,128]{2,1,0:T(8,128)(2,1)S(1)} %get-tuple-element.53), channel_id=1, source_target_pairs={{0,7},{1,2},{2,1},{3,4},{4,3},{5,6},{6,5},{7,0},{8,15},{9,10},{10,... | collective-permute-start | bytes 73736 | tf_op jit(solution)/shard_map/ppermute | solution.py:444
  7.2 2.9 %inner.1 = (f32[12,96,128]{2,1,0:T(8,128)S(1)}, f32[49,96,128]{2,1,0:T(8,128)S(1)}) custom-call(bf16[12,96,128]{2,1,0:T(8,128)(2,1)S(1)} %bitcast.9, f32[96,128]{1,0:T(8,128)S(1)} %pad_convert_fusion.weight_ref), custom_call_target="tpu_custom_call" | custom-call | flops 3300000000 | tf_op jit(solution)/shard_map/inner/pallas_call | solution.py:529
  10.2 0.7 %cotangent.1 = (bf16[384,384]{1,0:T(8,128)(2,1)S(1)}, bf16[3,96,128]{2,1,0:T(8,128)(2,1)S(1)}, bf16[6,96,128]{2,1,0:T(8,128)(2,1)S(1)}, bf16[6,96,128]{2,1,0:T(8,128)(2,1)S(1)}, bf16[6,96,128]{2,1,0:T(8,128)(2,1)S(1)}) custom-call(s32[2]{0:T(128)S(1)} %pad_add_fusion.place_ref, bf16[12,96,128]{2,1,0:T(8,128)(2,1)S(1)} %bitcast.10, ...), custom_call_target="tpu_custom_call" | custom-call | flops 1100000000 | tf_op jit(solution)/shard_map/cotangent/pallas_call | solution.py:538
  11.7 0.9 %collective-permute-start.2 = (bf16[4,96,128]{2,1,0:T(8,128)(2,1)S(1)}, bf16[4,96,128]{2,1,0:T(8,128)(2,1)S(1)}, u32[]{:S(2)}, u32[]{:S(2)}) collective-permute-start(bf16[4,96,128]{2,1,0:T(8,128)(2,1)S(1)} %get-tuple-element.61), channel_id=1, source_target_pairs={{0,7},{1,6},{2,5},{3,4},{4,3},{5,2},{6,1},{7,0},{8,15},{9,14},{10,... | collective-permute-start | bytes 294920 | tf_op jit(solution)/shard_map/ppermute | solution.py:444
  12.6 1.5 %collective-permute-start.6 = (bf16[6,96,128]{2,1,0:T(8,128)(2,1)S(1)}, bf16[6,96,128]{2,1,0:T(8,128)(2,1)S(1)}, u32[]{:S(2)}, u32[]{:S(2)}) collective-permute-start(bf16[6,96,128]{2,1,0:T(8,128)(2,1)S(1)} %get-tuple-element.66), channel_id=1, source_target_pairs={{0,8},{8,0},{16,24},{24,16},{1,9},{9,1},{17,25},{25,17},{2,10},{10... | collective-permute-start | bytes 442376 | tf_op jit(solution)/shard_map/ppermute | solution.py:444
  14.1 1.5 %collective-permute-start.7 = (bf16[6,96,128]{2,1,0:T(8,128)(2,1)S(1)}, bf16[6,96,128]{2,1,0:T(8,128)(2,1)S(1)}, u32[]{:S(2)}, u32[]{:S(2)}) collective-permute-start(bf16[6,96,128]{2,1,0:T(8,128)(2,1)S(1)} %get-tuple-element.67), channel_id=1, source_target_pairs={{0,16},{8,24},{16,0},{24,8},{1,17},{9,25},{17,1},{25,9},{2,18},{10... | collective-permute-start | bytes 442376 | tf_op jit(solution)/shard_map/ppermute | solution.py:444
  16.1 1.4 %rims.1.part_ref = f32[12,96,128]{2,1,0:T(8,128)S(1)} custom-call(f32[12,96,128]{2,1,0:T(8,128)S(1)} %get-tuple-element.52.inner_ref, f32[1,96,128]{2,1,0:T(8,128)S(1)} %get-tuple-element.55.packs_ref, f32[49,96,128]{2,1,0:T(8,128)S(1)} %get-tuple-element.56.spread_ref), custom_call_target="tpu_custom_call" | custom-call | flops 2200000000 | tf_op jit(solution)/shard_map/rims/pallas_call | solution.py:549
  18.0 1.3 %fold.1 = (bf16[3,96,128]{2,1,0:T(8,128)(2,1)S(1)}, bf16[3,96,128]{2,1,0:T(8,128)(2,1)S(1)}, bf16[3,96,128]{2,1,0:T(8,128)(2,1)S(1)}, bf16[3,96,128]{2,1,0:T(8,128)(2,1)S(1)}) custom-call(s32[2]{0:T(128)S(1)} %pad_add_fusion.place_ref, f32[12,96,128]{2,1,0:T(8,128)S(1)} %rims.1.part_ref, bf16[4,96,128]{2,1,0:T(8,128)(2,1)S(1)} %collective-permute-done.2.fold_ref, ...), custom_call_target="tpu_custom_call" | custom-call | flops 1320000000 | tf_op jit(solution)/shard_map/fold/pallas_call | solution.py:557
  19.4 1.6 %collective-permute-start.3 = (bf16[3,96,128]{2,1,0:T(8,128)(2,1)S(1)}, bf16[3,96,128]{2,1,0:T(8,128)(2,1)S(1)}, u32[]{:S(2)}, u32[]{:S(2)}) collective-permute-start(bf16[3,96,128]{2,1,0:T(8,128)(2,1)S(1)} %get-tuple-element.63), channel_id=1, source_target_pairs={{0,8},{8,0},{16,24},{24,16},{1,9},{9,1},{17,25},{25,17},{2,10},{10... | collective-permute-start | bytes 221192 | tf_op jit(solution)/shard_map/ppermute | solution.py:444
  20.9 1.5 %collective-permute-start.4 = (bf16[3,96,128]{2,1,0:T(8,128)(2,1)S(1)}, bf16[3,96,128]{2,1,0:T(8,128)(2,1)S(1)}, u32[]{:S(2)}, u32[]{:S(2)}) collective-permute-start(bf16[3,96,128]{2,1,0:T(8,128)(2,1)S(1)} %get-tuple-element.64), channel_id=1, source_target_pairs={{0,16},{8,24},{16,0},{24,8},{1,17},{9,25},{17,1},{25,9},{2,18},{10... | collective-permute-start | bytes 221192 | tf_op jit(solution)/shard_map/ppermute | solution.py:444
  22.9 1.4 %columns.1.columns_ref = f32[7,15,96,128]{3,2,1,0:T(8,128)S(1)} custom-call(bf16[12,96,128]{2,1,0:T(8,128)(2,1)S(1)} %bitcast.12, f32[1,96,128]{2,1,0:T(8,128)S(1)} %get-tuple-element.55.packs_ref, bf16[4,96,128]{2,1,0:T(8,128)(2,1)S(1)} %collective-permute-done.2.fold_ref), custom_call_target="tpu_custom_call" | custom-call | flops 2200000000 | tf_op jit(solution)/shard_map/columns/pallas_call | solution.py:567
  24.4 0.9 %collective-permute-done.4.refs_2_ = bf16[3,96,128]{2,1,0:T(8,128)(2,1)S(1)} collective-permute-done((bf16[3,96,128]{2,1,0:T(8,128)(2,1)S(1)}, bf16[3,96,128]{2,1,0:T(8,128)(2,1)S(1)}, u32[]{:S(2)}, u32[]{:S(2)}) %collective-permute-start.4) | collective-permute-done | bytes 73760 | tf_op jit(solution)/shard_map/ppermute | solution.py:444
  25.3 2.4 %collective-permute-done.5.refs_3_ = bf16[3,96,128]{2,1,0:T(8,128)(2,1)S(1)} collective-permute-done((bf16[3,96,128]{2,1,0:T(8,128)(2,1)S(1)}, bf16[3,96,128]{2,1,0:T(8,128)(2,1)S(1)}, u32[]{:S(2)}, u32[]{:S(2)}) %collective-permute-start.5) | collective-permute-done | bytes 73760 | tf_op jit(solution)/shard_map/ppermute | solution.py:444
  27.7 4.1 %cells.1 = (f32[384,384]{1,0:T(8,128)S(1)}, bf16[3,96,128]{2,1,0:T(8,128)(2,1)S(1)}, bf16[3,96,128]{2,1,0:T(8,128)(2,1)S(1)}, bf16[3,96,128]{2,1,0:T(8,128)(2,1)S(1)}, bf16[3,96,128]{2,1,0:T(8,128)(2,1)S(1)}) custom-call(s32[2]{0:T(128)S(1)} %pad_add_fusion.place_ref, bf16[3,96,128]{2,1,0:T(8,128)(2,1)S(1)} %get-tuple-element.69.refs_0_, ...), custom_call_target="tpu_custom_call" | custom-call | flops 5500000256 | tf_op jit(solution)/shard_map/cells/pallas_call | solution.py:575
  32.4 0.7 %collective-permute-start.10 = (bf16[3,96,128]{2,1,0:T(8,128)(2,1)S(1)}, bf16[3,96,128]{2,1,0:T(8,128)(2,1)S(1)}, u32[]{:S(2)}, u32[]{:S(2)}) collective-permute-start(bf16[3,96,128]{2,1,0:T(8,128)(2,1)S(1)} %get-tuple-element.80), channel_id=1, source_target_pairs={{0,16},{8,24},{16,0},{24,8},{1,17},{9,25},{17,1},{25,9},{2,18},{10... | collective-permute-start | bytes 221192 | tf_op jit(solution)/shard_map/ppermute | solution.py:444
  33.1 2.3 %collective-permute-start.11 = (bf16[3,96,128]{2,1,0:T(8,128)(2,1)S(1)}, bf16[3,96,128]{2,1,0:T(8,128)(2,1)S(1)}, u32[]{:S(2)}, u32[]{:S(2)}) collective-permute-start(bf16[3,96,128]{2,1,0:T(8,128)(2,1)S(1)} %get-tuple-element.81), channel_id=1, source_target_pairs={{0,24},{8,16},{16,8},{24,0},{1,25},{9,17},{17,9},{25,1},{2,26},{10... | collective-permute-start | bytes 221192 | tf_op jit(solution)/shard_map/ppermute | solution.py:444
  35.3 1.3 %finish.1 = bf16[3,384,128]{2,1,0:T(8,128)(2,1)} custom-call(s32[2]{0:T(128)S(1)} %pad_add_fusion.place_ref, bf16[12,96,128]{2,1,0:T(8,128)(2,1)S(1)} %bitcast.13, s32[3,128]{1,0:T(4,128)S(1)} %copy-done.6, f32[384,384]{1,0:T(8,128)S(1)} %get-tuple-element.74.projected_ref, bf16[6,96,128]{2,1,0:T(8,128)(2,1)S(1)} %collective-permute-done.6.refs_0_.refs_1_, ...), custom_call_target="tpu_custom_call" | custom-call | flops 1100000000 | tf_op jit(solution)/shard_map/finish/pallas_call | solution.py:584
  36.7 1.6 %collective-permute-done.11.refs_3_ = bf16[3,96,128]{2,1,0:T(8,128)(2,1)S(1)} collective-permute-done((bf16[3,96,128]{2,1,0:T(8,128)(2,1)S(1)}, bf16[3,96,128]{2,1,0:T(8,128)(2,1)S(1)}, u32[]{:S(2)}, u32[]{:S(2)}) %collective-permute-start.11) | collective-permute-done | bytes 73760 | tf_op jit(solution)/shard_map/ppermute | solution.py:444
  38.3 0.8 %regroup.1 = (bf16[12,96,128]{2,1,0:T(8,128)(2,1)S(1)}, bf16[1,96,128]{2,1,0:T(8,128)(2,1)S(1)}, bf16[1,96,128]{2,1,0:T(8,128)(2,1)S(1)}) custom-call(s32[2]{0:T(128)S(1)} %pad_add_fusion.place_ref, bf16[3,96,128]{2,1,0:T(8,128)(2,1)S(1)} %get-tuple-element.83.refs_0_, bf16[3,96,128]{2,1,0:T(8,128)(2,1)S(1)} %collective-permute-done.9.refs_1_, ...), custom_call_target="tpu_custom_call" | custom-call | flops 880000000 | tf_op jit(solution)/shard_map/regroup/pallas_call | solution.py:593
  39.5 2.7 %kernel_terms.1 = f32[56,128]{1,0:T(8,128)S(1)} custom-call(s32[2]{0:T(128)S(1)} %pad_add_fusion.place_ref, f32[7,15,96,128]{3,2,1,0:T(8,128)S(1)} %columns.1.columns_ref, bf16[3,96,128]{2,1,0:T(8,128)(2,1)S(1)} %get-tuple-element.83.refs_0_, bf16[3,96,128]{2,1,0:T(8,128)(2,1)S(1)} %collective-permute-done.9.refs_1_, ...), custom_call_target="tpu_custom_call" | custom-call | flops 11000000 | tf_op jit(solution)/shard_map/kernel_terms/pallas_call | solution.py:602
  42.5 1.8 %collective-permute-done.13.off_ref = bf16[1,96,128]{2,1,0:T(8,128)(2,1)S(1)} collective-permute-done((bf16[1,96,128]{2,1,0:T(8,128)(2,1)S(1)}, bf16[1,96,128]{2,1,0:T(8,128)(2,1)S(1)}, u32[]{:S(2)}, u32[]{:S(2)}) %collective-permute-start.13) | collective-permute-done | bytes 24608 | tf_op jit(solution)/shard_map/ppermute | solution.py:444
  44.8 2.0 %collective-permute-start.16 = (bf16[4,96,128]{2,1,0:T(8,128)(2,1)S(1)}, bf16[4,96,128]{2,1,0:T(8,128)(2,1)S(1)}, u32[]{:S(2)}, u32[]{:S(2)}) collective-permute-start(bf16[4,96,128]{2,1,0:T(8,128)(2,1)S(1)} %get-tuple-element.94), channel_id=1, source_target_pairs={{0,7},{1,6},{2,5},{3,4},{4,3},{5,2},{6,1},{7,0},{8,15},{9,14},{10,... | collective-permute-start | bytes 294920 | tf_op jit(solution)/shard_map/ppermute | solution.py:444
  46.8 4.7 %collective-permute-done.15 = f32[56,128]{1,0:T(8,128)S(1)} collective-permute-done((f32[56,128]{1,0:T(8,128)S(1)}, f32[56,128]{1,0:T(8,128)S(1)}, u32[]{:S(2)}, u32[]{:S(2)}) %collective-permute-start.15) | collective-permute-done | bytes 28704 | tf_op jit(solution)/shard_map/ppermute | solution.py:444
  52.0 3.7 %adjoint.1 = bf16[12,96,128]{2,1,0:T(8,128)(2,1)} custom-call(s32[2]{0:T(128)S(1)} %pad_add_fusion.place_ref, bf16[12,96,128]{2,1,0:T(8,128)(2,1)S(1)} %get-tuple-element.89.lines_ref.d_ref, f32[1,96,128]{2,1,0:T(8,128)S(1)} %get-tuple-element.96.packs_ref, bf16[4,96,128]{2,1,0:T(8,128)(2,1)S(1)} %collective-permute-done.16.fold_ref, ...), custom_call_target="tpu_custom_call" | custom-call | flops 4400000000 | tf_op jit(solution)/shard_map/adjoint/pallas_call | solution.py:620
  55.6 0.8 %collective-permute-done.17 = f32[56,128]{1,0:T(8,128)S(1)} collective-permute-done((f32[56,128]{1,0:T(8,128)S(1)}, f32[56,128]{1,0:T(8,128)S(1)}, u32[]{:S(2)}, u32[]{:S(2)}) %collective-permute-start.17) | collective-permute-done | bytes 28704 | tf_op jit(solution)/shard_map/ppermute | solution.py:444
  56.4 1.5 %collective-permute-start.18 = (f32[56,128]{1,0:T(8,128)S(1)}, f32[56,128]{1,0:T(8,128)S(1)}, u32[]{:S(2)}, u32[]{:S(2)}) collective-permute-start(f32[56,128]{1,0:T(8,128)S(1)} %add.22.terms_ref), channel_id=1, source_target_pairs={{0,8},{1,17},{2,10},{3,19},{4,12},{5,21},{6,14},{7,23},{8,0},{9,25... | collective-permute-start | bytes 86024 | tf_op jit(solution)/shard_map/ppermute | solution.py:467
  57.9 1.6 %collective-permute-start.19 = (f32[56,128]{1,0:T(8,128)S(1)}, f32[56,128]{1,0:T(8,128)S(1)}, u32[]{:S(2)}, u32[]{:S(2)}) collective-permute-start(f32[56,128]{1,0:T(8,128)S(1)} %add.22.terms_ref), channel_id=1, source_target_pairs={{0,24},{1,25},{2,26},{3,27},{4,28},{5,29},{6,30},{7,31},{8,16},{9,... | collective-permute-start | bytes 86024 | tf_op jit(solution)/shard_map/ppermute | solution.py:467
  59.6 0.8 %collective-permute-done.18.refs_0_ = f32[56,128]{1,0:T(8,128)S(1)} collective-permute-done((f32[56,128]{1,0:T(8,128)S(1)}, f32[56,128]{1,0:T(8,128)S(1)}, u32[]{:S(2)}, u32[]{:S(2)}) %collective-permute-start.18) | collective-permute-done | bytes 28704 | tf_op jit(solution)/shard_map/ppermute | solution.py:467
  60.3 2.4 %collective-permute-done.19.refs_1_ = f32[56,128]{1,0:T(8,128)S(1)} collective-permute-done((f32[56,128]{1,0:T(8,128)S(1)}, f32[56,128]{1,0:T(8,128)S(1)}, u32[]{:S(2)}, u32[]{:S(2)}) %collective-permute-start.19) | collective-permute-done | bytes 28704 | tf_op jit(solution)/shard_map/ppermute | solution.py:467
  62.7 1.3 %assemble.1 = f32[49,384]{1,0:T(8,128)} custom-call(s32[2]{0:T(128)S(1)} %pad_add_fusion.place_ref, f32[56,128]{1,0:T(8,128)S(1)} %add.22.terms_ref, f32[56,128]{1,0:T(8,128)S(1)} %collective-permute-done.18.refs_0_, f32[56,128]{1,0:T(8,128)S(1)} %collective-permute-done.19.refs_1_, f32[56,128]{1,0:T(8,128)S(1)} %collective-permute-done.20.refs_2_), custom_call_target="tpu_custom_call" | custom-call | flops 880000000 | tf_op jit(solution)/shard_map/assemble/pallas_call | solution.py:630
  (51 shorter events, 5.0 us)
Async XLA Ops:
  0.6 6.3 %copy-start = (bf16[384,49]{0,1:T(8,128)(2,1)S(1)}, bf16[384,49]{0,1:T(8,128)(2,1)}, u32[]{:S(2)}) copy-start(bf16[384,49]{0,1:T(8,128)(2,1)} %param.11) | copy-start | bytes 112900
  0.7 1.0 %copy-start.4 = (bf16[96,12,128]{2,0,1:T(8,128)(2,1)S(1)}, bf16[96,12,128]{2,0,1:T(8,128)(2,1)}, u32[]{:S(2)}) copy-start(bf16[96,12,128]{2,0,1:T(8,128)(2,1)} %param.8) | copy-start | bytes 884740
  1.7 5.5 %copy-start.5 = (bf16[96,12,128]{2,0,1:T(8,128)(2,1)S(1)}, bf16[96,12,128]{2,0,1:T(8,128)(2,1)}, u32[]{:S(2)}) copy-start(bf16[96,12,128]{2,0,1:T(8,128)(2,1)} %param.8) | copy-start | bytes 884740
  2.4 8.7 %collective-permute-start = (bf16[1,96,128]{2,1,0:T(8,128)(2,1)S(1)}, bf16[1,96,128]{2,1,0:T(8,128)(2,1)S(1)}, u32[]{:S(2)}, u32[]{:S(2)}) collective-permute-start(bf16[1,96,128]{2,1,0:T(8,128)(2,1)S(1)} %get-tuple-element.53), channel_id=1, source_target_pairs={{0,7},{1,2},{2,1},{3,4},{4,3},{5,6},{6,5},{7,0},{8,15},{9,10},{10,... | collective-permute-start | bytes 73736 | tf_op jit(solution)/shard_map/ppermute | solution.py:444
  7.0 4.2 %collective-permute-start.1 = (bf16[1,96,128]{2,1,0:T(8,128)(2,1)S(1)}, bf16[1,96,128]{2,1,0:T(8,128)(2,1)S(1)}, u32[]{:S(2)}, u32[]{:S(2)}) collective-permute-start(bf16[1,96,128]{2,1,0:T(8,128)(2,1)S(1)} %get-tuple-element.54), channel_id=1, source_target_pairs={{0,1},{1,0},{2,3},{3,2},{4,5},{5,4},{6,7},{7,6},{8,9},{9,8},{10,11... | collective-permute-start | bytes 73736 | tf_op jit(solution)/shard_map/ppermute | solution.py:444
  7.2 3.0 %copy-start.3 = (bf16[384,3,128]{2,0,1:T(8,128)(2,1)S(1)}, bf16[384,3,128]{2,0,1:T(8,128)(2,1)}, u32[]{:S(2)}) copy-start(bf16[384,3,128]{2,0,1:T(8,128)(2,1)} %param.9) | copy-start | bytes 884740
  7.2 3.0 %copy-start.6 = (s32[3,128]{1,0:T(4,128)S(1)}, s32[3,128]{1,0:T(4,128)}, u32[]{:S(2)}) copy-start(s32[3,128]{1,0:T(4,128)} %mask_ref.3) | copy-start | bytes 4612
  10.1 0.8 %copy-start.7 = (f32[384]{0:T(512)S(1)}, f32[384]{0:T(512)}, u32[]{:S(2)}) copy-start(f32[384]{0:T(512)} %param.12) | copy-start | bytes 4612
  10.2 0.9 %copy-start.8 = (f32[384]{0:T(512)S(1)}, f32[384]{0:T(512)}, u32[]{:S(2)}) copy-start(f32[384]{0:T(512)} %param.13) | copy-start | bytes 4612
  11.7 6.3 %collective-permute-start.2 = (bf16[4,96,128]{2,1,0:T(8,128)(2,1)S(1)}, bf16[4,96,128]{2,1,0:T(8,128)(2,1)S(1)}, u32[]{:S(2)}, u32[]{:S(2)}) collective-permute-start(bf16[4,96,128]{2,1,0:T(8,128)(2,1)S(1)} %get-tuple-element.61), channel_id=1, source_target_pairs={{0,7},{1,6},{2,5},{3,4},{4,3},{5,2},{6,1},{7,0},{8,15},{9,14},{10,... | collective-permute-start | bytes 294920 | tf_op jit(solution)/shard_map/ppermute | solution.py:444
  12.6 9.8 %collective-permute-start.6 = (bf16[6,96,128]{2,1,0:T(8,128)(2,1)S(1)}, bf16[6,96,128]{2,1,0:T(8,128)(2,1)S(1)}, u32[]{:S(2)}, u32[]{:S(2)}) collective-permute-start(bf16[6,96,128]{2,1,0:T(8,128)(2,1)S(1)} %get-tuple-element.66), channel_id=1, source_target_pairs={{0,8},{8,0},{16,24},{24,16},{1,9},{9,1},{17,25},{25,17},{2,10},{10... | collective-permute-start | bytes 442376 | tf_op jit(solution)/shard_map/ppermute | solution.py:444
  14.1 10.2 %collective-permute-start.7 = (bf16[6,96,128]{2,1,0:T(8,128)(2,1)S(1)}, bf16[6,96,128]{2,1,0:T(8,128)(2,1)S(1)}, u32[]{:S(2)}, u32[]{:S(2)}) collective-permute-start(bf16[6,96,128]{2,1,0:T(8,128)(2,1)S(1)} %get-tuple-element.67), channel_id=1, source_target_pairs={{0,16},{8,24},{16,0},{24,8},{1,17},{9,25},{17,1},{25,9},{2,18},{10... | collective-permute-start | bytes 442376 | tf_op jit(solution)/shard_map/ppermute | solution.py:444
  15.7 8.7 %collective-permute-start.8 = (bf16[6,96,128]{2,1,0:T(8,128)(2,1)S(1)}, bf16[6,96,128]{2,1,0:T(8,128)(2,1)S(1)}, u32[]{:S(2)}, u32[]{:S(2)}) collective-permute-start(bf16[6,96,128]{2,1,0:T(8,128)(2,1)S(1)} %get-tuple-element.68), channel_id=1, source_target_pairs={{0,24},{8,16},{16,8},{24,0},{1,25},{9,17},{17,9},{25,1},{2,26},{10... | collective-permute-start | bytes 442376 | tf_op jit(solution)/shard_map/ppermute | solution.py:444
  19.4 5.0 %collective-permute-start.3 = (bf16[3,96,128]{2,1,0:T(8,128)(2,1)S(1)}, bf16[3,96,128]{2,1,0:T(8,128)(2,1)S(1)}, u32[]{:S(2)}, u32[]{:S(2)}) collective-permute-start(bf16[3,96,128]{2,1,0:T(8,128)(2,1)S(1)} %get-tuple-element.63), channel_id=1, source_target_pairs={{0,8},{8,0},{16,24},{24,16},{1,9},{9,1},{17,25},{25,17},{2,10},{10... | collective-permute-start | bytes 221192 | tf_op jit(solution)/shard_map/ppermute | solution.py:444
  20.9 4.4 %collective-permute-start.4 = (bf16[3,96,128]{2,1,0:T(8,128)(2,1)S(1)}, bf16[3,96,128]{2,1,0:T(8,128)(2,1)S(1)}, u32[]{:S(2)}, u32[]{:S(2)}) collective-permute-start(bf16[3,96,128]{2,1,0:T(8,128)(2,1)S(1)} %get-tuple-element.64), channel_id=1, source_target_pairs={{0,16},{8,24},{16,0},{24,8},{1,17},{9,25},{17,1},{25,9},{2,18},{10... | collective-permute-start | bytes 221192 | tf_op jit(solution)/shard_map/ppermute | solution.py:444
  22.4 5.3 %copy-start.1 = (bf16[384,1536]{1,0:T(8,128)(2,1)S(1)}, bf16[384,1536]{1,0:T(8,128)(2,1)}, u32[]{:S(2)}) copy-start(bf16[384,1536]{1,0:T(8,128)(2,1)} %refs_7_.1) | copy-start | bytes 3538948
  22.4 5.3 %copy-start.2 = (bf16[1536,384]{1,0:T(8,128)(2,1)S(1)}, bf16[1536,384]{1,0:T(8,128)(2,1)}, u32[]{:S(2)}) copy-start(bf16[1536,384]{1,0:T(8,128)(2,1)} %refs_8_.1) | copy-start | bytes 3538948
  22.4 5.3 %collective-permute-start.5 = (bf16[3,96,128]{2,1,0:T(8,128)(2,1)S(1)}, bf16[3,96,128]{2,1,0:T(8,128)(2,1)S(1)}, u32[]{:S(2)}, u32[]{:S(2)}) collective-permute-start(bf16[3,96,128]{2,1,0:T(8,128)(2,1)S(1)} %get-tuple-element.65), channel_id=1, source_target_pairs={{0,24},{8,16},{16,8},{24,0},{1,25},{9,17},{17,9},{25,1},{2,26},{10... | collective-permute-start | bytes 221192 | tf_op jit(solution)/shard_map/ppermute | solution.py:444
  31.8 4.9 %collective-permute-start.9 = (bf16[3,96,128]{2,1,0:T(8,128)(2,1)S(1)}, bf16[3,96,128]{2,1,0:T(8,128)(2,1)S(1)}, u32[]{:S(2)}, u32[]{:S(2)}) collective-permute-start(bf16[3,96,128]{2,1,0:T(8,128)(2,1)S(1)} %get-tuple-element.79), channel_id=1, source_target_pairs={{0,8},{8,0},{16,24},{24,16},{1,9},{9,1},{17,25},{25,17},{2,10},{10... | collective-permute-start | bytes 221192 | tf_op jit(solution)/shard_map/ppermute | solution.py:444
  32.4 4.4 %collective-permute-start.10 = (bf16[3,96,128]{2,1,0:T(8,128)(2,1)S(1)}, bf16[3,96,128]{2,1,0:T(8,128)(2,1)S(1)}, u32[]{:S(2)}, u32[]{:S(2)}) collective-permute-start(bf16[3,96,128]{2,1,0:T(8,128)(2,1)S(1)} %get-tuple-element.80), channel_id=1, source_target_pairs={{0,16},{8,24},{16,0},{24,8},{1,17},{9,25},{17,1},{25,9},{2,18},{10... | collective-permute-start | bytes 221192 | tf_op jit(solution)/shard_map/ppermute | solution.py:444
  33.1 5.3 %collective-permute-start.11 = (bf16[3,96,128]{2,1,0:T(8,128)(2,1)S(1)}, bf16[3,96,128]{2,1,0:T(8,128)(2,1)S(1)}, u32[]{:S(2)}, u32[]{:S(2)}) collective-permute-start(bf16[3,96,128]{2,1,0:T(8,128)(2,1)S(1)} %get-tuple-element.81), channel_id=1, source_target_pairs={{0,24},{8,16},{16,8},{24,0},{1,25},{9,17},{17,9},{25,1},{2,26},{10... | collective-permute-start | bytes 221192 | tf_op jit(solution)/shard_map/ppermute | solution.py:444
  39.1 5.1 %collective-permute-start.13 = (bf16[1,96,128]{2,1,0:T(8,128)(2,1)S(1)}, bf16[1,96,128]{2,1,0:T(8,128)(2,1)S(1)}, u32[]{:S(2)}, u32[]{:S(2)}) collective-permute-start(bf16[1,96,128]{2,1,0:T(8,128)(2,1)S(1)} %get-tuple-element.90), channel_id=1, source_target_pairs={{0,7},{1,2},{2,1},{3,4},{4,3},{5,6},{6,5},{7,0},{8,15},{9,10},{10,... | collective-permute-start | bytes 73736 | tf_op jit(solution)/shard_map/ppermute | solution.py:444
  39.2 5.0 %collective-permute-start.14 = (bf16[1,96,128]{2,1,0:T(8,128)(2,1)S(1)}, bf16[1,96,128]{2,1,0:T(8,128)(2,1)S(1)}, u32[]{:S(2)}, u32[]{:S(2)}) collective-permute-start(bf16[1,96,128]{2,1,0:T(8,128)(2,1)S(1)} %get-tuple-element.91), channel_id=1, source_target_pairs={{0,1},{1,0},{2,3},{3,2},{4,5},{5,4},{6,7},{7,6},{8,9},{9,8},{10,11... | collective-permute-start | bytes 73736 | tf_op jit(solution)/shard_map/ppermute | solution.py:444
  42.1 2.7 %collective-permute-start.12 = (f32[56,128]{1,0:T(8,128)S(1)}, f32[56,128]{1,0:T(8,128)S(1)}, u32[]{:S(2)}, u32[]{:S(2)}) collective-permute-start(f32[56,128]{1,0:T(8,128)S(1)} %kernel_terms.1), channel_id=1, source_target_pairs={{0,1},{1,0},{2,3},{3,2},{4,5},{5,4},{6,7},{7,6},{8,9},{9,8},{10,11... | collective-permute-start | bytes 86024 | tf_op jit(solution)/shard_map/ppermute | solution.py:444
  44.8 6.6 %collective-permute-start.16 = (bf16[4,96,128]{2,1,0:T(8,128)(2,1)S(1)}, bf16[4,96,128]{2,1,0:T(8,128)(2,1)S(1)}, u32[]{:S(2)}, u32[]{:S(2)}) collective-permute-start(bf16[4,96,128]{2,1,0:T(8,128)(2,1)S(1)} %get-tuple-element.94), channel_id=1, source_target_pairs={{0,7},{1,6},{2,5},{3,4},{4,3},{5,2},{6,1},{7,0},{8,15},{9,14},{10,... | collective-permute-start | bytes 294920 | tf_op jit(solution)/shard_map/ppermute | solution.py:444
  46.8 4.7 %collective-permute-start.15 = (f32[56,128]{1,0:T(8,128)S(1)}, f32[56,128]{1,0:T(8,128)S(1)}, u32[]{:S(2)}, u32[]{:S(2)}) collective-permute-start(f32[56,128]{1,0:T(8,128)S(1)} %add.20), channel_id=1, source_target_pairs={{0,2},{1,3},{2,0},{3,1},{4,6},{5,7},{6,4},{7,5},{8,10},{9,11},{10,... | collective-permute-start | bytes 86024 | tf_op jit(solution)/shard_map/ppermute | solution.py:444
  51.5 5.0 %collective-permute-start.17 = (f32[56,128]{1,0:T(8,128)S(1)}, f32[56,128]{1,0:T(8,128)S(1)}, u32[]{:S(2)}, u32[]{:S(2)}) collective-permute-start(f32[56,128]{1,0:T(8,128)S(1)} %add.21), channel_id=1, source_target_pairs={{0,4},{1,5},{2,6},{3,7},{4,0},{5,1},{6,2},{7,3},{8,12},{9,13},{10,... | collective-permute-start | bytes 86024 | tf_op jit(solution)/shard_map/ppermute | solution.py:444
  56.4 3.9 %collective-permute-start.18 = (f32[56,128]{1,0:T(8,128)S(1)}, f32[56,128]{1,0:T(8,128)S(1)}, u32[]{:S(2)}, u32[]{:S(2)}) collective-permute-start(f32[56,128]{1,0:T(8,128)S(1)} %add.22.terms_ref), channel_id=1, source_target_pairs={{0,8},{1,17},{2,10},{3,19},{4,12},{5,21},{6,14},{7,23},{8,0},{9,25... | collective-permute-start | bytes 86024 | tf_op jit(solution)/shard_map/ppermute | solution.py:467
  57.9 4.8 %collective-permute-start.19 = (f32[56,128]{1,0:T(8,128)S(1)}, f32[56,128]{1,0:T(8,128)S(1)}, u32[]{:S(2)}, u32[]{:S(2)}) collective-permute-start(f32[56,128]{1,0:T(8,128)S(1)} %add.22.terms_ref), channel_id=1, source_target_pairs={{0,24},{1,25},{2,26},{3,27},{4,28},{5,29},{6,30},{7,31},{8,16},{9,... | collective-permute-start | bytes 86024 | tf_op jit(solution)/shard_map/ppermute | solution.py:467
  60.3 2.4 %collective-permute-start.20 = (f32[56,128]{1,0:T(8,128)S(1)}, f32[56,128]{1,0:T(8,128)S(1)}, u32[]{:S(2)}, u32[]{:S(2)}) collective-permute-start(f32[56,128]{1,0:T(8,128)S(1)} %collective-permute-done.18.refs_0_), channel_id=1, source_target_pairs={{0,1},{1,0},{2,3},{3,2},{4,5},{5,4},{6,7},{7,6},{8,9},{9,8},{10,11... | collective-permute-start | bytes 86024 | tf_op jit(solution)/shard_map/ppermute | solution.py:444

commit v4 on v3

--- a/solution.py
+++ b/solution.py
@@ -85,13 +85,52 @@
     return jnp.dot(value, exchange, preferred_element_type=F32)
 
 
-def flip_fold(lines_of, fold_ref, per, width):
+def fold_shape(channels, width):
+    parts = 4 if channels % 32 == 0 else 1
+    share = channels // parts
+    head = (share + 15) // 16 * 16 if parts > 1 else channels
+    return ((head + REACH * channels, width) if parts > 1 else (REACH + 1, channels, width)), head, parts
+
+
+def fold_lanes(per, width):
     lane = lanes_of((1, width))
-    ends = ones_where((lane >= SPAN * (per - REACH) - REACH) & (lane < SPAN * per - REACH))
-    packed = (fold_ref[REACH].astype(F32) * ends).astype(BF16)
+    begin = SPAN * (per - REACH) - REACH
+    return begin, ones_where((lane >= begin) & (lane < SPAN * per - REACH))
+
+
+def write_fold(fold_ref, value, lines_ref, channels, per, width):
+    _, head, parts = fold_shape(channels, width)
+    if parts == 1:
+        fold_ref[0:REACH] = lines_ref[...]
+        fold_ref[REACH] = value.astype(BF16)
+        return
+    begin, ends = fold_lanes(per, width)
+    share = channels // parts
+    kept = value * ends
+    packed = jnp.zeros((share, width), F32)
+    for part in range(parts):
+        packed = packed + pltpu.roll(kept[part * share : (part + 1) * share], (part * (width // parts) - begin) % width, 1)
+    if head > share:
+        packed = jnp.concatenate([packed, jnp.zeros((head - share, width), F32)], axis=0)
+    fold_ref[0:head, :] = packed.astype(BF16)
+    for row in range(REACH):
+        fold_ref[head + row * channels : head + (row + 1) * channels, :] = lines_ref[row]
+
+
+def flip_fold(lines_of, fold_ref, channels, per, width):
+    _, head, parts = fold_shape(channels, width)
+    begin, ends = fold_lanes(per, width)
+    if parts == 1:
+        packed = fold_ref[REACH].astype(F32)
+        rows = [fold_ref[row] for row in range(REACH)]
+    else:
+        held = fold_ref[0:head, :].astype(F32)[: channels // parts]
+        pieces = [pltpu.roll(held, (begin - part * (width // parts)) % width, 1) for part in range(parts)]
+        packed = jnp.concatenate(pieces, axis=0)
+        rows = [fold_ref[head + row * channels : head + (row + 1) * channels, :] for row in range(REACH)]
     for depth in range(REACH):
-        lines_of[depth] = flip_lanes(fold_ref[REACH - 1 - depth], width, width - 1)
-    return flip_lanes(packed, width, 2 * SPAN * per - SPAN - 1)
+        lines_of[depth] = flip_lanes(rows[REACH - 1 - depth], width, width - 1)
+    return flip_lanes((packed * ends).astype(BF16), width, 2 * SPAN * per - SPAN - 1)
 
 
 def each_block(channels, step):
@@ -107,7 +146,7 @@
 
 def fill(lines, edges, read, packs_ref, fold_ref, rows, width):
     per = groups_of(rows)[1]
-    folded = flip_fold(lines.at[pl.ds(rows, REACH)], fold_ref, per, width)
+    folded = flip_fold(lines.at[pl.ds(rows, REACH)], fold_ref, lines.shape[1], per, width)
     for row in range(rows):
         lines[row] = read(row)
         edges[row] = unpack(packs_ref[row // per], row % per, width)
@@ -141,8 +180,7 @@
         for group in range(count):
             value = on_ref[group].astype(F32) * near + off_ref[group].astype(F32) * far
             packs_ref[group] = value
-        fold_ref[0:REACH] = lines_ref[rows - REACH :]
-        fold_ref[REACH] = value.astype(BF16)
+        write_fold(fold_ref, value, lines_ref.at[pl.ds(rows - REACH, REACH)], channels, per, width)
 
     return body
 
@@ -227,7 +265,7 @@
     def body(place_ref, part_ref, fold_ref, spread_ref, *rest):
         sends, (total, lines, edges) = rest[:levels], rest[levels:]
         lev = place_ref[0]
-        folded = flip_fold(lines, fold_ref, per, width)
+        folded = flip_fold(lines, fold_ref, channels, per, width)
         for depth in range(REACH):
             edges[depth] = unpack(folded, per + depth, width)
         lane = lanes_of((8, width))
@@ -457,41 +495,25 @@
     return across(block, "lon", lambda i: lanes - 1 - i)
 
 
-def by_core(value, moves):
-    levels, lanes = lax.axis_size("lev"), lax.axis_size("lon")
-    pairs = []
-    for lev in range(levels):
-        for lon in range(lanes):
-            to_lev, to_lon = moves[lon % 2](lev, lon)
-            pairs.append((lev * lanes + lon, to_lev * lanes + to_lon))
-    return lax.ppermute(value, ("lev", "lon"), pairs)
-
-
-def fetch_over_lev(terms):
-    levels = lax.axis_size("lev")
-    got = []
-    for hop in range(1, levels, 2):
-        other = min(hop + 1, levels - 1)
-        got.append(by_core(terms, [lambda v, i: (v ^ hop, i), lambda v, i: (v ^ other, i)]))
-    return got, [across(part, "lon", lambda i: i ^ 1) for part in got[:-1]]
+def sum_over_chips(terms):
+    lanes = lax.axis_size("lon")
+    hop = 2
+    while hop < lanes:
+        if 2 * hop < lanes:
+            one, two, three = (across(terms, "lon", lambda i: i ^ (n * hop)) for n in (1, 2, 3))
+            terms = (terms + one) + (two + three)
+        else:
+            terms = terms + across(terms, "lon", lambda i: i ^ hop)
+        hop *= 4
+    return terms
 
 
 def assemble_body(levels, channels):
-    count = levels // 2
-
-    def body(place_ref, terms_ref, *refs):
-        got, mates, (out_ref, placed) = refs[:count], refs[count : 2 * count - 1], refs[2 * count - 1 :]
-        lev, odd = place_ref[0], place_ref[1]
-        for hop in range(levels):
-            if hop:
-                part = (hop - 1) // 2
-                value = got[part][...]
-                if part < count - 1:
-                    mine = odd if hop % 2 == 0 else 1 - odd
-                    value = jnp.where(mine == 1, value, mates[part][...])
-            else:
-                value = terms_ref[...]
-            placed[lev ^ hop] = value
+    def body(place_ref, *refs):
+        parts, (out_ref, placed) = refs[:levels], refs[levels:]
+        lev = place_ref[0]
+        for hop in range(levels):
+            placed[lev ^ hop] = parts[hop][...]
         for level in range(levels):
             out_ref[:, level * channels : (level + 1) * channels] = placed[level][: TAPS * TAPS, :channels]
 
@@ -518,7 +540,7 @@
 
     packs_call = call(
         packs_body(channels, rows, width),
-        [shaped(groups, channels, width, dtype=F32), shaped(REACH + 1, channels, width)],
+        [shaped(groups, channels, width, dtype=F32), shaped(*fold_shape(channels, width)[0])],
         [SMEM] + [VMEM] * 3,
         [],
         0.6,
@@ -611,12 +633,7 @@
     d_packs, d_fold = packs_call(place, d_lines, *edge_swap(off, on))
     terms, d_fold = lax.optimization_barrier((terms, d_fold))
     d_fold = mirror(d_fold)
-    terms = terms + across(terms, "lon", lambda i: i ^ 2)
-    terms, d_fold = lax.optimization_barrier((terms, d_fold))
-    hop = 4
-    while hop < lax.axis_size("lon"):
-        terms = terms + across(terms, "lon", lambda i: i ^ hop)
-        hop *= 2
+    terms = sum_over_chips(terms)
     d_snapshot = call(
         adjoint_body(levels, channels, rows, width),
         shaped(rows, channels, width),
@@ -625,16 +642,16 @@
         4.0,
         "adjoint",
     )(place, d_lines, d_packs, d_fold, spread, up_own, *others)
-    terms, d_snapshot = lax.optimization_barrier((terms, d_snapshot))
-    got, mates = fetch_over_lev(terms)
+    others = level_swap([terms] * (levels - 1))
+    others, _ = lax.optimization_barrier((others, d_snapshot))
     kernel_grad = call(
         assemble_body(levels, channels),
         shaped(TAPS * TAPS, total_channels, dtype=F32),
-        [SMEM] + [VMEM] * (2 * len(got)),
+        [SMEM] + [VMEM] * levels,
         [pltpu.VMEM((levels, TAP_ROWS, 128), F32)],
         0.8,
         "assemble",
-    )(place, terms, *got, *mates)
+    )(place, terms, *others)
     return (jnp.swapaxes(result, 0, 1), jnp.swapaxes(d_snapshot, 0, 1), kernel_grad.T)
 
 

time: 64.1 us -> 61.2 us (0.955)
  waiting for transfers between devices: 15.9 us -> 7.12 us
  starting transfers between devices: 22.3 us -> 27.9 us
    ppermute x19 -> x22, starting transfers between devices: 19.2 us -> 27.9 us  [across(): lax.ppermute(value, axis, [(i, target(i) % count) for i in range(count)])]
    ppermute x19 -> x22, waiting for transfers between devices: 12.7 us -> 7.12 us  [across(): lax.ppermute(value, axis, [(i, target(i) % count) for i in range(count)])]
    ppermute x2 -> x0, waiting for transfers between devices: 3.15 us -> none  [by_core(): return lax.ppermute(value, ('lev', 'lon'), pairs)]
    ppermute x2 -> x0, starting transfers between devices: 3.11 us -> none  [by_core(): return lax.ppermute(value, ('lev', 'lon'), pairs)]
  transfers between devices with their start and end apart: 21 -> 22, of which waited for: 9 -> 10; matrix products, arithmetic and copies ran while one was open for 1% -> 1% of each run, Pallas kernels for 25% -> 26%
where the time goes in v4:
time: 61.2 us; the launch traced here: 61 us
  starting transfers between devices  27.9 us (46%)
  Pallas kernels  23.6 us (39%)
  waiting for transfers between devices  7.12 us (12%)
  local copies, waits for them, and re-layouts  1.41 us (2%)
  between operations  0.9 us (1%)
    ppermute x22, starting transfers between devices, across(): lax.ppermute(value, axis, [(i, target(i) % count) for i in range(count)])  27.9 us
    ppermute x22, waiting for transfers between devices, across(): lax.ppermute(value, axis, [(i, target(i) % count) for i in range(count)])  7.12 us
    pallas_call x1, Pallas kernels, shards(): call(cell_body(levels, channels, height, width, 512), [shaped(total_chann...  4.07 us
    pallas_call x1, Pallas kernels, shards(): call(adjoint_body(levels, channels, rows, width), shaped(rows, channels,...  3.68 us
    pallas_call x1, Pallas kernels, shards(): call(inner_body(channels, rows, width), [shaped(rows, channels, width, dt...  2.92 us
    pallas_call x1, Pallas kernels, shards(): call(kernel_body(levels, channels, rows, width), shaped(TAP_ROWS, 128, dt...  2.66 us
    pallas_call x1, Pallas kernels, shards(): call(columns_body(channels, rows, width), shaped(TAPS, rows + REACH, chan...  1.43 us
    pallas_call x1, Pallas kernels, shards(): call(rims_body(channels, rows, width), shaped(rows, channels, width, dtyp...  1.38 us
  transfers between devices with their start and end apart: 22, of which 10 were waited for; matrix products, arithmetic and copies ran while one was open for 1% of the time, Pallas kernels for 26%

profile of v4, /device:TPU:0, one launch (start us, length us, event | category | flops | bytes accessed | tf_op | source)
XLA Modules:
  0.0 61.0 jit_solution(10280113148939297231)
XLA Ops:
  0.7 1.0 %copy-done.4 = bf16[96,12,128]{2,0,1:T(8,128)(2,1)S(1)} copy-done((bf16[96,12,128]{2,0,1:T(8,128)(2,1)S(1)}, bf16[96,12,128]{2,0,1:T(8,128)(2,1)}, u32[]{:S(2)}) %copy-start.4) | copy-done | bytes 294936
  1.7 0.7 %prepare.1 = (bf16[1,96,128]{2,1,0:T(8,128)(2,1)S(1)}, bf16[1,96,128]{2,1,0:T(8,128)(2,1)S(1)}) custom-call(s32[2]{0:T(128)S(1)} %pad_add_fusion.place_ref, bf16[12,96,128]{2,1,0:T(8,128)(2,1)S(1)} %bitcast.8), custom_call_target="tpu_custom_call" | custom-call | flops 1100000000 | tf_op jit(solution)/shard_map/prepare/pallas_call | solution.py:549
  2.4 4.6 %collective-permute-start = (bf16[1,96,128]{2,1,0:T(8,128)(2,1)S(1)}, bf16[1,96,128]{2,1,0:T(8,128)(2,1)S(1)}, u32[]{:S(2)}, u32[]{:S(2)}) collective-permute-start(bf16[1,96,128]{2,1,0:T(8,128)(2,1)S(1)} %get-tuple-element.52), channel_id=1, source_target_pairs={{0,7},{1,2},{2,1},{3,4},{4,3},{5,6},{6,5},{7,0},{8,15},{9,10},{10,... | collective-permute-start | bytes 73736 | tf_op jit(solution)/shard_map/ppermute | solution.py:482
  7.2 2.9 %inner.1 = (f32[12,96,128]{2,1,0:T(8,128)S(1)}, f32[49,96,128]{2,1,0:T(8,128)S(1)}) custom-call(bf16[12,96,128]{2,1,0:T(8,128)(2,1)S(1)} %bitcast.9, f32[96,128]{1,0:T(8,128)S(1)} %pad_convert_fusion.weight_ref), custom_call_target="tpu_custom_call" | custom-call | flops 3300000000 | tf_op jit(solution)/shard_map/inner/pallas_call | solution.py:551
  10.2 0.7 %cotangent.1 = (bf16[384,384]{1,0:T(8,128)(2,1)S(1)}, bf16[3,96,128]{2,1,0:T(8,128)(2,1)S(1)}, bf16[6,96,128]{2,1,0:T(8,128)(2,1)S(1)}, bf16[6,96,128]{2,1,0:T(8,128)(2,1)S(1)}, bf16[6,96,128]{2,1,0:T(8,128)(2,1)S(1)}) custom-call(s32[2]{0:T(128)S(1)} %pad_add_fusion.place_ref, bf16[12,96,128]{2,1,0:T(8,128)(2,1)S(1)} %bitcast.10, ...), custom_call_target="tpu_custom_call" | custom-call | flops 1100000000 | tf_op jit(solution)/shard_map/cotangent/pallas_call | solution.py:560
  11.2 0.6 %packs.2 = (f32[1,96,128]{2,1,0:T(8,128)S(1)}, bf16[320,128]{1,0:T(8,128)(2,1)S(1)}) custom-call(s32[2]{0:T(128)S(1)} %pad_add_fusion.place_ref, bf16[12,96,128]{2,1,0:T(8,128)(2,1)S(1)} %bitcast.11, bf16[1,96,128]{2,1,0:T(8,128)(2,1)S(1)} %collective-permute-done.off_ref, bf16[1,96,128]{2,1,0:T(8,128)(2,1)S(1)} %collective-permute-done.1.on_ref), custom_call_target="tpu_custom_call" | custom-call | flops 660000000 | tf_op jit(solution)/shard_map/packs/pallas_call | solution.py:559
  11.8 0.9 %collective-permute-start.2 = (bf16[320,128]{1,0:T(8,128)(2,1)S(1)}, bf16[320,128]{1,0:T(8,128)(2,1)S(1)}, u32[]{:S(2)}, u32[]{:S(2)}) collective-permute-start(bf16[320,128]{1,0:T(8,128)(2,1)S(1)} %get-tuple-element.60), channel_id=1, source_target_pairs={{0,7},{1,6},{2,5},{3,4},{4,3},{5,2},{6,1},{7,0},{8,15},{9,14},{10,... | collective-permute-start | bytes 245768 | tf_op jit(solution)/shard_map/ppermute | solution.py:482
  12.7 1.5 %collective-permute-start.6 = (bf16[6,96,128]{2,1,0:T(8,128)(2,1)S(1)}, bf16[6,96,128]{2,1,0:T(8,128)(2,1)S(1)}, u32[]{:S(2)}, u32[]{:S(2)}) collective-permute-start(bf16[6,96,128]{2,1,0:T(8,128)(2,1)S(1)} %get-tuple-element.65), channel_id=1, source_target_pairs={{0,8},{8,0},{16,24},{24,16},{1,9},{9,1},{17,25},{25,17},{2,10},{10... | collective-permute-start | bytes 442376 | tf_op jit(solution)/shard_map/ppermute | solution.py:482
  14.2 1.5 %collective-permute-start.7 = (bf16[6,96,128]{2,1,0:T(8,128)(2,1)S(1)}, bf16[6,96,128]{2,1,0:T(8,128)(2,1)S(1)}, u32[]{:S(2)}, u32[]{:S(2)}) collective-permute-start(bf16[6,96,128]{2,1,0:T(8,128)(2,1)S(1)} %get-tuple-element.66), channel_id=1, source_target_pairs={{0,16},{8,24},{16,0},{24,8},{1,17},{9,25},{17,1},{25,9},{2,18},{10... | collective-permute-start | bytes 442376 | tf_op jit(solution)/shard_map/ppermute | solution.py:482
  16.1 1.4 %rims.1.part_ref = f32[12,96,128]{2,1,0:T(8,128)S(1)} custom-call(f32[12,96,128]{2,1,0:T(8,128)S(1)} %get-tuple-element.51.inner_ref, f32[1,96,128]{2,1,0:T(8,128)S(1)} %get-tuple-element.54.packs_ref, f32[49,96,128]{2,1,0:T(8,128)S(1)} %get-tuple-element.55.spread_ref), custom_call_target="tpu_custom_call" | custom-call | flops 2200000000 | tf_op jit(solution)/shard_map/rims/pallas_call | solution.py:571
  17.7 1.3 %fold.1 = (bf16[3,96,128]{2,1,0:T(8,128)(2,1)S(1)}, bf16[3,96,128]{2,1,0:T(8,128)(2,1)S(1)}, bf16[3,96,128]{2,1,0:T(8,128)(2,1)S(1)}, bf16[3,96,128]{2,1,0:T(8,128)(2,1)S(1)}) custom-call(s32[2]{0:T(128)S(1)} %pad_add_fusion.place_ref, f32[12,96,128]{2,1,0:T(8,128)S(1)} %rims.1.part_ref, bf16[320,128]{1,0:T(8,128)(2,1)S(1)} %collective-permute-done.2.fold_ref, ...), custom_call_target="tpu_custom_call" | custom-call | flops 1320000000 | tf_op jit(solution)/shard_map/fold/pallas_call | solution.py:579
  19.0 1.6 %collective-permute-start.3 = (bf16[3,96,128]{2,1,0:T(8,128)(2,1)S(1)}, bf16[3,96,128]{2,1,0:T(8,128)(2,1)S(1)}, u32[]{:S(2)}, u32[]{:S(2)}) collective-permute-start(bf16[3,96,128]{2,1,0:T(8,128)(2,1)S(1)} %get-tuple-element.62), channel_id=1, source_target_pairs={{0,8},{8,0},{16,24},{24,16},{1,9},{9,1},{17,25},{25,17},{2,10},{10... | collective-permute-start | bytes 221192 | tf_op jit(solution)/shard_map/ppermute | solution.py:482
  20.6 1.5 %collective-permute-start.4 = (bf16[3,96,128]{2,1,0:T(8,128)(2,1)S(1)}, bf16[3,96,128]{2,1,0:T(8,128)(2,1)S(1)}, u32[]{:S(2)}, u32[]{:S(2)}) collective-permute-start(bf16[3,96,128]{2,1,0:T(8,128)(2,1)S(1)} %get-tuple-element.63), channel_id=1, source_target_pairs={{0,16},{8,24},{16,0},{24,8},{1,17},{9,25},{17,1},{25,9},{2,18},{10... | collective-permute-start | bytes 221192 | tf_op jit(solution)/shard_map/ppermute | solution.py:482
  22.6 1.4 %columns.1.columns_ref = f32[7,15,96,128]{3,2,1,0:T(8,128)S(1)} custom-call(bf16[12,96,128]{2,1,0:T(8,128)(2,1)S(1)} %bitcast.12, f32[1,96,128]{2,1,0:T(8,128)S(1)} %get-tuple-element.54.packs_ref, bf16[320,128]{1,0:T(8,128)(2,1)S(1)} %collective-permute-done.2.fold_ref), custom_call_target="tpu_custom_call" | custom-call | flops 2200000000 | tf_op jit(solution)/shard_map/columns/pallas_call | solution.py:589
  24.1 0.9 %collective-permute-done.4.refs_2_ = bf16[3,96,128]{2,1,0:T(8,128)(2,1)S(1)} collective-permute-done((bf16[3,96,128]{2,1,0:T(8,128)(2,1)S(1)}, bf16[3,96,128]{2,1,0:T(8,128)(2,1)S(1)}, u32[]{:S(2)}, u32[]{:S(2)}) %collective-permute-start.4) | collective-permute-done | bytes 73760 | tf_op jit(solution)/shard_map/ppermute | solution.py:482
  25.0 2.4 %collective-permute-done.5.refs_3_ = bf16[3,96,128]{2,1,0:T(8,128)(2,1)S(1)} collective-permute-done((bf16[3,96,128]{2,1,0:T(8,128)(2,1)S(1)}, bf16[3,96,128]{2,1,0:T(8,128)(2,1)S(1)}, u32[]{:S(2)}, u32[]{:S(2)}) %collective-permute-start.5) | collective-permute-done | bytes 73760 | tf_op jit(solution)/shard_map/ppermute | solution.py:482
  27.4 4.1 %cells.1 = (f32[384,384]{1,0:T(8,128)S(1)}, bf16[3,96,128]{2,1,0:T(8,128)(2,1)S(1)}, bf16[3,96,128]{2,1,0:T(8,128)(2,1)S(1)}, bf16[3,96,128]{2,1,0:T(8,128)(2,1)S(1)}, bf16[3,96,128]{2,1,0:T(8,128)(2,1)S(1)}) custom-call(s32[2]{0:T(128)S(1)} %pad_add_fusion.place_ref, bf16[3,96,128]{2,1,0:T(8,128)(2,1)S(1)} %get-tuple-element.68.refs_0_, ...), custom_call_target="tpu_custom_call" | custom-call | flops 5500000256 | tf_op jit(solution)/shard_map/cells/pallas_call | solution.py:597
  31.5 0.6 collective-permute-start.9
  32.1 0.7 %collective-permute-start.10 = (bf16[3,96,128]{2,1,0:T(8,128)(2,1)S(1)}, bf16[3,96,128]{2,1,0:T(8,128)(2,1)S(1)}, u32[]{:S(2)}, u32[]{:S(2)}) collective-permute-start(bf16[3,96,128]{2,1,0:T(8,128)(2,1)S(1)} %get-tuple-element.79), channel_id=1, source_target_pairs={{0,16},{8,24},{16,0},{24,8},{1,17},{9,25},{17,1},{25,9},{2,18},{10... | collective-permute-start | bytes 221192 | tf_op jit(solution)/shard_map/ppermute | solution.py:482
  32.8 2.3 %collective-permute-start.11 = (bf16[3,96,128]{2,1,0:T(8,128)(2,1)S(1)}, bf16[3,96,128]{2,1,0:T(8,128)(2,1)S(1)}, u32[]{:S(2)}, u32[]{:S(2)}) collective-permute-start(bf16[3,96,128]{2,1,0:T(8,128)(2,1)S(1)} %get-tuple-element.80), channel_id=1, source_target_pairs={{0,24},{8,16},{16,8},{24,0},{1,25},{9,17},{17,9},{25,1},{2,26},{10... | collective-permute-start | bytes 221192 | tf_op jit(solution)/shard_map/ppermute | solution.py:482
  35.0 1.3 %finish.1 = bf16[3,384,128]{2,1,0:T(8,128)(2,1)} custom-call(s32[2]{0:T(128)S(1)} %pad_add_fusion.place_ref, bf16[12,96,128]{2,1,0:T(8,128)(2,1)S(1)} %bitcast.13, s32[3,128]{1,0:T(4,128)S(1)} %copy-done.6, f32[384,384]{1,0:T(8,128)S(1)} %get-tuple-element.73.projected_ref, bf16[6,96,128]{2,1,0:T(8,128)(2,1)S(1)} %collective-permute-done.6.refs_0_.refs_1_, ...), custom_call_target="tpu_custom_call" | custom-call | flops 1100000000 | tf_op jit(solution)/shard_map/finish/pallas_call | solution.py:606
  36.4 1.6 %collective-permute-done.11.refs_3_ = bf16[3,96,128]{2,1,0:T(8,128)(2,1)S(1)} collective-permute-done((bf16[3,96,128]{2,1,0:T(8,128)(2,1)S(1)}, bf16[3,96,128]{2,1,0:T(8,128)(2,1)S(1)}, u32[]{:S(2)}, u32[]{:S(2)}) %collective-permute-start.11) | collective-permute-done | bytes 73760 | tf_op jit(solution)/shard_map/ppermute | solution.py:482
  38.0 0.8 %regroup.1 = (bf16[12,96,128]{2,1,0:T(8,128)(2,1)S(1)}, bf16[1,96,128]{2,1,0:T(8,128)(2,1)S(1)}, bf16[1,96,128]{2,1,0:T(8,128)(2,1)S(1)}) custom-call(s32[2]{0:T(128)S(1)} %pad_add_fusion.place_ref, bf16[3,96,128]{2,1,0:T(8,128)(2,1)S(1)} %get-tuple-element.82.refs_0_, bf16[3,96,128]{2,1,0:T(8,128)(2,1)S(1)} %collective-permute-done.9.refs_1_, ...), custom_call_target="tpu_custom_call" | custom-call | flops 880000000 | tf_op jit(solution)/shard_map/regroup/pallas_call | solution.py:615
  38.9 2.8 %collective-permute-start.12 = (bf16[1,96,128]{2,1,0:T(8,128)(2,1)S(1)}, bf16[1,96,128]{2,1,0:T(8,128)(2,1)S(1)}, u32[]{:S(2)}, u32[]{:S(2)}) collective-permute-start(bf16[1,96,128]{2,1,0:T(8,128)(2,1)S(1)} %get-tuple-element.88), channel_id=1, source_target_pairs={{0,7},{1,2},{2,1},{3,4},{4,3},{5,6},{6,5},{7,0},{8,15},{9,10},{10,... | collective-permute-start | bytes 73736 | tf_op jit(solution)/shard_map/ppermute | solution.py:482
  41.7 2.7 %kernel_terms.1 = f32[56,128]{1,0:T(8,128)S(1)} custom-call(s32[2]{0:T(128)S(1)} %pad_add_fusion.place_ref, f32[7,15,96,128]{3,2,1,0:T(8,128)S(1)} %columns.1.columns_ref, bf16[3,96,128]{2,1,0:T(8,128)(2,1)S(1)} %get-tuple-element.82.refs_0_, bf16[3,96,128]{2,1,0:T(8,128)(2,1)S(1)} %collective-permute-done.9.refs_1_, ...), custom_call_target="tpu_custom_call" | custom-call | flops 11000000 | tf_op jit(solution)/shard_map/kernel_terms/pallas_call | solution.py:624
  44.5 0.6 %packs.3 = (f32[1,96,128]{2,1,0:T(8,128)S(1)}, bf16[320,128]{1,0:T(8,128)(2,1)S(1)}) custom-call(s32[2]{0:T(128)S(1)} %pad_add_fusion.place_ref, bf16[12,96,128]{2,1,0:T(8,128)(2,1)S(1)} %get-tuple-element.86.lines_ref.d_ref, bf16[1,96,128]{2,1,0:T(8,128)(2,1)S(1)} %collective-permute-done.12.off_ref, bf16[1,96,128]{2,1,0:T(8,128)(2,1)S(1)} %collective-permute-done.13.on_ref), custom_call_target="tpu_custom_call" | custom-call | flops 660000000 | tf_op jit(solution)/shard_map/packs/pallas_call | solution.py:633
  45.6 0.8 %collective-permute-start.18 = (f32[56,128]{1,0:T(8,128)S(1)}, f32[56,128]{1,0:T(8,128)S(1)}, u32[]{:S(2)}, u32[]{:S(2)}) collective-permute-start(f32[56,128]{1,0:T(8,128)S(1)} %add.23), channel_id=1, source_target_pairs={{0,6},{1,7},{2,4},{3,5},{4,2},{5,3},{6,0},{7,1},{8,14},{9,15},{10,... | collective-permute-start | bytes 86024 | tf_op jit(solution)/shard_map/ppermute | solution.py:482
  46.4 3.6 %collective-permute-start.16 = (f32[56,128]{1,0:T(8,128)S(1)}, f32[56,128]{1,0:T(8,128)S(1)}, u32[]{:S(2)}, u32[]{:S(2)}) collective-permute-start(f32[56,128]{1,0:T(8,128)S(1)} %add.23), channel_id=1, source_target_pairs={{0,2},{1,3},{2,0},{3,1},{4,6},{5,7},{6,4},{7,5},{8,10},{9,11},{10,... | collective-permute-start | bytes 86024 | tf_op jit(solution)/shard_map/ppermute | solution.py:482
  50.0 1.0 %collective-permute-start.15 = (bf16[320,128]{1,0:T(8,128)(2,1)S(1)}, bf16[320,128]{1,0:T(8,128)(2,1)S(1)}, u32[]{:S(2)}, u32[]{:S(2)}) collective-permute-start(bf16[320,128]{1,0:T(8,128)(2,1)S(1)} %get-tuple-element.93), channel_id=1, source_target_pairs={{0,7},{1,6},{2,5},{3,4},{4,3},{5,2},{6,1},{7,0},{8,15},{9,14},{10,... | collective-permute-start | bytes 245768 | tf_op jit(solution)/shard_map/ppermute | solution.py:482
  52.3 2.5 %collective-permute-start.21 = (f32[56,128]{1,0:T(8,128)S(1)}, f32[56,128]{1,0:T(8,128)S(1)}, u32[]{:S(2)}, u32[]{:S(2)}) collective-permute-start(f32[56,128]{1,0:T(8,128)S(1)} %add_add_fusion.refs_0_), channel_id=1, source_target_pairs={{0,24},{8,16},{16,8},{24,0},{1,25},{9,17},{17,9},{25,1},{2,26},{10... | collective-permute-start | bytes 86024 | tf_op jit(solution)/shard_map/ppermute | solution.py:482
  56.1 3.7 %adjoint.1 = bf16[12,96,128]{2,1,0:T(8,128)(2,1)} custom-call(s32[2]{0:T(128)S(1)} %pad_add_fusion.place_ref, bf16[12,96,128]{2,1,0:T(8,128)(2,1)S(1)} %get-tuple-element.86.lines_ref.d_ref, f32[1,96,128]{2,1,0:T(8,128)S(1)} %get-tuple-element.90.packs_ref, bf16[320,128]{1,0:T(8,128)(2,1)S(1)} %collective-permute-done.15.fold_ref, ...), custom_call_target="tpu_custom_call" | custom-call | flops 4400000000 | tf_op jit(solution)/shard_map/adjoint/pallas_call | solution.py:637
  59.8 1.3 %assemble.1 = f32[49,384]{1,0:T(8,128)} custom-call(s32[2]{0:T(128)S(1)} %pad_add_fusion.place_ref, f32[56,128]{1,0:T(8,128)S(1)} %add_add_fusion.refs_0_, f32[56,128]{1,0:T(8,128)S(1)} %collective-permute-done.19.refs_1_, f32[56,128]{1,0:T(8,128)S(1)} %collective-permute-done.20.refs_2_, f32[56,128]{1,0:T(8,128)S(1)} %collective-permute-done.21.refs_3_), custom_call_target="tpu_custom_call" | custom-call | flops 880000000 | tf_op jit(solution)/shard_map/assemble/pallas_call | solution.py:647
  (52 shorter events, 4.9 us)
Async XLA Ops:
  0.6 6.3 %copy-start = (bf16[384,49]{0,1:T(8,128)(2,1)S(1)}, bf16[384,49]{0,1:T(8,128)(2,1)}, u32[]{:S(2)}) copy-start(bf16[384,49]{0,1:T(8,128)(2,1)} %param.11) | copy-start | bytes 112900
  0.7 1.0 %copy-start.4 = (bf16[96,12,128]{2,0,1:T(8,128)(2,1)S(1)}, bf16[96,12,128]{2,0,1:T(8,128)(2,1)}, u32[]{:S(2)}) copy-start(bf16[96,12,128]{2,0,1:T(8,128)(2,1)} %param.8) | copy-start | bytes 884740
  1.7 5.5 %copy-start.5 = (bf16[96,12,128]{2,0,1:T(8,128)(2,1)S(1)}, bf16[96,12,128]{2,0,1:T(8,128)(2,1)}, u32[]{:S(2)}) copy-start(bf16[96,12,128]{2,0,1:T(8,128)(2,1)} %param.8) | copy-start | bytes 884740
  2.4 8.7 %collective-permute-start = (bf16[1,96,128]{2,1,0:T(8,128)(2,1)S(1)}, bf16[1,96,128]{2,1,0:T(8,128)(2,1)S(1)}, u32[]{:S(2)}, u32[]{:S(2)}) collective-permute-start(bf16[1,96,128]{2,1,0:T(8,128)(2,1)S(1)} %get-tuple-element.52), channel_id=1, source_target_pairs={{0,7},{1,2},{2,1},{3,4},{4,3},{5,6},{6,5},{7,0},{8,15},{9,10},{10,... | collective-permute-start | bytes 73736 | tf_op jit(solution)/shard_map/ppermute | solution.py:482
  7.0 4.2 %collective-permute-start.1 = (bf16[1,96,128]{2,1,0:T(8,128)(2,1)S(1)}, bf16[1,96,128]{2,1,0:T(8,128)(2,1)S(1)}, u32[]{:S(2)}, u32[]{:S(2)}) collective-permute-start(bf16[1,96,128]{2,1,0:T(8,128)(2,1)S(1)} %get-tuple-element.53), channel_id=1, source_target_pairs={{0,1},{1,0},{2,3},{3,2},{4,5},{5,4},{6,7},{7,6},{8,9},{9,8},{10,11... | collective-permute-start | bytes 73736 | tf_op jit(solution)/shard_map/ppermute | solution.py:482
  7.2 3.0 %copy-start.3 = (bf16[384,3,128]{2,0,1:T(8,128)(2,1)S(1)}, bf16[384,3,128]{2,0,1:T(8,128)(2,1)}, u32[]{:S(2)}) copy-start(bf16[384,3,128]{2,0,1:T(8,128)(2,1)} %param.9) | copy-start | bytes 884740
  7.2 3.0 %copy-start.6 = (s32[3,128]{1,0:T(4,128)S(1)}, s32[3,128]{1,0:T(4,128)}, u32[]{:S(2)}) copy-start(s32[3,128]{1,0:T(4,128)} %mask_ref.3) | copy-start | bytes 4612
  10.1 0.8 %copy-start.7 = (f32[384]{0:T(512)S(1)}, f32[384]{0:T(512)}, u32[]{:S(2)}) copy-start(f32[384]{0:T(512)} %param.12) | copy-start | bytes 4612
  10.2 0.9 %copy-start.8 = (f32[384]{0:T(512)S(1)}, f32[384]{0:T(512)}, u32[]{:S(2)}) copy-start(f32[384]{0:T(512)} %param.13) | copy-start | bytes 4612
  11.8 5.9 %collective-permute-start.2 = (bf16[320,128]{1,0:T(8,128)(2,1)S(1)}, bf16[320,128]{1,0:T(8,128)(2,1)S(1)}, u32[]{:S(2)}, u32[]{:S(2)}) collective-permute-start(bf16[320,128]{1,0:T(8,128)(2,1)S(1)} %get-tuple-element.60), channel_id=1, source_target_pairs={{0,7},{1,6},{2,5},{3,4},{4,3},{5,2},{6,1},{7,0},{8,15},{9,14},{10,... | collective-permute-start | bytes 245768 | tf_op jit(solution)/shard_map/ppermute | solution.py:482
  12.7 9.5 %collective-permute-start.6 = (bf16[6,96,128]{2,1,0:T(8,128)(2,1)S(1)}, bf16[6,96,128]{2,1,0:T(8,128)(2,1)S(1)}, u32[]{:S(2)}, u32[]{:S(2)}) collective-permute-start(bf16[6,96,128]{2,1,0:T(8,128)(2,1)S(1)} %get-tuple-element.65), channel_id=1, source_target_pairs={{0,8},{8,0},{16,24},{24,16},{1,9},{9,1},{17,25},{25,17},{2,10},{10... | collective-permute-start | bytes 442376 | tf_op jit(solution)/shard_map/ppermute | solution.py:482
  14.2 9.9 %collective-permute-start.7 = (bf16[6,96,128]{2,1,0:T(8,128)(2,1)S(1)}, bf16[6,96,128]{2,1,0:T(8,128)(2,1)S(1)}, u32[]{:S(2)}, u32[]{:S(2)}) collective-permute-start(bf16[6,96,128]{2,1,0:T(8,128)(2,1)S(1)} %get-tuple-element.66), channel_id=1, source_target_pairs={{0,16},{8,24},{16,0},{24,8},{1,17},{9,25},{17,1},{25,9},{2,18},{10... | collective-permute-start | bytes 442376 | tf_op jit(solution)/shard_map/ppermute | solution.py:482
  15.7 8.4 %collective-permute-start.8 = (bf16[6,96,128]{2,1,0:T(8,128)(2,1)S(1)}, bf16[6,96,128]{2,1,0:T(8,128)(2,1)S(1)}, u32[]{:S(2)}, u32[]{:S(2)}) collective-permute-start(bf16[6,96,128]{2,1,0:T(8,128)(2,1)S(1)} %get-tuple-element.67), channel_id=1, source_target_pairs={{0,24},{8,16},{16,8},{24,0},{1,25},{9,17},{17,9},{25,1},{2,26},{10... | collective-permute-start | bytes 442376 | tf_op jit(solution)/shard_map/ppermute | solution.py:482
  19.0 5.0 %collective-permute-start.3 = (bf16[3,96,128]{2,1,0:T(8,128)(2,1)S(1)}, bf16[3,96,128]{2,1,0:T(8,128)(2,1)S(1)}, u32[]{:S(2)}, u32[]{:S(2)}) collective-permute-start(bf16[3,96,128]{2,1,0:T(8,128)(2,1)S(1)} %get-tuple-element.62), channel_id=1, source_target_pairs={{0,8},{8,0},{16,24},{24,16},{1,9},{9,1},{17,25},{25,17},{2,10},{10... | collective-permute-start | bytes 221192 | tf_op jit(solution)/shard_map/ppermute | solution.py:482
  20.6 4.4 %collective-permute-start.4 = (bf16[3,96,128]{2,1,0:T(8,128)(2,1)S(1)}, bf16[3,96,128]{2,1,0:T(8,128)(2,1)S(1)}, u32[]{:S(2)}, u32[]{:S(2)}) collective-permute-start(bf16[3,96,128]{2,1,0:T(8,128)(2,1)S(1)} %get-tuple-element.63), channel_id=1, source_target_pairs={{0,16},{8,24},{16,0},{24,8},{1,17},{9,25},{17,1},{25,9},{2,18},{10... | collective-permute-start | bytes 221192 | tf_op jit(solution)/shard_map/ppermute | solution.py:482
  22.1 5.3 %copy-start.1 = (bf16[384,1536]{1,0:T(8,128)(2,1)S(1)}, bf16[384,1536]{1,0:T(8,128)(2,1)}, u32[]{:S(2)}) copy-start(bf16[384,1536]{1,0:T(8,128)(2,1)} %refs_7_.1) | copy-start | bytes 3538948
  22.1 5.3 %copy-start.2 = (bf16[1536,384]{1,0:T(8,128)(2,1)S(1)}, bf16[1536,384]{1,0:T(8,128)(2,1)}, u32[]{:S(2)}) copy-start(bf16[1536,384]{1,0:T(8,128)(2,1)} %refs_8_.1) | copy-start | bytes 3538948
  22.1 5.3 %collective-permute-start.5 = (bf16[3,96,128]{2,1,0:T(8,128)(2,1)S(1)}, bf16[3,96,128]{2,1,0:T(8,128)(2,1)S(1)}, u32[]{:S(2)}, u32[]{:S(2)}) collective-permute-start(bf16[3,96,128]{2,1,0:T(8,128)(2,1)S(1)} %get-tuple-element.64), channel_id=1, source_target_pairs={{0,24},{8,16},{16,8},{24,0},{1,25},{9,17},{17,9},{25,1},{2,26},{10... | collective-permute-start | bytes 221192 | tf_op jit(solution)/shard_map/ppermute | solution.py:482
  31.5 4.9 %collective-permute-start.9 = (bf16[3,96,128]{2,1,0:T(8,128)(2,1)S(1)}, bf16[3,96,128]{2,1,0:T(8,128)(2,1)S(1)}, u32[]{:S(2)}, u32[]{:S(2)}) collective-permute-start(bf16[3,96,128]{2,1,0:T(8,128)(2,1)S(1)} %get-tuple-element.78), channel_id=1, source_target_pairs={{0,8},{8,0},{16,24},{24,16},{1,9},{9,1},{17,25},{25,17},{2,10},{10... | collective-permute-start | bytes 221192 | tf_op jit(solution)/shard_map/ppermute | solution.py:482
  32.1 4.4 %collective-permute-start.10 = (bf16[3,96,128]{2,1,0:T(8,128)(2,1)S(1)}, bf16[3,96,128]{2,1,0:T(8,128)(2,1)S(1)}, u32[]{:S(2)}, u32[]{:S(2)}) collective-permute-start(bf16[3,96,128]{2,1,0:T(8,128)(2,1)S(1)} %get-tuple-element.79), channel_id=1, source_target_pairs={{0,16},{8,24},{16,0},{24,8},{1,17},{9,25},{17,1},{25,9},{2,18},{10... | collective-permute-start | bytes 221192 | tf_op jit(solution)/shard_map/ppermute | solution.py:482
  32.8 5.3 %collective-permute-start.11 = (bf16[3,96,128]{2,1,0:T(8,128)(2,1)S(1)}, bf16[3,96,128]{2,1,0:T(8,128)(2,1)S(1)}, u32[]{:S(2)}, u32[]{:S(2)}) collective-permute-start(bf16[3,96,128]{2,1,0:T(8,128)(2,1)S(1)} %get-tuple-element.80), channel_id=1, source_target_pairs={{0,24},{8,16},{16,8},{24,0},{1,25},{9,17},{17,9},{25,1},{2,26},{10... | collective-permute-start | bytes 221192 | tf_op jit(solution)/shard_map/ppermute | solution.py:482
  38.8 5.6 %collective-permute-start.13 = (bf16[1,96,128]{2,1,0:T(8,128)(2,1)S(1)}, bf16[1,96,128]{2,1,0:T(8,128)(2,1)S(1)}, u32[]{:S(2)}, u32[]{:S(2)}) collective-permute-start(bf16[1,96,128]{2,1,0:T(8,128)(2,1)S(1)} %get-tuple-element.89), channel_id=1, source_target_pairs={{0,1},{1,0},{2,3},{3,2},{4,5},{5,4},{6,7},{7,6},{8,9},{9,8},{10,11... | collective-permute-start | bytes 73736 | tf_op jit(solution)/shard_map/ppermute | solution.py:482
  38.9 5.6 %collective-permute-start.12 = (bf16[1,96,128]{2,1,0:T(8,128)(2,1)S(1)}, bf16[1,96,128]{2,1,0:T(8,128)(2,1)S(1)}, u32[]{:S(2)}, u32[]{:S(2)}) collective-permute-start(bf16[1,96,128]{2,1,0:T(8,128)(2,1)S(1)} %get-tuple-element.88), channel_id=1, source_target_pairs={{0,7},{1,2},{2,1},{3,4},{4,3},{5,6},{6,5},{7,0},{8,15},{9,10},{10,... | collective-permute-start | bytes 73736 | tf_op jit(solution)/shard_map/ppermute | solution.py:482
  44.4 1.2 %collective-permute-start.14 = (f32[56,128]{1,0:T(8,128)S(1)}, f32[56,128]{1,0:T(8,128)S(1)}, u32[]{:S(2)}, u32[]{:S(2)}) collective-permute-start(f32[56,128]{1,0:T(8,128)S(1)} %kernel_terms.1), channel_id=1, source_target_pairs={{0,1},{1,0},{2,3},{3,2},{4,5},{5,4},{6,7},{7,6},{8,9},{9,8},{10,11... | collective-permute-start | bytes 86024 | tf_op jit(solution)/shard_map/ppermute | solution.py:482
  45.6 5.8 %collective-permute-start.18 = (f32[56,128]{1,0:T(8,128)S(1)}, f32[56,128]{1,0:T(8,128)S(1)}, u32[]{:S(2)}, u32[]{:S(2)}) collective-permute-start(f32[56,128]{1,0:T(8,128)S(1)} %add.23), channel_id=1, source_target_pairs={{0,6},{1,7},{2,4},{3,5},{4,2},{5,3},{6,0},{7,1},{8,14},{9,15},{10,... | collective-permute-start | bytes 86024 | tf_op jit(solution)/shard_map/ppermute | solution.py:482
  46.4 5.5 %collective-permute-start.17 = (f32[56,128]{1,0:T(8,128)S(1)}, f32[56,128]{1,0:T(8,128)S(1)}, u32[]{:S(2)}, u32[]{:S(2)}) collective-permute-start(f32[56,128]{1,0:T(8,128)S(1)} %add.23), channel_id=1, source_target_pairs={{0,4},{1,5},{2,6},{3,7},{4,0},{5,1},{6,2},{7,3},{8,12},{9,13},{10,... | collective-permute-start | bytes 86024 | tf_op jit(solution)/shard_map/ppermute | solution.py:482
  46.4 5.8 %collective-permute-start.16 = (f32[56,128]{1,0:T(8,128)S(1)}, f32[56,128]{1,0:T(8,128)S(1)}, u32[]{:S(2)}, u32[]{:S(2)}) collective-permute-start(f32[56,128]{1,0:T(8,128)S(1)} %add.23), channel_id=1, source_target_pairs={{0,2},{1,3},{2,0},{3,1},{4,6},{5,7},{6,4},{7,5},{8,10},{9,11},{10,... | collective-permute-start | bytes 86024 | tf_op jit(solution)/shard_map/ppermute | solution.py:482
  50.0 6.0 %collective-permute-start.15 = (bf16[320,128]{1,0:T(8,128)(2,1)S(1)}, bf16[320,128]{1,0:T(8,128)(2,1)S(1)}, u32[]{:S(2)}, u32[]{:S(2)}) collective-permute-start(bf16[320,128]{1,0:T(8,128)(2,1)S(1)} %get-tuple-element.93), channel_id=1, source_target_pairs={{0,7},{1,6},{2,5},{3,4},{4,3},{5,2},{6,1},{7,0},{8,15},{9,14},{10,... | collective-permute-start | bytes 245768 | tf_op jit(solution)/shard_map/ppermute | solution.py:482
  52.3 7.4 %collective-permute-start.21 = (f32[56,128]{1,0:T(8,128)S(1)}, f32[56,128]{1,0:T(8,128)S(1)}, u32[]{:S(2)}, u32[]{:S(2)}) collective-permute-start(f32[56,128]{1,0:T(8,128)S(1)} %add_add_fusion.refs_0_), channel_id=1, source_target_pairs={{0,24},{8,16},{16,8},{24,0},{1,25},{9,17},{17,9},{25,1},{2,26},{10... | collective-permute-start | bytes 86024 | tf_op jit(solution)/shard_map/ppermute | solution.py:482
  54.8 4.9 %collective-permute-start.20 = (f32[56,128]{1,0:T(8,128)S(1)}, f32[56,128]{1,0:T(8,128)S(1)}, u32[]{:S(2)}, u32[]{:S(2)}) collective-permute-start(f32[56,128]{1,0:T(8,128)S(1)} %add_add_fusion.refs_0_), channel_id=1, source_target_pairs={{0,16},{8,24},{16,0},{24,8},{1,17},{9,25},{17,1},{25,9},{2,18},{10... | collective-permute-start | bytes 86024 | tf_op jit(solution)/shard_map/ppermute | solution.py:482
  55.3 4.4 %collective-permute-start.19 = (f32[56,128]{1,0:T(8,128)S(1)}, f32[56,128]{1,0:T(8,128)S(1)}, u32[]{:S(2)}, u32[]{:S(2)}) collective-permute-start(f32[56,128]{1,0:T(8,128)S(1)} %add_add_fusion.refs_0_), channel_id=1, source_target_pairs={{0,8},{8,0},{16,24},{24,16},{1,9},{9,1},{17,25},{25,17},{2,10},{10... | collective-permute-start | bytes 86024 | tf_op jit(solution)/shard_map/ppermute | solution.py:482

commit v5 on v4

--- a/solution.py
+++ b/solution.py
@@ -122,14 +122,16 @@
     begin, ends = fold_lanes(per, width)
     if parts == 1:
         packed = fold_ref[REACH].astype(F32)
-        rows = [fold_ref[row] for row in range(REACH)]
+        for depth in range(REACH):
+            lines_of[depth] = flip_lanes(fold_ref[REACH - 1 - depth], width, width - 1)
     else:
         held = fold_ref[0:head, :].astype(F32)[: channels // parts]
         pieces = [pltpu.roll(held, (begin - part * (width // parts)) % width, 1) for part in range(parts)]
         packed = jnp.concatenate(pieces, axis=0)
-        rows = [fold_ref[head + row * channels : head + (row + 1) * channels, :] for row in range(REACH)]
-    for depth in range(REACH):
-        lines_of[depth] = flip_lanes(rows[REACH - 1 - depth], width, width - 1)
+        flipped = flip_lanes(fold_ref[head : head + REACH * channels, :], width, width - 1)
+        for depth in range(REACH):
+            row = REACH - 1 - depth
+            lines_of[depth] = flipped[row * channels : (row + 1) * channels]
     return flip_lanes((packed * ends).astype(BF16), width, 2 * SPAN * per - SPAN - 1)
 
 
@@ -188,16 +190,22 @@
 def inner_body(channels, rows, width):
     def body(snap_ref, weight_ref, out_ref, spread_ref, lines):
         lines[...] = snap_ref[...].astype(F32)
+        weights = weight_ref[...].astype(BF16)
+        row = lax.broadcasted_iota(jnp.int32, (128, 2 * width), 0)
+        second = jnp.where(lax.broadcasted_iota(jnp.int32, (128, 2 * width), 1) < width, 0, 1)
+        for tap in range(0, TAPS * TAPS, 2):
+            pick = jnp.where(row == second + tap, 1.0, 0.0).astype(BF16)
+            pair = jnp.dot(weights, pick, preferred_element_type=F32)
+            spread_ref[tap] = pair[:, :width]
+            if tap + 1 < TAPS * TAPS:
+                spread_ref[tap + 1] = pair[:, width:]
         lane = lanes_of((8, width))
 
         def step(block, carry):
             span = pl.ds(block * 8, 8)
-            weights = weight_ref[span, :]
             sums = [None] * rows
             for col in range(TAPS):
-                taps = [jnp.broadcast_to(weights[:, a * TAPS + col : a * TAPS + col + 1], (8, width)) for a in range(TAPS)]
-                for a in range(TAPS):
-                    spread_ref[a * TAPS + col, span, :] = taps[a]
+                taps = [spread_ref[a * TAPS + col, span, :] for a in range(TAPS)]
                 for source in range(rows):
                     moved = shifted(lines[source, span, :], 0.0, col - REACH, lane, width)
                     for a in range(TAPS):
@@ -557,6 +565,7 @@
         "inner",
     )(lines, weights)
     packs, fold = packs_call(place, lines, off, on)
+    late_cotangent, _ = lax.optimization_barrier((jnp.swapaxes(cotangent, 0, 1), fold))
     upstream, up_own, *early_sends = call(
         cotangent_body(levels, channels, height, width),
         [shaped(total_channels, cells), block] + [shaped(2 * height, channels, width)] * (levels - 1),
@@ -564,8 +573,7 @@
         [pltpu.VMEM((height, total_channels, width), F32)],
         1.0,
         "cotangent",
-    )(place, lines, jnp.swapaxes(cotangent, 0, 1), ocean_mask)
-    early_sends, fold = lax.optimization_barrier((early_sends, fold))
+    )(place, lines, late_cotangent, ocean_mask)
     others = level_swap(early_sends)
     fold = mirror(fold)
     part = call(
@@ -585,7 +593,8 @@
         "fold",
     )(place, part, fold, spread)
     convs = [conv_own] + level_swap(conv_sends)
-    convs, others = lax.optimization_barrier((convs, others))
+    convs, others = lax.optimization_barrier((convs[::-1], others))
+    convs = convs[::-1]
     columns = call(
         columns_body(channels, rows, width),
         shaped(TAPS, rows + REACH, channels, width, dtype=F32),
@@ -611,7 +620,8 @@
         1.0,
         "finish",
     )(place, lines, ocean_mask, projected, *others)
-    result, d_blocks = lax.optimization_barrier((result, d_blocks))
+    result, d_blocks = lax.optimization_barrier((result, d_blocks[::-1]))
+    d_blocks = d_blocks[::-1]
     d_lines, off, on = call(
         gather_body(levels, channels, rows, width),
         [shaped(rows, channels, width), pack, pack],

time: 61.2 us -> 60.1 us (0.982)
  waiting for transfers between devices: 7.12 us -> 5.89 us
  starting transfers between devices: 27.9 us -> 28.7 us
    ppermute x22, waiting for transfers between devices: 7.12 us -> 5.89 us  [across(): lax.ppermute(value, axis, [(i, target(i) % count) for i in range(count)])]
    ppermute x22, starting transfers between devices: 27.9 us -> 28.7 us  [across(): lax.ppermute(value, axis, [(i, target(i) % count) for i in range(count)])]
  transfers between devices with their start and end apart: 22 -> 22, of which waited for: 10 -> 12; matrix products, arithmetic and copies ran while one was open for 1% -> 1% of each run, Pallas kernels for 26% -> 26%
where the time goes in v5:
time: 60.1 us; the launch traced here: 60 us
  starting transfers between devices  28.7 us (48%)
  Pallas kernels  23 us (38%)
  waiting for transfers between devices  5.89 us (10%)
  local copies, waits for them, and re-layouts  1.41 us (2%)
  between operations  0.88 us (1%)
    ppermute x22, starting transfers between devices, across(): lax.ppermute(value, axis, [(i, target(i) % count) for i in range(count)])  28.7 us
    ppermute x22, waiting for transfers between devices, across(): lax.ppermute(value, axis, [(i, target(i) % count) for i in range(count)])  5.89 us
    pallas_call x1, Pallas kernels, shards(): call(cell_body(levels, channels, height, width, 512), [shaped(total_chann...  4.08 us
    pallas_call x1, Pallas kernels, shards(): call(adjoint_body(levels, channels, rows, width), shaped(rows, channels,...  3.68 us
    pallas_call x1, Pallas kernels, shards(): call(kernel_body(levels, channels, rows, width), shaped(TAP_ROWS, 128, dt...  2.66 us
    pallas_call x1, Pallas kernels, shards(): call(inner_body(channels, rows, width), [shaped(rows, channels, width, dt...  2.35 us
    pallas_call x1, Pallas kernels, shards(): call(columns_body(channels, rows, width), shaped(TAPS, rows + REACH, chan...  1.42 us
    pallas_call x1, Pallas kernels, shards(): call(rims_body(channels, rows, width), shaped(rows, channels, width, dtyp...  1.38 us
  transfers between devices with their start and end apart: 22, of which 12 were waited for; matrix products, arithmetic and copies ran while one was open for 1% of the time, Pallas kernels for 26%

profile of v5, /device:TPU:0, one launch (start us, length us, event | category | flops | bytes accessed | tf_op | source)
XLA Modules:
  0.0 60.0 jit_solution(6177133763102735477)
XLA Ops:
  0.7 1.0 %copy-done.4 = bf16[96,12,128]{2,0,1:T(8,128)(2,1)S(1)} copy-done((bf16[96,12,128]{2,0,1:T(8,128)(2,1)S(1)}, bf16[96,12,128]{2,0,1:T(8,128)(2,1)}, u32[]{:S(2)}) %copy-start.4) | copy-done | bytes 294936
  1.7 0.7 %prepare.1 = (bf16[1,96,128]{2,1,0:T(8,128)(2,1)S(1)}, bf16[1,96,128]{2,1,0:T(8,128)(2,1)S(1)}) custom-call(s32[2]{0:T(128)S(1)} %pad_add_fusion.place_ref, bf16[12,96,128]{2,1,0:T(8,128)(2,1)S(1)} %bitcast.8), custom_call_target="tpu_custom_call" | custom-call | flops 1100000000 | tf_op jit(solution)/shard_map/prepare/pallas_call | solution.py:557
  2.4 4.6 %collective-permute-start = (bf16[1,96,128]{2,1,0:T(8,128)(2,1)S(1)}, bf16[1,96,128]{2,1,0:T(8,128)(2,1)S(1)}, u32[]{:S(2)}, u32[]{:S(2)}) collective-permute-start(bf16[1,96,128]{2,1,0:T(8,128)(2,1)S(1)} %get-tuple-element.49), channel_id=1, source_target_pairs={{0,7},{1,2},{2,1},{3,4},{4,3},{5,6},{6,5},{7,0},{8,15},{9,10},{10,... | collective-permute-start | bytes 73736 | tf_op jit(solution)/shard_map/ppermute | solution.py:490
  7.2 2.4 %inner.1 = (f32[12,96,128]{2,1,0:T(8,128)S(1)}, f32[49,96,128]{2,1,0:T(8,128)S(1)}) custom-call(bf16[12,96,128]{2,1,0:T(8,128)(2,1)S(1)} %bitcast.9, f32[96,128]{1,0:T(8,128)S(1)} %pad_convert_fusion.weight_ref), custom_call_target="tpu_custom_call" | custom-call | flops 3300000000 | tf_op jit(solution)/shard_map/inner/pallas_call | solution.py:559
  9.9 0.6 %packs.2 = (f32[1,96,128]{2,1,0:T(8,128)S(1)}, bf16[320,128]{1,0:T(8,128)(2,1)S(1)}) custom-call(s32[2]{0:T(128)S(1)} %pad_add_fusion.place_ref, bf16[12,96,128]{2,1,0:T(8,128)(2,1)S(1)} %bitcast.10, bf16[1,96,128]{2,1,0:T(8,128)(2,1)S(1)} %collective-permute-done.off_ref, bf16[1,96,128]{2,1,0:T(8,128)(2,1)S(1)} %collective-permute-done.1.on_ref), custom_call_target="tpu_custom_call" | custom-call | flops 660000000 | tf_op jit(solution)/shard_map/packs/pallas_call | solution.py:567
  10.5 2.2 %collective-permute-start.2 = (bf16[320,128]{1,0:T(8,128)(2,1)S(1)}, bf16[320,128]{1,0:T(8,128)(2,1)S(1)}, u32[]{:S(2)}, u32[]{:S(2)}) collective-permute-start(bf16[320,128]{1,0:T(8,128)(2,1)S(1)} %get-tuple-element.53), channel_id=1, source_target_pairs={{0,7},{1,6},{2,5},{3,4},{4,3},{5,2},{6,1},{7,0},{8,15},{9,14},{10,... | collective-permute-start | bytes 245768 | tf_op jit(solution)/shard_map/ppermute | solution.py:490
  12.7 0.7 %cotangent.1 = (bf16[384,384]{1,0:T(8,128)(2,1)S(1)}, bf16[3,96,128]{2,1,0:T(8,128)(2,1)S(1)}, bf16[6,96,128]{2,1,0:T(8,128)(2,1)S(1)}, bf16[6,96,128]{2,1,0:T(8,128)(2,1)S(1)}, bf16[6,96,128]{2,1,0:T(8,128)(2,1)S(1)}) custom-call(s32[2]{0:T(128)S(1)} %pad_add_fusion.place_ref, bf16[12,96,128]{2,1,0:T(8,128)(2,1)S(1)} %bitcast.11, ...), custom_call_target="tpu_custom_call" | custom-call | flops 1100000000 | tf_op jit(solution)/shard_map/cotangent/pallas_call | solution.py:569
  13.4 1.6 %collective-permute-start.6 = (bf16[6,96,128]{2,1,0:T(8,128)(2,1)S(1)}, bf16[6,96,128]{2,1,0:T(8,128)(2,1)S(1)}, u32[]{:S(2)}, u32[]{:S(2)}) collective-permute-start(bf16[6,96,128]{2,1,0:T(8,128)(2,1)S(1)} %get-tuple-element.59), channel_id=1, source_target_pairs={{0,8},{8,0},{16,24},{24,16},{1,9},{9,1},{17,25},{25,17},{2,10},{10... | collective-permute-start | bytes 442376 | tf_op jit(solution)/shard_map/ppermute | solution.py:490
  14.9 1.5 %collective-permute-start.7 = (bf16[6,96,128]{2,1,0:T(8,128)(2,1)S(1)}, bf16[6,96,128]{2,1,0:T(8,128)(2,1)S(1)}, u32[]{:S(2)}, u32[]{:S(2)}) collective-permute-start(bf16[6,96,128]{2,1,0:T(8,128)(2,1)S(1)} %get-tuple-element.60), channel_id=1, source_target_pairs={{0,16},{8,24},{16,0},{24,8},{1,17},{9,25},{17,1},{25,9},{2,18},{10... | collective-permute-start | bytes 442376 | tf_op jit(solution)/shard_map/ppermute | solution.py:490
  16.9 1.4 %rims.1.part_ref = f32[12,96,128]{2,1,0:T(8,128)S(1)} custom-call(f32[12,96,128]{2,1,0:T(8,128)S(1)} %get-tuple-element.48.inner_ref, f32[1,96,128]{2,1,0:T(8,128)S(1)} %get-tuple-element.51.packs_ref, f32[49,96,128]{2,1,0:T(8,128)S(1)} %get-tuple-element.52.spread_ref), custom_call_target="tpu_custom_call" | custom-call | flops 2200000000 | tf_op jit(solution)/shard_map/rims/pallas_call | solution.py:579
  18.3 1.3 %fold.1 = (bf16[3,96,128]{2,1,0:T(8,128)(2,1)S(1)}, bf16[3,96,128]{2,1,0:T(8,128)(2,1)S(1)}, bf16[3,96,128]{2,1,0:T(8,128)(2,1)S(1)}, bf16[3,96,128]{2,1,0:T(8,128)(2,1)S(1)}) custom-call(s32[2]{0:T(128)S(1)} %pad_add_fusion.place_ref, f32[12,96,128]{2,1,0:T(8,128)S(1)} %rims.1.part_ref, bf16[320,128]{1,0:T(8,128)(2,1)S(1)} %collective-permute-done.2.fold_ref, ...), custom_call_target="tpu_custom_call" | custom-call | flops 1320000000 | tf_op jit(solution)/shard_map/fold/pallas_call | solution.py:587
  19.7 2.5 %collective-permute-start.3 = (bf16[3,96,128]{2,1,0:T(8,128)(2,1)S(1)}, bf16[3,96,128]{2,1,0:T(8,128)(2,1)S(1)}, u32[]{:S(2)}, u32[]{:S(2)}) collective-permute-start(bf16[3,96,128]{2,1,0:T(8,128)(2,1)S(1)} %get-tuple-element.54), channel_id=1, source_target_pairs={{0,24},{8,16},{16,8},{24,0},{1,25},{9,17},{17,9},{25,1},{2,26},{10... | collective-permute-start | bytes 221192 | tf_op jit(solution)/shard_map/ppermute | solution.py:490
  23.2 1.4 %columns.1.columns_ref = f32[7,15,96,128]{3,2,1,0:T(8,128)S(1)} custom-call(bf16[12,96,128]{2,1,0:T(8,128)(2,1)S(1)} %bitcast.12, f32[1,96,128]{2,1,0:T(8,128)S(1)} %get-tuple-element.51.packs_ref, bf16[320,128]{1,0:T(8,128)(2,1)S(1)} %collective-permute-done.2.fold_ref), custom_call_target="tpu_custom_call" | custom-call | flops 2200000000 | tf_op jit(solution)/shard_map/columns/pallas_call | solution.py:598
  24.7 1.1 %collective-permute-done.3.refs_3_ = bf16[3,96,128]{2,1,0:T(8,128)(2,1)S(1)} collective-permute-done((bf16[3,96,128]{2,1,0:T(8,128)(2,1)S(1)}, bf16[3,96,128]{2,1,0:T(8,128)(2,1)S(1)}, u32[]{:S(2)}, u32[]{:S(2)}) %collective-permute-start.3) | collective-permute-done | bytes 73760 | tf_op jit(solution)/shard_map/ppermute | solution.py:490
  25.7 0.8 %collective-permute-done.4.refs_2_ = bf16[3,96,128]{2,1,0:T(8,128)(2,1)S(1)} collective-permute-done((bf16[3,96,128]{2,1,0:T(8,128)(2,1)S(1)}, bf16[3,96,128]{2,1,0:T(8,128)(2,1)S(1)}, u32[]{:S(2)}, u32[]{:S(2)}) %collective-permute-start.4) | collective-permute-done | bytes 73760 | tf_op jit(solution)/shard_map/ppermute | solution.py:490
  27.0 4.1 %cells.1 = (f32[384,384]{1,0:T(8,128)S(1)}, bf16[3,96,128]{2,1,0:T(8,128)(2,1)S(1)}, bf16[3,96,128]{2,1,0:T(8,128)(2,1)S(1)}, bf16[3,96,128]{2,1,0:T(8,128)(2,1)S(1)}, bf16[3,96,128]{2,1,0:T(8,128)(2,1)S(1)}) custom-call(s32[2]{0:T(128)S(1)} %pad_add_fusion.place_ref, bf16[3,96,128]{2,1,0:T(8,128)(2,1)S(1)} %get-tuple-element.62.refs_0_, ...), custom_call_target="tpu_custom_call" | custom-call | flops 5500000256 | tf_op jit(solution)/shard_map/cells/pallas_call | solution.py:606
  31.1 1.6 %collective-permute-start.9 = (bf16[3,96,128]{2,1,0:T(8,128)(2,1)S(1)}, bf16[3,96,128]{2,1,0:T(8,128)(2,1)S(1)}, u32[]{:S(2)}, u32[]{:S(2)}) collective-permute-start(bf16[3,96,128]{2,1,0:T(8,128)(2,1)S(1)} %get-tuple-element.71), channel_id=1, source_target_pairs={{0,24},{8,16},{16,8},{24,0},{1,25},{9,17},{17,9},{25,1},{2,26},{10... | collective-permute-start | bytes 221192 | tf_op jit(solution)/shard_map/ppermute | solution.py:490
  33.2 1.5 %collective-permute-start.11 = (bf16[3,96,128]{2,1,0:T(8,128)(2,1)S(1)}, bf16[3,96,128]{2,1,0:T(8,128)(2,1)S(1)}, u32[]{:S(2)}, u32[]{:S(2)}) collective-permute-start(bf16[3,96,128]{2,1,0:T(8,128)(2,1)S(1)} %get-tuple-element.73), channel_id=1, source_target_pairs={{0,8},{8,0},{16,24},{24,16},{1,9},{9,1},{17,25},{25,17},{2,10},{10... | collective-permute-start | bytes 221192 | tf_op jit(solution)/shard_map/ppermute | solution.py:490
  34.7 1.3 %finish.1 = bf16[3,384,128]{2,1,0:T(8,128)(2,1)} custom-call(s32[2]{0:T(128)S(1)} %pad_add_fusion.place_ref, bf16[12,96,128]{2,1,0:T(8,128)(2,1)S(1)} %bitcast.13, s32[3,128]{1,0:T(4,128)S(1)} %copy-done.6, f32[384,384]{1,0:T(8,128)S(1)} %get-tuple-element.67.projected_ref, bf16[6,96,128]{2,1,0:T(8,128)(2,1)S(1)} %collective-permute-done.6.refs_0_.refs_1_, ...), custom_call_target="tpu_custom_call" | custom-call | flops 1100000000 | tf_op jit(solution)/shard_map/finish/pallas_call | solution.py:615
  36.5 0.8 %collective-permute-done.10.refs_2_ = bf16[3,96,128]{2,1,0:T(8,128)(2,1)S(1)} collective-permute-done((bf16[3,96,128]{2,1,0:T(8,128)(2,1)S(1)}, bf16[3,96,128]{2,1,0:T(8,128)(2,1)S(1)}, u32[]{:S(2)}, u32[]{:S(2)}) %collective-permute-start.10) | collective-permute-done | bytes 73760 | tf_op jit(solution)/shard_map/ppermute | solution.py:490
  37.5 0.8 %regroup.1 = (bf16[12,96,128]{2,1,0:T(8,128)(2,1)S(1)}, bf16[1,96,128]{2,1,0:T(8,128)(2,1)S(1)}, bf16[1,96,128]{2,1,0:T(8,128)(2,1)S(1)}) custom-call(s32[2]{0:T(128)S(1)} %pad_add_fusion.place_ref, bf16[3,96,128]{2,1,0:T(8,128)(2,1)S(1)} %get-tuple-element.76.refs_0_, bf16[3,96,128]{2,1,0:T(8,128)(2,1)S(1)} %collective-permute-done.11.refs_1_, ...), custom_call_target="tpu_custom_call" | custom-call | flops 880000000 | tf_op jit(solution)/shard_map/regroup/pallas_call | solution.py:625
  38.4 2.3 %collective-permute-start.12 = (bf16[1,96,128]{2,1,0:T(8,128)(2,1)S(1)}, bf16[1,96,128]{2,1,0:T(8,128)(2,1)S(1)}, u32[]{:S(2)}, u32[]{:S(2)}) collective-permute-start(bf16[1,96,128]{2,1,0:T(8,128)(2,1)S(1)} %get-tuple-element.82), channel_id=1, source_target_pairs={{0,7},{1,2},{2,1},{3,4},{4,3},{5,6},{6,5},{7,0},{8,15},{9,10},{10,... | collective-permute-start | bytes 73736 | tf_op jit(solution)/shard_map/ppermute | solution.py:490
  40.7 2.7 %kernel_terms.1 = f32[56,128]{1,0:T(8,128)S(1)} custom-call(s32[2]{0:T(128)S(1)} %pad_add_fusion.place_ref, f32[7,15,96,128]{3,2,1,0:T(8,128)S(1)} %columns.1.columns_ref, bf16[3,96,128]{2,1,0:T(8,128)(2,1)S(1)} %get-tuple-element.76.refs_0_, bf16[3,96,128]{2,1,0:T(8,128)(2,1)S(1)} %collective-permute-done.11.refs_1_, ...), custom_call_target="tpu_custom_call" | custom-call | flops 11000000 | tf_op jit(solution)/shard_map/kernel_terms/pallas_call | solution.py:634
  43.5 0.6 %packs.3 = (f32[1,96,128]{2,1,0:T(8,128)S(1)}, bf16[320,128]{1,0:T(8,128)(2,1)S(1)}) custom-call(s32[2]{0:T(128)S(1)} %pad_add_fusion.place_ref, bf16[12,96,128]{2,1,0:T(8,128)(2,1)S(1)} %get-tuple-element.80.lines_ref.d_ref, bf16[1,96,128]{2,1,0:T(8,128)(2,1)S(1)} %collective-permute-done.12.off_ref, bf16[1,96,128]{2,1,0:T(8,128)(2,1)S(1)} %collective-permute-done.13.on_ref), custom_call_target="tpu_custom_call" | custom-call | flops 660000000 | tf_op jit(solution)/shard_map/packs/pallas_call | solution.py:643
  44.6 1.4 %collective-permute-start.18 = (f32[56,128]{1,0:T(8,128)S(1)}, f32[56,128]{1,0:T(8,128)S(1)}, u32[]{:S(2)}, u32[]{:S(2)}) collective-permute-start(f32[56,128]{1,0:T(8,128)S(1)} %add.23), channel_id=1, source_target_pairs={{0,6},{1,7},{2,4},{3,5},{4,2},{5,3},{6,0},{7,1},{8,14},{9,15},{10,... | collective-permute-start | bytes 86024 | tf_op jit(solution)/shard_map/ppermute | solution.py:490
  46.0 3.0 %collective-permute-start.16 = (f32[56,128]{1,0:T(8,128)S(1)}, f32[56,128]{1,0:T(8,128)S(1)}, u32[]{:S(2)}, u32[]{:S(2)}) collective-permute-start(f32[56,128]{1,0:T(8,128)S(1)} %add.23), channel_id=1, source_target_pairs={{0,2},{1,3},{2,0},{3,1},{4,6},{5,7},{6,4},{7,5},{8,10},{9,11},{10,... | collective-permute-start | bytes 86024 | tf_op jit(solution)/shard_map/ppermute | solution.py:490
  49.0 1.0 %collective-permute-start.15 = (bf16[320,128]{1,0:T(8,128)(2,1)S(1)}, bf16[320,128]{1,0:T(8,128)(2,1)S(1)}, u32[]{:S(2)}, u32[]{:S(2)}) collective-permute-start(bf16[320,128]{1,0:T(8,128)(2,1)S(1)} %get-tuple-element.87), channel_id=1, source_target_pairs={{0,7},{1,6},{2,5},{3,4},{4,3},{5,2},{6,1},{7,0},{8,15},{9,14},{10,... | collective-permute-start | bytes 245768 | tf_op jit(solution)/shard_map/ppermute | solution.py:490
  50.3 1.0 %collective-permute-done.17 = f32[56,128]{1,0:T(8,128)S(1)} collective-permute-done((f32[56,128]{1,0:T(8,128)S(1)}, f32[56,128]{1,0:T(8,128)S(1)}, u32[]{:S(2)}, u32[]{:S(2)}) %collective-permute-start.17) | collective-permute-done | bytes 28704 | tf_op jit(solution)/shard_map/ppermute | solution.py:490
  51.4 2.2 %collective-permute-start.21 = (f32[56,128]{1,0:T(8,128)S(1)}, f32[56,128]{1,0:T(8,128)S(1)}, u32[]{:S(2)}, u32[]{:S(2)}) collective-permute-start(f32[56,128]{1,0:T(8,128)S(1)} %add_add_fusion.refs_0_), channel_id=1, source_target_pairs={{0,24},{8,16},{16,8},{24,0},{1,25},{9,17},{17,9},{25,1},{2,26},{10... | collective-permute-start | bytes 86024 | tf_op jit(solution)/shard_map/ppermute | solution.py:490
  54.1 0.9 %collective-permute-start.19 = (f32[56,128]{1,0:T(8,128)S(1)}, f32[56,128]{1,0:T(8,128)S(1)}, u32[]{:S(2)}, u32[]{:S(2)}) collective-permute-start(f32[56,128]{1,0:T(8,128)S(1)} %add_add_fusion.refs_0_), channel_id=1, source_target_pairs={{0,8},{8,0},{16,24},{24,16},{1,9},{9,1},{17,25},{25,17},{2,10},{10... | collective-permute-start | bytes 86024 | tf_op jit(solution)/shard_map/ppermute | solution.py:490
  55.0 3.7 %adjoint.1 = bf16[12,96,128]{2,1,0:T(8,128)(2,1)} custom-call(s32[2]{0:T(128)S(1)} %pad_add_fusion.place_ref, bf16[12,96,128]{2,1,0:T(8,128)(2,1)S(1)} %get-tuple-element.80.lines_ref.d_ref, f32[1,96,128]{2,1,0:T(8,128)S(1)} %get-tuple-element.84.packs_ref, bf16[320,128]{1,0:T(8,128)(2,1)S(1)} %collective-permute-done.15.fold_ref, ...), custom_call_target="tpu_custom_call" | custom-call | flops 4400000000 | tf_op jit(solution)/shard_map/adjoint/pallas_call | solution.py:647
  58.7 1.3 %assemble.1 = f32[49,384]{1,0:T(8,128)} custom-call(s32[2]{0:T(128)S(1)} %pad_add_fusion.place_ref, f32[56,128]{1,0:T(8,128)S(1)} %add_add_fusion.refs_0_, f32[56,128]{1,0:T(8,128)S(1)} %collective-permute-done.19.refs_1_, f32[56,128]{1,0:T(8,128)S(1)} %collective-permute-done.20.refs_2_, f32[56,128]{1,0:T(8,128)S(1)} %collective-permute-done.21.refs_3_), custom_call_target="tpu_custom_call" | custom-call | flops 880000000 | tf_op jit(solution)/shard_map/assemble/pallas_call | solution.py:657
  (52 shorter events, 5.4 us)
Async XLA Ops:
  0.6 6.3 %copy-start = (bf16[384,49]{0,1:T(8,128)(2,1)S(1)}, bf16[384,49]{0,1:T(8,128)(2,1)}, u32[]{:S(2)}) copy-start(bf16[384,49]{0,1:T(8,128)(2,1)} %param.11) | copy-start | bytes 112900
  0.7 1.0 %copy-start.4 = (bf16[96,12,128]{2,0,1:T(8,128)(2,1)S(1)}, bf16[96,12,128]{2,0,1:T(8,128)(2,1)}, u32[]{:S(2)}) copy-start(bf16[96,12,128]{2,0,1:T(8,128)(2,1)} %param.8) | copy-start | bytes 884740
  1.7 5.5 %copy-start.5 = (bf16[96,12,128]{2,0,1:T(8,128)(2,1)S(1)}, bf16[96,12,128]{2,0,1:T(8,128)(2,1)}, u32[]{:S(2)}) copy-start(bf16[96,12,128]{2,0,1:T(8,128)(2,1)} %param.8) | copy-start | bytes 884740
  2.4 7.4 %collective-permute-start = (bf16[1,96,128]{2,1,0:T(8,128)(2,1)S(1)}, bf16[1,96,128]{2,1,0:T(8,128)(2,1)S(1)}, u32[]{:S(2)}, u32[]{:S(2)}) collective-permute-start(bf16[1,96,128]{2,1,0:T(8,128)(2,1)S(1)} %get-tuple-element.49), channel_id=1, source_target_pairs={{0,7},{1,2},{2,1},{3,4},{4,3},{5,6},{6,5},{7,0},{8,15},{9,10},{10,... | collective-permute-start | bytes 73736 | tf_op jit(solution)/shard_map/ppermute | solution.py:490
  7.0 2.9 %collective-permute-start.1 = (bf16[1,96,128]{2,1,0:T(8,128)(2,1)S(1)}, bf16[1,96,128]{2,1,0:T(8,128)(2,1)S(1)}, u32[]{:S(2)}, u32[]{:S(2)}) collective-permute-start(bf16[1,96,128]{2,1,0:T(8,128)(2,1)S(1)} %get-tuple-element.50), channel_id=1, source_target_pairs={{0,1},{1,0},{2,3},{3,2},{4,5},{5,4},{6,7},{7,6},{8,9},{9,8},{10,11... | collective-permute-start | bytes 73736 | tf_op jit(solution)/shard_map/ppermute | solution.py:490
  7.2 2.4 %copy-start.7 = (f32[384]{0:T(512)S(1)}, f32[384]{0:T(512)}, u32[]{:S(2)}) copy-start(f32[384]{0:T(512)} %param.12) | copy-start | bytes 4612
  7.2 2.5 %copy-start.8 = (f32[384]{0:T(512)S(1)}, f32[384]{0:T(512)}, u32[]{:S(2)}) copy-start(f32[384]{0:T(512)} %param.13) | copy-start | bytes 4612
  9.6 3.1 %copy-start.3 = (bf16[384,3,128]{2,0,1:T(8,128)(2,1)S(1)}, bf16[384,3,128]{2,0,1:T(8,128)(2,1)}, u32[]{:S(2)}) copy-start(bf16[384,3,128]{2,0,1:T(8,128)(2,1)} %param.9) | copy-start | bytes 884740
  9.6 3.1 %copy-start.6 = (s32[3,128]{1,0:T(4,128)S(1)}, s32[3,128]{1,0:T(4,128)}, u32[]{:S(2)}) copy-start(s32[3,128]{1,0:T(4,128)} %mask_ref.3) | copy-start | bytes 4612
  10.5 7.8 %collective-permute-start.2 = (bf16[320,128]{1,0:T(8,128)(2,1)S(1)}, bf16[320,128]{1,0:T(8,128)(2,1)S(1)}, u32[]{:S(2)}, u32[]{:S(2)}) collective-permute-start(bf16[320,128]{1,0:T(8,128)(2,1)S(1)} %get-tuple-element.53), channel_id=1, source_target_pairs={{0,7},{1,6},{2,5},{3,4},{4,3},{5,2},{6,1},{7,0},{8,15},{9,14},{10,... | collective-permute-start | bytes 245768 | tf_op jit(solution)/shard_map/ppermute | solution.py:490
  13.4 9.3 %collective-permute-start.6 = (bf16[6,96,128]{2,1,0:T(8,128)(2,1)S(1)}, bf16[6,96,128]{2,1,0:T(8,128)(2,1)S(1)}, u32[]{:S(2)}, u32[]{:S(2)}) collective-permute-start(bf16[6,96,128]{2,1,0:T(8,128)(2,1)S(1)} %get-tuple-element.59), channel_id=1, source_target_pairs={{0,8},{8,0},{16,24},{24,16},{1,9},{9,1},{17,25},{25,17},{2,10},{10... | collective-permute-start | bytes 442376 | tf_op jit(solution)/shard_map/ppermute | solution.py:490
  14.9 9.7 %collective-permute-start.7 = (bf16[6,96,128]{2,1,0:T(8,128)(2,1)S(1)}, bf16[6,96,128]{2,1,0:T(8,128)(2,1)S(1)}, u32[]{:S(2)}, u32[]{:S(2)}) collective-permute-start(bf16[6,96,128]{2,1,0:T(8,128)(2,1)S(1)} %get-tuple-element.60), channel_id=1, source_target_pairs={{0,16},{8,24},{16,0},{24,8},{1,17},{9,25},{17,1},{25,9},{2,18},{10... | collective-permute-start | bytes 442376 | tf_op jit(solution)/shard_map/ppermute | solution.py:490
  16.4 8.2 %collective-permute-start.8 = (bf16[6,96,128]{2,1,0:T(8,128)(2,1)S(1)}, bf16[6,96,128]{2,1,0:T(8,128)(2,1)S(1)}, u32[]{:S(2)}, u32[]{:S(2)}) collective-permute-start(bf16[6,96,128]{2,1,0:T(8,128)(2,1)S(1)} %get-tuple-element.61), channel_id=1, source_target_pairs={{0,24},{8,16},{16,8},{24,0},{1,25},{9,17},{17,9},{25,1},{2,26},{10... | collective-permute-start | bytes 442376 | tf_op jit(solution)/shard_map/ppermute | solution.py:490
  19.7 6.1 %collective-permute-start.3 = (bf16[3,96,128]{2,1,0:T(8,128)(2,1)S(1)}, bf16[3,96,128]{2,1,0:T(8,128)(2,1)S(1)}, u32[]{:S(2)}, u32[]{:S(2)}) collective-permute-start(bf16[3,96,128]{2,1,0:T(8,128)(2,1)S(1)} %get-tuple-element.54), channel_id=1, source_target_pairs={{0,24},{8,16},{16,8},{24,0},{1,25},{9,17},{17,9},{25,1},{2,26},{10... | collective-permute-start | bytes 221192 | tf_op jit(solution)/shard_map/ppermute | solution.py:490
  22.2 4.4 %collective-permute-start.4 = (bf16[3,96,128]{2,1,0:T(8,128)(2,1)S(1)}, bf16[3,96,128]{2,1,0:T(8,128)(2,1)S(1)}, u32[]{:S(2)}, u32[]{:S(2)}) collective-permute-start(bf16[3,96,128]{2,1,0:T(8,128)(2,1)S(1)} %get-tuple-element.55), channel_id=1, source_target_pairs={{0,16},{8,24},{16,0},{24,8},{1,17},{9,25},{17,1},{25,9},{2,18},{10... | collective-permute-start | bytes 221192 | tf_op jit(solution)/shard_map/ppermute | solution.py:490
  22.7 4.4 %copy-start.1 = (bf16[384,1536]{1,0:T(8,128)(2,1)S(1)}, bf16[384,1536]{1,0:T(8,128)(2,1)}, u32[]{:S(2)}) copy-start(bf16[384,1536]{1,0:T(8,128)(2,1)} %refs_7_.1) | copy-start | bytes 3538948
  22.7 4.4 %copy-start.2 = (bf16[1536,384]{1,0:T(8,128)(2,1)S(1)}, bf16[1536,384]{1,0:T(8,128)(2,1)}, u32[]{:S(2)}) copy-start(bf16[1536,384]{1,0:T(8,128)(2,1)} %refs_8_.1) | copy-start | bytes 3538948
  22.7 4.4 %collective-permute-start.5 = (bf16[3,96,128]{2,1,0:T(8,128)(2,1)S(1)}, bf16[3,96,128]{2,1,0:T(8,128)(2,1)S(1)}, u32[]{:S(2)}, u32[]{:S(2)}) collective-permute-start(bf16[3,96,128]{2,1,0:T(8,128)(2,1)S(1)} %get-tuple-element.56), channel_id=1, source_target_pairs={{0,8},{8,0},{16,24},{24,16},{1,9},{9,1},{17,25},{25,17},{2,10},{10... | collective-permute-start | bytes 221192 | tf_op jit(solution)/shard_map/ppermute | solution.py:490
  31.1 5.3 %collective-permute-start.9 = (bf16[3,96,128]{2,1,0:T(8,128)(2,1)S(1)}, bf16[3,96,128]{2,1,0:T(8,128)(2,1)S(1)}, u32[]{:S(2)}, u32[]{:S(2)}) collective-permute-start(bf16[3,96,128]{2,1,0:T(8,128)(2,1)S(1)} %get-tuple-element.71), channel_id=1, source_target_pairs={{0,24},{8,16},{16,8},{24,0},{1,25},{9,17},{17,9},{25,1},{2,26},{10... | collective-permute-start | bytes 221192 | tf_op jit(solution)/shard_map/ppermute | solution.py:490
  32.7 4.5 %collective-permute-start.10 = (bf16[3,96,128]{2,1,0:T(8,128)(2,1)S(1)}, bf16[3,96,128]{2,1,0:T(8,128)(2,1)S(1)}, u32[]{:S(2)}, u32[]{:S(2)}) collective-permute-start(bf16[3,96,128]{2,1,0:T(8,128)(2,1)S(1)} %get-tuple-element.72), channel_id=1, source_target_pairs={{0,16},{8,24},{16,0},{24,8},{1,17},{9,25},{17,1},{25,9},{2,18},{10... | collective-permute-start | bytes 221192 | tf_op jit(solution)/shard_map/ppermute | solution.py:490
  33.2 4.4 %collective-permute-start.11 = (bf16[3,96,128]{2,1,0:T(8,128)(2,1)S(1)}, bf16[3,96,128]{2,1,0:T(8,128)(2,1)S(1)}, u32[]{:S(2)}, u32[]{:S(2)}) collective-permute-start(bf16[3,96,128]{2,1,0:T(8,128)(2,1)S(1)} %get-tuple-element.73), channel_id=1, source_target_pairs={{0,8},{8,0},{16,24},{24,16},{1,9},{9,1},{17,25},{25,17},{2,10},{10... | collective-permute-start | bytes 221192 | tf_op jit(solution)/shard_map/ppermute | solution.py:490
  38.3 5.1 %collective-permute-start.13 = (bf16[1,96,128]{2,1,0:T(8,128)(2,1)S(1)}, bf16[1,96,128]{2,1,0:T(8,128)(2,1)S(1)}, u32[]{:S(2)}, u32[]{:S(2)}) collective-permute-start(bf16[1,96,128]{2,1,0:T(8,128)(2,1)S(1)} %get-tuple-element.83), channel_id=1, source_target_pairs={{0,1},{1,0},{2,3},{3,2},{4,5},{5,4},{6,7},{7,6},{8,9},{9,8},{10,11... | collective-permute-start | bytes 73736 | tf_op jit(solution)/shard_map/ppermute | solution.py:490
  38.4 5.1 %collective-permute-start.12 = (bf16[1,96,128]{2,1,0:T(8,128)(2,1)S(1)}, bf16[1,96,128]{2,1,0:T(8,128)(2,1)S(1)}, u32[]{:S(2)}, u32[]{:S(2)}) collective-permute-start(bf16[1,96,128]{2,1,0:T(8,128)(2,1)S(1)} %get-tuple-element.82), channel_id=1, source_target_pairs={{0,7},{1,2},{2,1},{3,4},{4,3},{5,6},{6,5},{7,0},{8,15},{9,10},{10,... | collective-permute-start | bytes 73736 | tf_op jit(solution)/shard_map/ppermute | solution.py:490
  43.3 1.2 %collective-permute-start.14 = (f32[56,128]{1,0:T(8,128)S(1)}, f32[56,128]{1,0:T(8,128)S(1)}, u32[]{:S(2)}, u32[]{:S(2)}) collective-permute-start(f32[56,128]{1,0:T(8,128)S(1)} %kernel_terms.1), channel_id=1, source_target_pairs={{0,1},{1,0},{2,3},{3,2},{4,5},{5,4},{6,7},{7,6},{8,9},{9,8},{10,11... | collective-permute-start | bytes 86024 | tf_op jit(solution)/shard_map/ppermute | solution.py:490
  44.6 5.7 %collective-permute-start.18 = (f32[56,128]{1,0:T(8,128)S(1)}, f32[56,128]{1,0:T(8,128)S(1)}, u32[]{:S(2)}, u32[]{:S(2)}) collective-permute-start(f32[56,128]{1,0:T(8,128)S(1)} %add.23), channel_id=1, source_target_pairs={{0,6},{1,7},{2,4},{3,5},{4,2},{5,3},{6,0},{7,1},{8,14},{9,15},{10,... | collective-permute-start | bytes 86024 | tf_op jit(solution)/shard_map/ppermute | solution.py:490
  46.0 5.3 %collective-permute-start.17 = (f32[56,128]{1,0:T(8,128)S(1)}, f32[56,128]{1,0:T(8,128)S(1)}, u32[]{:S(2)}, u32[]{:S(2)}) collective-permute-start(f32[56,128]{1,0:T(8,128)S(1)} %add.23), channel_id=1, source_target_pairs={{0,4},{1,5},{2,6},{3,7},{4,0},{5,1},{6,2},{7,3},{8,12},{9,13},{10,... | collective-permute-start | bytes 86024 | tf_op jit(solution)/shard_map/ppermute | solution.py:490
  46.0 5.4 %collective-permute-start.16 = (f32[56,128]{1,0:T(8,128)S(1)}, f32[56,128]{1,0:T(8,128)S(1)}, u32[]{:S(2)}, u32[]{:S(2)}) collective-permute-start(f32[56,128]{1,0:T(8,128)S(1)} %add.23), channel_id=1, source_target_pairs={{0,2},{1,3},{2,0},{3,1},{4,6},{5,7},{6,4},{7,5},{8,10},{9,11},{10,... | collective-permute-start | bytes 86024 | tf_op jit(solution)/shard_map/ppermute | solution.py:490
  49.0 6.0 %collective-permute-start.15 = (bf16[320,128]{1,0:T(8,128)(2,1)S(1)}, bf16[320,128]{1,0:T(8,128)(2,1)S(1)}, u32[]{:S(2)}, u32[]{:S(2)}) collective-permute-start(bf16[320,128]{1,0:T(8,128)(2,1)S(1)} %get-tuple-element.87), channel_id=1, source_target_pairs={{0,7},{1,6},{2,5},{3,4},{4,3},{5,2},{6,1},{7,0},{8,15},{9,14},{10,... | collective-permute-start | bytes 245768 | tf_op jit(solution)/shard_map/ppermute | solution.py:490
  51.4 7.3 %collective-permute-start.21 = (f32[56,128]{1,0:T(8,128)S(1)}, f32[56,128]{1,0:T(8,128)S(1)}, u32[]{:S(2)}, u32[]{:S(2)}) collective-permute-start(f32[56,128]{1,0:T(8,128)S(1)} %add_add_fusion.refs_0_), channel_id=1, source_target_pairs={{0,24},{8,16},{16,8},{24,0},{1,25},{9,17},{17,9},{25,1},{2,26},{10... | collective-permute-start | bytes 86024 | tf_op jit(solution)/shard_map/ppermute | solution.py:490
  53.6 5.1 %collective-permute-start.20 = (f32[56,128]{1,0:T(8,128)S(1)}, f32[56,128]{1,0:T(8,128)S(1)}, u32[]{:S(2)}, u32[]{:S(2)}) collective-permute-start(f32[56,128]{1,0:T(8,128)S(1)} %add_add_fusion.refs_0_), channel_id=1, source_target_pairs={{0,16},{8,24},{16,0},{24,8},{1,17},{9,25},{17,1},{25,9},{2,18},{10... | collective-permute-start | bytes 86024 | tf_op jit(solution)/shard_map/ppermute | solution.py:490
  54.1 4.6 %collective-permute-start.19 = (f32[56,128]{1,0:T(8,128)S(1)}, f32[56,128]{1,0:T(8,128)S(1)}, u32[]{:S(2)}, u32[]{:S(2)}) collective-permute-start(f32[56,128]{1,0:T(8,128)S(1)} %add_add_fusion.refs_0_), channel_id=1, source_target_pairs={{0,8},{8,0},{16,24},{24,16},{1,9},{9,1},{17,25},{25,17},{2,10},{10... | collective-permute-start | bytes 86024 | tf_op jit(solution)/shard_map/ppermute | solution.py:490

commit v6 on v5

--- a/solution.py
+++ b/solution.py
@@ -135,9 +135,9 @@
     return flip_lanes((packed * ends).astype(BF16), width, 2 * SPAN * per - SPAN - 1)
 
 
-def each_block(channels, step):
+def each_block(channels, step, most=4):
     blocks = channels // 8
-    unroll = max(n for n in range(1, 5) if blocks % n == 0)
+    unroll = max(n for n in range(1, most + 1) if blocks % n == 0)
     lax.fori_loop(0, blocks, step, 0, unroll=unroll)
 
 
@@ -291,7 +291,7 @@
                 total[rows - 1 - up, span, :] = sums[up]
             return carry
 
-        each_block(channels, step)
+        each_block(channels, step, 12)
         total[0 : rows - REACH] = part_ref[0 : rows - REACH]
         for hop in range(levels):
             sends[hop][...] = total[pl.ds((lev ^ hop) * height, height)].astype(BF16)
@@ -479,7 +479,7 @@
                 total[row, span, :] = total[row, span, :] + sums[row]
             return carry
 
-        each_block(channels, step)
+        each_block(channels, step, 12)
         out_ref[...] = total[...].astype(BF16)
 
     return body
@@ -518,10 +518,13 @@
 
 def assemble_body(levels, channels):
     def body(place_ref, *refs):
-        parts, (out_ref, placed) = refs[:levels], refs[levels:]
+        parts, out_ref = refs[:levels], refs[levels]
+        placed = {}
         lev = place_ref[0]
         for hop in range(levels):
-            placed[lev ^ hop] = parts[hop][...]
+            value = parts[hop][...]
+            for level in range(levels):
+                placed[level] = value if hop == 0 else jnp.where(lev ^ hop == level, value, placed[level])
         for level in range(levels):
             out_ref[:, level * channels : (level + 1) * channels] = placed[level][: TAPS * TAPS, :channels]
 
@@ -658,7 +661,7 @@
         assemble_body(levels, channels),
         shaped(TAPS * TAPS, total_channels, dtype=F32),
         [SMEM] + [VMEM] * levels,
-        [pltpu.VMEM((levels, TAP_ROWS, 128), F32)],
+        [],
         0.8,
         "assemble",
     )(place, terms, *others)

time: 60.1 us -> 60 us (level)
  transfers between devices with their start and end apart: 22 -> 22, of which waited for: 12 -> 11; matrix products, arithmetic and copies ran while one was open for 1% -> 1% of each run, Pallas kernels for 26% -> 25%
where the time goes in v6:
time: 60 us; the launch traced here: 59.8 us
  starting transfers between devices  28.9 us (48%)
  Pallas kernels  22.6 us (38%)
  waiting for transfers between devices  5.9 us (10%)
  local copies, waits for them, and re-layouts  1.41 us (2%)
  between operations  0.89 us (1%)
    ppermute x22, starting transfers between devices, across(): lax.ppermute(value, axis, [(i, target(i) % count) for i in range(count)])  28.9 us
    ppermute x22, waiting for transfers between devices, across(): lax.ppermute(value, axis, [(i, target(i) % count) for i in range(count)])  5.9 us
    pallas_call x1, Pallas kernels, shards(): call(cell_body(levels, channels, height, width, 512), [shaped(total_chann...  4.07 us
    pallas_call x1, Pallas kernels, shards(): call(adjoint_body(levels, channels, rows, width), shaped(rows, channels,...  3.49 us
    pallas_call x1, Pallas kernels, shards(): call(kernel_body(levels, channels, rows, width), shaped(TAP_ROWS, 128, dt...  2.66 us
    pallas_call x1, Pallas kernels, shards(): call(inner_body(channels, rows, width), [shaped(rows, channels, width, dt...  2.35 us
    pallas_call x1, Pallas kernels, shards(): call(columns_body(channels, rows, width), shaped(TAPS, rows + REACH, chan...  1.42 us
    pallas_call x1, Pallas kernels, shards(): call(rims_body(channels, rows, width), shaped(rows, channels, width, dtyp...  1.38 us
  transfers between devices with their start and end apart: 22, of which 11 were waited for; matrix products, arithmetic and copies ran while one was open for 1% of the time, Pallas kernels for 25%

profile of v6, /device:TPU:0, one launch (start us, length us, event | category | flops | bytes accessed | tf_op | source)
XLA Modules:
  0.0 59.8 jit_solution(2705013978450304873)
XLA Ops:
  0.7 1.0 %copy-done.4 = bf16[96,12,128]{2,0,1:T(8,128)(2,1)S(1)} copy-done((bf16[96,12,128]{2,0,1:T(8,128)(2,1)S(1)}, bf16[96,12,128]{2,0,1:T(8,128)(2,1)}, u32[]{:S(2)}) %copy-start.4) | copy-done | bytes 294936
  1.7 0.7 %prepare.1 = (bf16[1,96,128]{2,1,0:T(8,128)(2,1)S(1)}, bf16[1,96,128]{2,1,0:T(8,128)(2,1)S(1)}) custom-call(s32[2]{0:T(128)S(1)} %pad_add_fusion.place_ref, bf16[12,96,128]{2,1,0:T(8,128)(2,1)S(1)} %bitcast.8), custom_call_target="tpu_custom_call" | custom-call | flops 1100000000 | tf_op jit(solution)/shard_map/prepare/pallas_call | solution.py:560
  2.4 4.6 %collective-permute-start = (bf16[1,96,128]{2,1,0:T(8,128)(2,1)S(1)}, bf16[1,96,128]{2,1,0:T(8,128)(2,1)S(1)}, u32[]{:S(2)}, u32[]{:S(2)}) collective-permute-start(bf16[1,96,128]{2,1,0:T(8,128)(2,1)S(1)} %get-tuple-element.49), channel_id=1, source_target_pairs={{0,7},{1,2},{2,1},{3,4},{4,3},{5,6},{6,5},{7,0},{8,15},{9,10},{10,... | collective-permute-start | bytes 73736 | tf_op jit(solution)/shard_map/ppermute | solution.py:490
  7.2 2.4 %inner.1 = (f32[12,96,128]{2,1,0:T(8,128)S(1)}, f32[49,96,128]{2,1,0:T(8,128)S(1)}) custom-call(bf16[12,96,128]{2,1,0:T(8,128)(2,1)S(1)} %bitcast.9, f32[96,128]{1,0:T(8,128)S(1)} %pad_convert_fusion.weight_ref), custom_call_target="tpu_custom_call" | custom-call | flops 3300000000 | tf_op jit(solution)/shard_map/inner/pallas_call | solution.py:562
  9.9 0.6 %packs.2 = (f32[1,96,128]{2,1,0:T(8,128)S(1)}, bf16[320,128]{1,0:T(8,128)(2,1)S(1)}) custom-call(s32[2]{0:T(128)S(1)} %pad_add_fusion.place_ref, bf16[12,96,128]{2,1,0:T(8,128)(2,1)S(1)} %bitcast.10, bf16[1,96,128]{2,1,0:T(8,128)(2,1)S(1)} %collective-permute-done.off_ref, bf16[1,96,128]{2,1,0:T(8,128)(2,1)S(1)} %collective-permute-done.1.on_ref), custom_call_target="tpu_custom_call" | custom-call | flops 660000000 | tf_op jit(solution)/shard_map/packs/pallas_call | solution.py:570
  10.5 2.2 %collective-permute-start.2 = (bf16[320,128]{1,0:T(8,128)(2,1)S(1)}, bf16[320,128]{1,0:T(8,128)(2,1)S(1)}, u32[]{:S(2)}, u32[]{:S(2)}) collective-permute-start(bf16[320,128]{1,0:T(8,128)(2,1)S(1)} %get-tuple-element.53), channel_id=1, source_target_pairs={{0,7},{1,6},{2,5},{3,4},{4,3},{5,2},{6,1},{7,0},{8,15},{9,14},{10,... | collective-permute-start | bytes 245768 | tf_op jit(solution)/shard_map/ppermute | solution.py:490
  12.7 0.7 %cotangent.1 = (bf16[384,384]{1,0:T(8,128)(2,1)S(1)}, bf16[3,96,128]{2,1,0:T(8,128)(2,1)S(1)}, bf16[6,96,128]{2,1,0:T(8,128)(2,1)S(1)}, bf16[6,96,128]{2,1,0:T(8,128)(2,1)S(1)}, bf16[6,96,128]{2,1,0:T(8,128)(2,1)S(1)}) custom-call(s32[2]{0:T(128)S(1)} %pad_add_fusion.place_ref, bf16[12,96,128]{2,1,0:T(8,128)(2,1)S(1)} %bitcast.11, ...), custom_call_target="tpu_custom_call" | custom-call | flops 1100000000 | tf_op jit(solution)/shard_map/cotangent/pallas_call | solution.py:572
  13.4 1.6 %collective-permute-start.6 = (bf16[6,96,128]{2,1,0:T(8,128)(2,1)S(1)}, bf16[6,96,128]{2,1,0:T(8,128)(2,1)S(1)}, u32[]{:S(2)}, u32[]{:S(2)}) collective-permute-start(bf16[6,96,128]{2,1,0:T(8,128)(2,1)S(1)} %get-tuple-element.59), channel_id=1, source_target_pairs={{0,8},{8,0},{16,24},{24,16},{1,9},{9,1},{17,25},{25,17},{2,10},{10... | collective-permute-start | bytes 442376 | tf_op jit(solution)/shard_map/ppermute | solution.py:490
  14.9 1.5 %collective-permute-start.7 = (bf16[6,96,128]{2,1,0:T(8,128)(2,1)S(1)}, bf16[6,96,128]{2,1,0:T(8,128)(2,1)S(1)}, u32[]{:S(2)}, u32[]{:S(2)}) collective-permute-start(bf16[6,96,128]{2,1,0:T(8,128)(2,1)S(1)} %get-tuple-element.60), channel_id=1, source_target_pairs={{0,16},{8,24},{16,0},{24,8},{1,17},{9,25},{17,1},{25,9},{2,18},{10... | collective-permute-start | bytes 442376 | tf_op jit(solution)/shard_map/ppermute | solution.py:490
  16.9 1.4 %rims.1.part_ref = f32[12,96,128]{2,1,0:T(8,128)S(1)} custom-call(f32[12,96,128]{2,1,0:T(8,128)S(1)} %get-tuple-element.48.inner_ref, f32[1,96,128]{2,1,0:T(8,128)S(1)} %get-tuple-element.51.packs_ref, f32[49,96,128]{2,1,0:T(8,128)S(1)} %get-tuple-element.52.spread_ref), custom_call_target="tpu_custom_call" | custom-call | flops 2200000000 | tf_op jit(solution)/shard_map/rims/pallas_call | solution.py:582
  18.3 1.1 %fold.1 = (bf16[3,96,128]{2,1,0:T(8,128)(2,1)S(1)}, bf16[3,96,128]{2,1,0:T(8,128)(2,1)S(1)}, bf16[3,96,128]{2,1,0:T(8,128)(2,1)S(1)}, bf16[3,96,128]{2,1,0:T(8,128)(2,1)S(1)}) custom-call(s32[2]{0:T(128)S(1)} %pad_add_fusion.place_ref, f32[12,96,128]{2,1,0:T(8,128)S(1)} %rims.1.part_ref, bf16[320,128]{1,0:T(8,128)(2,1)S(1)} %collective-permute-done.2.fold_ref, ...), custom_call_target="tpu_custom_call" | custom-call | flops 1320000000 | tf_op jit(solution)/shard_map/fold/pallas_call | solution.py:590
  19.5 2.5 %collective-permute-start.3 = (bf16[3,96,128]{2,1,0:T(8,128)(2,1)S(1)}, bf16[3,96,128]{2,1,0:T(8,128)(2,1)S(1)}, u32[]{:S(2)}, u32[]{:S(2)}) collective-permute-start(bf16[3,96,128]{2,1,0:T(8,128)(2,1)S(1)} %get-tuple-element.54), channel_id=1, source_target_pairs={{0,24},{8,16},{16,8},{24,0},{1,25},{9,17},{17,9},{25,1},{2,26},{10... | collective-permute-start | bytes 221192 | tf_op jit(solution)/shard_map/ppermute | solution.py:490
  23.0 1.4 %columns.1.columns_ref = f32[7,15,96,128]{3,2,1,0:T(8,128)S(1)} custom-call(bf16[12,96,128]{2,1,0:T(8,128)(2,1)S(1)} %bitcast.12, f32[1,96,128]{2,1,0:T(8,128)S(1)} %get-tuple-element.51.packs_ref, bf16[320,128]{1,0:T(8,128)(2,1)S(1)} %collective-permute-done.2.fold_ref), custom_call_target="tpu_custom_call" | custom-call | flops 2200000000 | tf_op jit(solution)/shard_map/columns/pallas_call | solution.py:601
  24.5 1.1 %collective-permute-done.3.refs_3_ = bf16[3,96,128]{2,1,0:T(8,128)(2,1)S(1)} collective-permute-done((bf16[3,96,128]{2,1,0:T(8,128)(2,1)S(1)}, bf16[3,96,128]{2,1,0:T(8,128)(2,1)S(1)}, u32[]{:S(2)}, u32[]{:S(2)}) %collective-permute-start.3) | collective-permute-done | bytes 73760 | tf_op jit(solution)/shard_map/ppermute | solution.py:490
  25.5 0.8 %collective-permute-done.4.refs_2_ = bf16[3,96,128]{2,1,0:T(8,128)(2,1)S(1)} collective-permute-done((bf16[3,96,128]{2,1,0:T(8,128)(2,1)S(1)}, bf16[3,96,128]{2,1,0:T(8,128)(2,1)S(1)}, u32[]{:S(2)}, u32[]{:S(2)}) %collective-permute-start.4) | collective-permute-done | bytes 73760 | tf_op jit(solution)/shard_map/ppermute | solution.py:490
  26.8 4.1 %cells.1 = (f32[384,384]{1,0:T(8,128)S(1)}, bf16[3,96,128]{2,1,0:T(8,128)(2,1)S(1)}, bf16[3,96,128]{2,1,0:T(8,128)(2,1)S(1)}, bf16[3,96,128]{2,1,0:T(8,128)(2,1)S(1)}, bf16[3,96,128]{2,1,0:T(8,128)(2,1)S(1)}) custom-call(s32[2]{0:T(128)S(1)} %pad_add_fusion.place_ref, bf16[3,96,128]{2,1,0:T(8,128)(2,1)S(1)} %get-tuple-element.62.refs_0_, ...), custom_call_target="tpu_custom_call" | custom-call | flops 5500000256 | tf_op jit(solution)/shard_map/cells/pallas_call | solution.py:609
  30.9 1.6 %collective-permute-start.9 = (bf16[3,96,128]{2,1,0:T(8,128)(2,1)S(1)}, bf16[3,96,128]{2,1,0:T(8,128)(2,1)S(1)}, u32[]{:S(2)}, u32[]{:S(2)}) collective-permute-start(bf16[3,96,128]{2,1,0:T(8,128)(2,1)S(1)} %get-tuple-element.71), channel_id=1, source_target_pairs={{0,24},{8,16},{16,8},{24,0},{1,25},{9,17},{17,9},{25,1},{2,26},{10... | collective-permute-start | bytes 221192 | tf_op jit(solution)/shard_map/ppermute | solution.py:490
  33.0 1.5 %collective-permute-start.11 = (bf16[3,96,128]{2,1,0:T(8,128)(2,1)S(1)}, bf16[3,96,128]{2,1,0:T(8,128)(2,1)S(1)}, u32[]{:S(2)}, u32[]{:S(2)}) collective-permute-start(bf16[3,96,128]{2,1,0:T(8,128)(2,1)S(1)} %get-tuple-element.73), channel_id=1, source_target_pairs={{0,8},{8,0},{16,24},{24,16},{1,9},{9,1},{17,25},{25,17},{2,10},{10... | collective-permute-start | bytes 221192 | tf_op jit(solution)/shard_map/ppermute | solution.py:490
  34.5 1.3 %finish.1 = bf16[3,384,128]{2,1,0:T(8,128)(2,1)} custom-call(s32[2]{0:T(128)S(1)} %pad_add_fusion.place_ref, bf16[12,96,128]{2,1,0:T(8,128)(2,1)S(1)} %bitcast.13, s32[3,128]{1,0:T(4,128)S(1)} %copy-done.6, f32[384,384]{1,0:T(8,128)S(1)} %get-tuple-element.67.projected_ref, bf16[6,96,128]{2,1,0:T(8,128)(2,1)S(1)} %collective-permute-done.6.refs_0_.refs_1_, ...), custom_call_target="tpu_custom_call" | custom-call | flops 1100000000 | tf_op jit(solution)/shard_map/finish/pallas_call | solution.py:618
  36.2 0.8 %collective-permute-done.10.refs_2_ = bf16[3,96,128]{2,1,0:T(8,128)(2,1)S(1)} collective-permute-done((bf16[3,96,128]{2,1,0:T(8,128)(2,1)S(1)}, bf16[3,96,128]{2,1,0:T(8,128)(2,1)S(1)}, u32[]{:S(2)}, u32[]{:S(2)}) %collective-permute-start.10) | collective-permute-done | bytes 73760 | tf_op jit(solution)/shard_map/ppermute | solution.py:490
  37.3 0.8 %regroup.1 = (bf16[12,96,128]{2,1,0:T(8,128)(2,1)S(1)}, bf16[1,96,128]{2,1,0:T(8,128)(2,1)S(1)}, bf16[1,96,128]{2,1,0:T(8,128)(2,1)S(1)}) custom-call(s32[2]{0:T(128)S(1)} %pad_add_fusion.place_ref, bf16[3,96,128]{2,1,0:T(8,128)(2,1)S(1)} %get-tuple-element.76.refs_0_, bf16[3,96,128]{2,1,0:T(8,128)(2,1)S(1)} %collective-permute-done.11.refs_1_, ...), custom_call_target="tpu_custom_call" | custom-call | flops 880000000 | tf_op jit(solution)/shard_map/regroup/pallas_call | solution.py:628
  38.2 2.5 %collective-permute-start.12 = (bf16[1,96,128]{2,1,0:T(8,128)(2,1)S(1)}, bf16[1,96,128]{2,1,0:T(8,128)(2,1)S(1)}, u32[]{:S(2)}, u32[]{:S(2)}) collective-permute-start(bf16[1,96,128]{2,1,0:T(8,128)(2,1)S(1)} %get-tuple-element.82), channel_id=1, source_target_pairs={{0,7},{1,2},{2,1},{3,4},{4,3},{5,6},{6,5},{7,0},{8,15},{9,10},{10,... | collective-permute-start | bytes 73736 | tf_op jit(solution)/shard_map/ppermute | solution.py:490
  40.7 2.7 %kernel_terms.1 = f32[56,128]{1,0:T(8,128)S(1)} custom-call(s32[2]{0:T(128)S(1)} %pad_add_fusion.place_ref, f32[7,15,96,128]{3,2,1,0:T(8,128)S(1)} %columns.1.columns_ref, bf16[3,96,128]{2,1,0:T(8,128)(2,1)S(1)} %get-tuple-element.76.refs_0_, bf16[3,96,128]{2,1,0:T(8,128)(2,1)S(1)} %collective-permute-done.11.refs_1_, ...), custom_call_target="tpu_custom_call" | custom-call | flops 11000000 | tf_op jit(solution)/shard_map/kernel_terms/pallas_call | solution.py:637
  43.4 0.6 %packs.3 = (f32[1,96,128]{2,1,0:T(8,128)S(1)}, bf16[320,128]{1,0:T(8,128)(2,1)S(1)}) custom-call(s32[2]{0:T(128)S(1)} %pad_add_fusion.place_ref, bf16[12,96,128]{2,1,0:T(8,128)(2,1)S(1)} %get-tuple-element.80.lines_ref.d_ref, bf16[1,96,128]{2,1,0:T(8,128)(2,1)S(1)} %collective-permute-done.12.off_ref, bf16[1,96,128]{2,1,0:T(8,128)(2,1)S(1)} %collective-permute-done.13.on_ref), custom_call_target="tpu_custom_call" | custom-call | flops 660000000 | tf_op jit(solution)/shard_map/packs/pallas_call | solution.py:646
  44.6 1.2 %collective-permute-start.18 = (f32[56,128]{1,0:T(8,128)S(1)}, f32[56,128]{1,0:T(8,128)S(1)}, u32[]{:S(2)}, u32[]{:S(2)}) collective-permute-start(f32[56,128]{1,0:T(8,128)S(1)} %add.23), channel_id=1, source_target_pairs={{0,6},{1,7},{2,4},{3,5},{4,2},{5,3},{6,0},{7,1},{8,14},{9,15},{10,... | collective-permute-start | bytes 86024 | tf_op jit(solution)/shard_map/ppermute | solution.py:490
  45.8 3.2 %collective-permute-start.16 = (f32[56,128]{1,0:T(8,128)S(1)}, f32[56,128]{1,0:T(8,128)S(1)}, u32[]{:S(2)}, u32[]{:S(2)}) collective-permute-start(f32[56,128]{1,0:T(8,128)S(1)} %add.23), channel_id=1, source_target_pairs={{0,2},{1,3},{2,0},{3,1},{4,6},{5,7},{6,4},{7,5},{8,10},{9,11},{10,... | collective-permute-start | bytes 86024 | tf_op jit(solution)/shard_map/ppermute | solution.py:490
  49.0 1.0 %collective-permute-start.15 = (bf16[320,128]{1,0:T(8,128)(2,1)S(1)}, bf16[320,128]{1,0:T(8,128)(2,1)S(1)}, u32[]{:S(2)}, u32[]{:S(2)}) collective-permute-start(bf16[320,128]{1,0:T(8,128)(2,1)S(1)} %get-tuple-element.87), channel_id=1, source_target_pairs={{0,7},{1,6},{2,5},{3,4},{4,3},{5,2},{6,1},{7,0},{8,15},{9,14},{10,... | collective-permute-start | bytes 245768 | tf_op jit(solution)/shard_map/ppermute | solution.py:490
  50.3 1.0 %collective-permute-done.17 = f32[56,128]{1,0:T(8,128)S(1)} collective-permute-done((f32[56,128]{1,0:T(8,128)S(1)}, f32[56,128]{1,0:T(8,128)S(1)}, u32[]{:S(2)}, u32[]{:S(2)}) %collective-permute-start.17) | collective-permute-done | bytes 28704 | tf_op jit(solution)/shard_map/ppermute | solution.py:490
  51.4 2.0 %collective-permute-start.21 = (f32[56,128]{1,0:T(8,128)S(1)}, f32[56,128]{1,0:T(8,128)S(1)}, u32[]{:S(2)}, u32[]{:S(2)}) collective-permute-start(f32[56,128]{1,0:T(8,128)S(1)} %add_add_fusion.refs_0_), channel_id=1, source_target_pairs={{0,24},{8,16},{16,8},{24,0},{1,25},{9,17},{17,9},{25,1},{2,26},{10... | collective-permute-start | bytes 86024 | tf_op jit(solution)/shard_map/ppermute | solution.py:490
  53.9 1.1 %collective-permute-start.19 = (f32[56,128]{1,0:T(8,128)S(1)}, f32[56,128]{1,0:T(8,128)S(1)}, u32[]{:S(2)}, u32[]{:S(2)}) collective-permute-start(f32[56,128]{1,0:T(8,128)S(1)} %add_add_fusion.refs_0_), channel_id=1, source_target_pairs={{0,8},{8,0},{16,24},{24,16},{1,9},{9,1},{17,25},{25,17},{2,10},{10... | collective-permute-start | bytes 86024 | tf_op jit(solution)/shard_map/ppermute | solution.py:490
  55.0 3.5 %adjoint.1 = bf16[12,96,128]{2,1,0:T(8,128)(2,1)} custom-call(s32[2]{0:T(128)S(1)} %pad_add_fusion.place_ref, bf16[12,96,128]{2,1,0:T(8,128)(2,1)S(1)} %get-tuple-element.80.lines_ref.d_ref, f32[1,96,128]{2,1,0:T(8,128)S(1)} %get-tuple-element.84.packs_ref, bf16[320,128]{1,0:T(8,128)(2,1)S(1)} %collective-permute-done.15.fold_ref, ...), custom_call_target="tpu_custom_call" | custom-call | flops 4400000000 | tf_op jit(solution)/shard_map/adjoint/pallas_call | solution.py:650
  58.5 1.3 %assemble.1 = f32[49,384]{1,0:T(8,128)} custom-call(s32[2]{0:T(128)S(1)} %pad_add_fusion.place_ref, f32[56,128]{1,0:T(8,128)S(1)} %add_add_fusion.refs_0_, f32[56,128]{1,0:T(8,128)S(1)} %collective-permute-done.19.refs_1_, f32[56,128]{1,0:T(8,128)S(1)} %collective-permute-done.20.refs_2_, f32[56,128]{1,0:T(8,128)S(1)} %collective-permute-done.21.refs_3_), custom_call_target="tpu_custom_call" | custom-call | flops 880000000 | tf_op jit(solution)/shard_map/assemble/pallas_call | solution.py:660
  (52 shorter events, 5.5 us)
Async XLA Ops:
  0.6 6.3 %copy-start = (bf16[384,49]{0,1:T(8,128)(2,1)S(1)}, bf16[384,49]{0,1:T(8,128)(2,1)}, u32[]{:S(2)}) copy-start(bf16[384,49]{0,1:T(8,128)(2,1)} %param.11) | copy-start | bytes 112900
  0.7 1.0 %copy-start.4 = (bf16[96,12,128]{2,0,1:T(8,128)(2,1)S(1)}, bf16[96,12,128]{2,0,1:T(8,128)(2,1)}, u32[]{:S(2)}) copy-start(bf16[96,12,128]{2,0,1:T(8,128)(2,1)} %param.8) | copy-start | bytes 884740
  1.7 5.5 %copy-start.5 = (bf16[96,12,128]{2,0,1:T(8,128)(2,1)S(1)}, bf16[96,12,128]{2,0,1:T(8,128)(2,1)}, u32[]{:S(2)}) copy-start(bf16[96,12,128]{2,0,1:T(8,128)(2,1)} %param.8) | copy-start | bytes 884740
  2.4 7.4 %collective-permute-start = (bf16[1,96,128]{2,1,0:T(8,128)(2,1)S(1)}, bf16[1,96,128]{2,1,0:T(8,128)(2,1)S(1)}, u32[]{:S(2)}, u32[]{:S(2)}) collective-permute-start(bf16[1,96,128]{2,1,0:T(8,128)(2,1)S(1)} %get-tuple-element.49), channel_id=1, source_target_pairs={{0,7},{1,2},{2,1},{3,4},{4,3},{5,6},{6,5},{7,0},{8,15},{9,10},{10,... | collective-permute-start | bytes 73736 | tf_op jit(solution)/shard_map/ppermute | solution.py:490
  7.0 2.9 %collective-permute-start.1 = (bf16[1,96,128]{2,1,0:T(8,128)(2,1)S(1)}, bf16[1,96,128]{2,1,0:T(8,128)(2,1)S(1)}, u32[]{:S(2)}, u32[]{:S(2)}) collective-permute-start(bf16[1,96,128]{2,1,0:T(8,128)(2,1)S(1)} %get-tuple-element.50), channel_id=1, source_target_pairs={{0,1},{1,0},{2,3},{3,2},{4,5},{5,4},{6,7},{7,6},{8,9},{9,8},{10,11... | collective-permute-start | bytes 73736 | tf_op jit(solution)/shard_map/ppermute | solution.py:490
  7.2 2.4 %copy-start.7 = (f32[384]{0:T(512)S(1)}, f32[384]{0:T(512)}, u32[]{:S(2)}) copy-start(f32[384]{0:T(512)} %param.12) | copy-start | bytes 4612
  7.2 2.5 %copy-start.8 = (f32[384]{0:T(512)S(1)}, f32[384]{0:T(512)}, u32[]{:S(2)}) copy-start(f32[384]{0:T(512)} %param.13) | copy-start | bytes 4612
  9.6 3.1 %copy-start.3 = (bf16[384,3,128]{2,0,1:T(8,128)(2,1)S(1)}, bf16[384,3,128]{2,0,1:T(8,128)(2,1)}, u32[]{:S(2)}) copy-start(bf16[384,3,128]{2,0,1:T(8,128)(2,1)} %param.9) | copy-start | bytes 884740
  9.6 3.1 %copy-start.6 = (s32[3,128]{1,0:T(4,128)S(1)}, s32[3,128]{1,0:T(4,128)}, u32[]{:S(2)}) copy-start(s32[3,128]{1,0:T(4,128)} %mask_ref.3) | copy-start | bytes 4612
  10.5 7.8 %collective-permute-start.2 = (bf16[320,128]{1,0:T(8,128)(2,1)S(1)}, bf16[320,128]{1,0:T(8,128)(2,1)S(1)}, u32[]{:S(2)}, u32[]{:S(2)}) collective-permute-start(bf16[320,128]{1,0:T(8,128)(2,1)S(1)} %get-tuple-element.53), channel_id=1, source_target_pairs={{0,7},{1,6},{2,5},{3,4},{4,3},{5,2},{6,1},{7,0},{8,15},{9,14},{10,... | collective-permute-start | bytes 245768 | tf_op jit(solution)/shard_map/ppermute | solution.py:490
  13.4 9.1 %collective-permute-start.6 = (bf16[6,96,128]{2,1,0:T(8,128)(2,1)S(1)}, bf16[6,96,128]{2,1,0:T(8,128)(2,1)S(1)}, u32[]{:S(2)}, u32[]{:S(2)}) collective-permute-start(bf16[6,96,128]{2,1,0:T(8,128)(2,1)S(1)} %get-tuple-element.59), channel_id=1, source_target_pairs={{0,8},{8,0},{16,24},{24,16},{1,9},{9,1},{17,25},{25,17},{2,10},{10... | collective-permute-start | bytes 442376 | tf_op jit(solution)/shard_map/ppermute | solution.py:490
  14.9 9.5 %collective-permute-start.7 = (bf16[6,96,128]{2,1,0:T(8,128)(2,1)S(1)}, bf16[6,96,128]{2,1,0:T(8,128)(2,1)S(1)}, u32[]{:S(2)}, u32[]{:S(2)}) collective-permute-start(bf16[6,96,128]{2,1,0:T(8,128)(2,1)S(1)} %get-tuple-element.60), channel_id=1, source_target_pairs={{0,16},{8,24},{16,0},{24,8},{1,17},{9,25},{17,1},{25,9},{2,18},{10... | collective-permute-start | bytes 442376 | tf_op jit(solution)/shard_map/ppermute | solution.py:490
  16.4 8.0 %collective-permute-start.8 = (bf16[6,96,128]{2,1,0:T(8,128)(2,1)S(1)}, bf16[6,96,128]{2,1,0:T(8,128)(2,1)S(1)}, u32[]{:S(2)}, u32[]{:S(2)}) collective-permute-start(bf16[6,96,128]{2,1,0:T(8,128)(2,1)S(1)} %get-tuple-element.61), channel_id=1, source_target_pairs={{0,24},{8,16},{16,8},{24,0},{1,25},{9,17},{17,9},{25,1},{2,26},{10... | collective-permute-start | bytes 442376 | tf_op jit(solution)/shard_map/ppermute | solution.py:490
  19.5 6.1 %collective-permute-start.3 = (bf16[3,96,128]{2,1,0:T(8,128)(2,1)S(1)}, bf16[3,96,128]{2,1,0:T(8,128)(2,1)S(1)}, u32[]{:S(2)}, u32[]{:S(2)}) collective-permute-start(bf16[3,96,128]{2,1,0:T(8,128)(2,1)S(1)} %get-tuple-element.54), channel_id=1, source_target_pairs={{0,24},{8,16},{16,8},{24,0},{1,25},{9,17},{17,9},{25,1},{2,26},{10... | collective-permute-start | bytes 221192 | tf_op jit(solution)/shard_map/ppermute | solution.py:490
  22.0 4.4 %collective-permute-start.4 = (bf16[3,96,128]{2,1,0:T(8,128)(2,1)S(1)}, bf16[3,96,128]{2,1,0:T(8,128)(2,1)S(1)}, u32[]{:S(2)}, u32[]{:S(2)}) collective-permute-start(bf16[3,96,128]{2,1,0:T(8,128)(2,1)S(1)} %get-tuple-element.55), channel_id=1, source_target_pairs={{0,16},{8,24},{16,0},{24,8},{1,17},{9,25},{17,1},{25,9},{2,18},{10... | collective-permute-start | bytes 221192 | tf_op jit(solution)/shard_map/ppermute | solution.py:490
  22.5 4.4 %copy-start.1 = (bf16[384,1536]{1,0:T(8,128)(2,1)S(1)}, bf16[384,1536]{1,0:T(8,128)(2,1)}, u32[]{:S(2)}) copy-start(bf16[384,1536]{1,0:T(8,128)(2,1)} %refs_7_.1) | copy-start | bytes 3538948
  22.5 4.4 %copy-start.2 = (bf16[1536,384]{1,0:T(8,128)(2,1)S(1)}, bf16[1536,384]{1,0:T(8,128)(2,1)}, u32[]{:S(2)}) copy-start(bf16[1536,384]{1,0:T(8,128)(2,1)} %refs_8_.1) | copy-start | bytes 3538948
  22.5 4.4 %collective-permute-start.5 = (bf16[3,96,128]{2,1,0:T(8,128)(2,1)S(1)}, bf16[3,96,128]{2,1,0:T(8,128)(2,1)S(1)}, u32[]{:S(2)}, u32[]{:S(2)}) collective-permute-start(bf16[3,96,128]{2,1,0:T(8,128)(2,1)S(1)} %get-tuple-element.56), channel_id=1, source_target_pairs={{0,8},{8,0},{16,24},{24,16},{1,9},{9,1},{17,25},{25,17},{2,10},{10... | collective-permute-start | bytes 221192 | tf_op jit(solution)/shard_map/ppermute | solution.py:490
  30.9 5.3 %collective-permute-start.9 = (bf16[3,96,128]{2,1,0:T(8,128)(2,1)S(1)}, bf16[3,96,128]{2,1,0:T(8,128)(2,1)S(1)}, u32[]{:S(2)}, u32[]{:S(2)}) collective-permute-start(bf16[3,96,128]{2,1,0:T(8,128)(2,1)S(1)} %get-tuple-element.71), channel_id=1, source_target_pairs={{0,24},{8,16},{16,8},{24,0},{1,25},{9,17},{17,9},{25,1},{2,26},{10... | collective-permute-start | bytes 221192 | tf_op jit(solution)/shard_map/ppermute | solution.py:490
  32.5 4.5 %collective-permute-start.10 = (bf16[3,96,128]{2,1,0:T(8,128)(2,1)S(1)}, bf16[3,96,128]{2,1,0:T(8,128)(2,1)S(1)}, u32[]{:S(2)}, u32[]{:S(2)}) collective-permute-start(bf16[3,96,128]{2,1,0:T(8,128)(2,1)S(1)} %get-tuple-element.72), channel_id=1, source_target_pairs={{0,16},{8,24},{16,0},{24,8},{1,17},{9,25},{17,1},{25,9},{2,18},{10... | collective-permute-start | bytes 221192 | tf_op jit(solution)/shard_map/ppermute | solution.py:490
  33.0 4.4 %collective-permute-start.11 = (bf16[3,96,128]{2,1,0:T(8,128)(2,1)S(1)}, bf16[3,96,128]{2,1,0:T(8,128)(2,1)S(1)}, u32[]{:S(2)}, u32[]{:S(2)}) collective-permute-start(bf16[3,96,128]{2,1,0:T(8,128)(2,1)S(1)} %get-tuple-element.73), channel_id=1, source_target_pairs={{0,8},{8,0},{16,24},{24,16},{1,9},{9,1},{17,25},{25,17},{2,10},{10... | collective-permute-start | bytes 221192 | tf_op jit(solution)/shard_map/ppermute | solution.py:490
  38.1 5.3 %collective-permute-start.13 = (bf16[1,96,128]{2,1,0:T(8,128)(2,1)S(1)}, bf16[1,96,128]{2,1,0:T(8,128)(2,1)S(1)}, u32[]{:S(2)}, u32[]{:S(2)}) collective-permute-start(bf16[1,96,128]{2,1,0:T(8,128)(2,1)S(1)} %get-tuple-element.83), channel_id=1, source_target_pairs={{0,1},{1,0},{2,3},{3,2},{4,5},{5,4},{6,7},{7,6},{8,9},{9,8},{10,11... | collective-permute-start | bytes 73736 | tf_op jit(solution)/shard_map/ppermute | solution.py:490
  38.2 5.2 %collective-permute-start.12 = (bf16[1,96,128]{2,1,0:T(8,128)(2,1)S(1)}, bf16[1,96,128]{2,1,0:T(8,128)(2,1)S(1)}, u32[]{:S(2)}, u32[]{:S(2)}) collective-permute-start(bf16[1,96,128]{2,1,0:T(8,128)(2,1)S(1)} %get-tuple-element.82), channel_id=1, source_target_pairs={{0,7},{1,2},{2,1},{3,4},{4,3},{5,6},{6,5},{7,0},{8,15},{9,10},{10,... | collective-permute-start | bytes 73736 | tf_op jit(solution)/shard_map/ppermute | solution.py:490
  43.3 1.2 %collective-permute-start.14 = (f32[56,128]{1,0:T(8,128)S(1)}, f32[56,128]{1,0:T(8,128)S(1)}, u32[]{:S(2)}, u32[]{:S(2)}) collective-permute-start(f32[56,128]{1,0:T(8,128)S(1)} %kernel_terms.1), channel_id=1, source_target_pairs={{0,1},{1,0},{2,3},{3,2},{4,5},{5,4},{6,7},{7,6},{8,9},{9,8},{10,11... | collective-permute-start | bytes 86024 | tf_op jit(solution)/shard_map/ppermute | solution.py:490
  44.6 5.7 %collective-permute-start.18 = (f32[56,128]{1,0:T(8,128)S(1)}, f32[56,128]{1,0:T(8,128)S(1)}, u32[]{:S(2)}, u32[]{:S(2)}) collective-permute-start(f32[56,128]{1,0:T(8,128)S(1)} %add.23), channel_id=1, source_target_pairs={{0,6},{1,7},{2,4},{3,5},{4,2},{5,3},{6,0},{7,1},{8,14},{9,15},{10,... | collective-permute-start | bytes 86024 | tf_op jit(solution)/shard_map/ppermute | solution.py:490
  45.8 5.5 %collective-permute-start.17 = (f32[56,128]{1,0:T(8,128)S(1)}, f32[56,128]{1,0:T(8,128)S(1)}, u32[]{:S(2)}, u32[]{:S(2)}) collective-permute-start(f32[56,128]{1,0:T(8,128)S(1)} %add.23), channel_id=1, source_target_pairs={{0,4},{1,5},{2,6},{3,7},{4,0},{5,1},{6,2},{7,3},{8,12},{9,13},{10,... | collective-permute-start | bytes 86024 | tf_op jit(solution)/shard_map/ppermute | solution.py:490
  45.8 5.6 %collective-permute-start.16 = (f32[56,128]{1,0:T(8,128)S(1)}, f32[56,128]{1,0:T(8,128)S(1)}, u32[]{:S(2)}, u32[]{:S(2)}) collective-permute-start(f32[56,128]{1,0:T(8,128)S(1)} %add.23), channel_id=1, source_target_pairs={{0,2},{1,3},{2,0},{3,1},{4,6},{5,7},{6,4},{7,5},{8,10},{9,11},{10,... | collective-permute-start | bytes 86024 | tf_op jit(solution)/shard_map/ppermute | solution.py:490
  49.0 6.0 %collective-permute-start.15 = (bf16[320,128]{1,0:T(8,128)(2,1)S(1)}, bf16[320,128]{1,0:T(8,128)(2,1)S(1)}, u32[]{:S(2)}, u32[]{:S(2)}) collective-permute-start(bf16[320,128]{1,0:T(8,128)(2,1)S(1)} %get-tuple-element.87), channel_id=1, source_target_pairs={{0,7},{1,6},{2,5},{3,4},{4,3},{5,2},{6,1},{7,0},{8,15},{9,14},{10,... | collective-permute-start | bytes 245768 | tf_op jit(solution)/shard_map/ppermute | solution.py:490
  51.4 7.1 %collective-permute-start.21 = (f32[56,128]{1,0:T(8,128)S(1)}, f32[56,128]{1,0:T(8,128)S(1)}, u32[]{:S(2)}, u32[]{:S(2)}) collective-permute-start(f32[56,128]{1,0:T(8,128)S(1)} %add_add_fusion.refs_0_), channel_id=1, source_target_pairs={{0,24},{8,16},{16,8},{24,0},{1,25},{9,17},{17,9},{25,1},{2,26},{10... | collective-permute-start | bytes 86024 | tf_op jit(solution)/shard_map/ppermute | solution.py:490
  53.4 5.2 %collective-permute-start.20 = (f32[56,128]{1,0:T(8,128)S(1)}, f32[56,128]{1,0:T(8,128)S(1)}, u32[]{:S(2)}, u32[]{:S(2)}) collective-permute-start(f32[56,128]{1,0:T(8,128)S(1)} %add_add_fusion.refs_0_), channel_id=1, source_target_pairs={{0,16},{8,24},{16,0},{24,8},{1,17},{9,25},{17,1},{25,9},{2,18},{10... | collective-permute-start | bytes 86024 | tf_op jit(solution)/shard_map/ppermute | solution.py:490
  53.9 4.6 %collective-permute-start.19 = (f32[56,128]{1,0:T(8,128)S(1)}, f32[56,128]{1,0:T(8,128)S(1)}, u32[]{:S(2)}, u32[]{:S(2)}) collective-permute-start(f32[56,128]{1,0:T(8,128)S(1)} %add_add_fusion.refs_0_), channel_id=1, source_target_pairs={{0,8},{8,0},{16,24},{24,16},{1,9},{9,1},{17,25},{25,17},{2,10},{10... | collective-permute-start | bytes 86024 | tf_op jit(solution)/shard_map/ppermute | solution.py:490
